TPU v7x, 256 devices: a whole 4x4x8 slice. The times are simulated.
256 devices in a mesh: seq: 32 (over y, x, core), head: 8 (over z).
Axes of the slice: x: 4, y: 4, z: 8, core: 2. Of those that a mesh axis runs over, the one named last changes fastest.
Arguments:
- queries: bfloat16 [8192, 4096], P('seq', 'head'), may hold values from -0.59765625 to 0.59765625
- keys: bfloat16 [8192, 4096], P('seq', 'head'), may hold values from -0.59765625 to 0.59765625
- values: bfloat16 [8192, 4096], P('seq', 'head'), may hold values from -6 to 6
- log_decay: float32 [32, 8192], P('head', 'seq'), may hold values from -0.8 to 0, as said below
- lengths: int32 [16], replicated, may hold values from 1 to 2048, as said below
- out_weight: bfloat16 [4096, 4096], P('seq', 'head'), may hold values from -0.09375 to 0.09375
- out_grad: bfloat16 [8192, 4096], P('seq', 'head'), may hold values from -0.29882812 to 0.29882812
Outputs:
- mixed: bfloat16 [8192, 4096], P('seq', 'head')
- grad_queries: bfloat16 [8192, 4096], P('seq', 'head')
- grad_keys: bfloat16 [8192, 4096], P('seq', 'head')
- grad_values: bfloat16 [8192, 4096], P('seq', 'head')
- grad_weight: float32 [4096, 4096], P('seq', 'head')
Inputs may be any that keep to these rules, and one draw needn't show every extreme that they name: `log_decay`: every entry is negative; tokens where a document starts cut the state whatever their value. The 16 lengths sum to 8192; the longest document has exactly 2048 tokens.
All inputs are finite; a program needn't handle non-finite values.
Results may differ from a plain program's by a relative error of at most 0.015.
Values may be sent and summed in bfloat16 or wider, within the bound.
No kernel may reach another device: no remote copies, remote signals or barrier semaphores. Data moves between devices by JAX's collectives and lax.ppermute only.
A program may use at most 64 MiB of HBM per device.

v0:
```python
import jax
import jax.numpy as jnp
from jax import lax
from jax.sharding import PartitionSpec as P

HIGH = lax.Precision.HIGHEST


def shifted(value, axis, steps):
    count = lax.axis_size(axis)
    initial, last = (max(0, -steps), min(count, count - steps))
    return lax.ppermute(value, axis, [(source, source + steps) for source in range(initial, last)])


def doc_index(lengths, positions):
    starts = jnp.cumsum(lengths, dtype=jnp.int32) - lengths
    above = (positions[:, None] >= starts[None, :]).astype(jnp.int32)
    return jnp.sum(above, axis=1, dtype=jnp.int32) - 1


def block_masks(log_decay, docs, prev_doc, last_doc, next_doc):
    count = docs.shape[0]
    cumul = jnp.cumsum(log_decay, axis=1)
    order = jnp.arange(count, dtype=jnp.int32)
    joint = jnp.logical_and(order[:, None] >= order[None, :], docs[:, None] == docs[None, :])[None]
    spread = jnp.where(joint, cumul[:, :, None] - cumul[:, None, :], 0.0)
    decay = jnp.where(joint, jnp.exp(spread), 0.0)
    zero = jnp.zeros_like(cumul)
    tail = cumul[:, -1:] - cumul
    enter = jnp.where((docs == prev_doc)[None], jnp.exp(cumul), zero)
    keep = jnp.where((docs == last_doc)[None], jnp.exp(tail), zero)
    leave = jnp.where((docs == next_doc)[None], jnp.exp(tail), zero)
    through = jnp.where(prev_doc == last_doc, jnp.exp(cumul[:, -1]), jnp.zeros_like(cumul[:, -1]))
    return (decay, enter, keep, leave, through)


def relay_forward(through, summary):

    def turn(step, prefix):
        return shifted(through[:, None, None] * prefix + summary, "seq", 1)

    return lax.fori_loop(0, lax.axis_size("seq") - 1, turn, jnp.zeros_like(summary))


def relay_backward(through, summary):

    def turn(step, prefix):
        return shifted(through[:, None, None] * prefix + summary, "seq", -1)

    return lax.fori_loop(0, lax.axis_size("seq") - 1, turn, jnp.zeros_like(summary))


def body(queries, keys, values, log_decay, lengths, out_weight, out_grad):
    rows = queries.shape[0]
    heads = log_decay.shape[0]
    width = queries.shape[1] // heads
    first = lax.axis_index("seq") * rows
    positions = first + jnp.arange(rows, dtype=jnp.int32)
    docs = doc_index(lengths, positions)
    edges = doc_index(lengths, jnp.stack([first - 1, first + rows - 1, first + rows]))
    decay, enter, keep, leave, through = block_masks(log_decay, docs, edges[0], edges[1], edges[2])
    q3 = queries.reshape(rows, heads, width)
    k3 = keys.reshape(rows, heads, width)
    v3 = values.reshape(rows, heads, width)
    q32, k32, v32 = (q3.astype(jnp.float32), k3.astype(jnp.float32), v3.astype(jnp.float32))
    scores = jnp.einsum("the,she->hts", q3, k3, preferred_element_type=jnp.float32)
    attn = (scores * decay).astype(jnp.bfloat16)
    local = jnp.einsum("hts,shf->thf", attn, v3, preferred_element_type=jnp.float32)
    summary = jnp.einsum("the,thf->hef", k32 * keep.T[:, :, None], v32, precision=HIGH)
    state_in = relay_forward(through, summary)
    carried = jnp.einsum("the,hef->thf", q32, state_in, precision=HIGH) * enter.T[:, :, None]
    attended = (local + carried).astype(jnp.bfloat16).reshape(rows, heads * width)
    partial_value = lax.dot_general(
        attended,
        lax.all_gather(out_weight, "seq", axis=0, tiled=True),
        (((1,), (1,)), ((), ())),
        preferred_element_type=jnp.float32,
    )
    mixed = lax.psum_scatter(partial_value, "head", scatter_dimension=1, tiled=True).astype(
        jnp.bfloat16
    )
    full_grad = lax.all_gather(out_grad, "head", axis=1, tiled=True)
    columns = full_grad
    pulled = jnp.dot(
        columns,
        lax.all_gather(out_weight, "seq", axis=0, tiled=True),
        preferred_element_type=jnp.float32,
    )
    grad_att = pulled.astype(jnp.bfloat16)
    columns = full_grad
    grad_weight = lax.psum_scatter(
        lax.dot_general(
            columns, attended, (((0,), (0,)), ((), ())), preferred_element_type=jnp.float32
        ).astype(jnp.bfloat16),
        "seq",
        scatter_dimension=0,
        tiled=True,
    ).astype(jnp.float32)
    g3 = grad_att.reshape(rows, heads, width)
    g32 = g3.astype(jnp.float32)
    pulls = jnp.einsum("thf,shf->hts", g3, v3, preferred_element_type=jnp.float32)
    back = (pulls * decay).astype(jnp.bfloat16)
    summary_back = jnp.einsum("the,thf->hef", q32 * enter.T[:, :, None], g32, precision=HIGH)
    carry_in = relay_backward(through, summary_back)
    grad_q = jnp.einsum("hts,she->the", back, k3, preferred_element_type=jnp.float32)
    grad_q = (
        grad_q + jnp.einsum("hef,thf->the", state_in, g32, precision=HIGH) * enter.T[:, :, None]
    )
    grad_k = jnp.einsum("hts,the->she", back, q3, preferred_element_type=jnp.float32)
    grad_k = (
        grad_k + jnp.einsum("hef,thf->the", carry_in, v32, precision=HIGH) * leave.T[:, :, None]
    )
    grad_v = jnp.einsum("hts,thf->shf", attn, g3, preferred_element_type=jnp.float32)
    grad_v = (
        grad_v + jnp.einsum("hef,the->thf", carry_in, k32, precision=HIGH) * leave.T[:, :, None]
    )
    shape = (rows, heads * width)
    return (
        mixed,
        grad_q.astype(jnp.bfloat16).reshape(shape),
        grad_k.astype(jnp.bfloat16).reshape(shape),
        grad_v.astype(jnp.bfloat16).reshape(shape),
        grad_weight,
    )


def solution(mesh):
    in_specs = (
        P("seq", "head"),
        P("seq", "head"),
        P("seq", "head"),
        P("head", "seq"),
        P(),
        P("seq", "head"),
        P("seq", "head"),
    )
    out_specs = (
        P("seq", "head"),
        P("seq", "head"),
        P("seq", "head"),
        P("seq", "head"),
        P("seq", "head"),
    )
    return jax.shard_map(body, mesh=mesh, in_specs=in_specs, out_specs=out_specs, check_vma=False)
```

profile of v0, /device:TPU:39, one launch (start us, length us, event | category | flops | bytes accessed | tf_op | source)
XLA Modules:
  0.0 678.9 jit_solution(11164095333828120195)
XLA Ops:
  21.5 309.6 %while.20 = (s32[]{:T(128)}, f32[4,128,128]{2,1,0:T(8,128)S(1)}, f32[4]{0:T(128)S(1)}, f32[4,128,128]{2,1,0:T(8,128)S(1)}, s32[]{:T(128)}) while((s32[]{:T(128)}, f32[4,128,128]{2,1,0:T(8,128)S(1)}, f32[4]{0:T(128)S(1)}, f32[4,128,128]{2,1,0:T(8,128)S(1)}, s32[]{:T(128)}) %tuple.45), condition=%wide.region_6.7_spmd, body=%wide.region_5.6_spmd.sunk | while | flops 131074 | bytes 1835125 | solution.py:42
  95.1 8.4 %collective-permute-done = f32[4,128,128]{2,1,0:T(8,128)S(1)} collective-permute-done((f32[4,128,128]{2,1,0:T(8,128)S(1)}, f32[4,128,128]{2,1,0:T(8,128)S(1)}, u32[]{:S(2)}, u32[]{:S(2)}) %collective-permute-start) | collective-permute-done | bytes 262176 | tf_op jit(solution)/shard_map/while/body/eval_jaxpr/ppermute | solution.py:12
  353.9 312.1 %while.21 = (s32[]{:T(128)}, f32[4,128,128]{2,1,0:T(8,128)S(1)}, f32[4]{0:T(128)S(1)}, f32[4,128,128]{2,1,0:T(8,128)S(1)}, s32[]{:T(128)}) while((s32[]{:T(128)}, f32[4,128,128]{2,1,0:T(8,128)S(1)}, f32[4]{0:T(128)S(1)}, f32[4,128,128]{2,1,0:T(8,128)S(1)}, s32[]{:T(128)}) %tuple.59), condition=%wide.region_9.10_spmd, body=%wide.region_8.9_spmd.sunk | while | flops 131074 | bytes 1835125 | solution.py:50
  356.0 8.6 %collective-permute-done.1 = f32[4,128,128]{2,1,0:T(8,128)S(1)} collective-permute-done((f32[4,128,128]{2,1,0:T(8,128)S(1)}, f32[4,128,128]{2,1,0:T(8,128)S(1)}, u32[]{:S(2)}, u32[]{:S(2)}) %collective-permute-start.1) | collective-permute-done | bytes 262176 | tf_op jit(solution)/shard_map/while/body/eval_jaxpr/ppermute | solution.py:12
  366.6 7.9 %collective-permute-done.1 = f32[4,128,128]{2,1,0:T(8,128)S(1)} collective-permute-done((f32[4,128,128]{2,1,0:T(8,128)S(1)}, f32[4,128,128]{2,1,0:T(8,128)S(1)}, u32[]{:S(2)}, u32[]{:S(2)}) %collective-permute-start.1) | collective-permute-done | bytes 262176 | tf_op jit(solution)/shard_map/while/body/eval_jaxpr/ppermute | solution.py:12
  376.5 7.9 %collective-permute-done.1 = f32[4,128,128]{2,1,0:T(8,128)S(1)} collective-permute-done((f32[4,128,128]{2,1,0:T(8,128)S(1)}, f32[4,128,128]{2,1,0:T(8,128)S(1)}, u32[]{:S(2)}, u32[]{:S(2)}) %collective-permute-start.1) | collective-permute-done | bytes 262176 | tf_op jit(solution)/shard_map/while/body/eval_jaxpr/ppermute | solution.py:12
  386.4 7.9 %collective-permute-done.1 = f32[4,128,128]{2,1,0:T(8,128)S(1)} collective-permute-done((f32[4,128,128]{2,1,0:T(8,128)S(1)}, f32[4,128,128]{2,1,0:T(8,128)S(1)}, u32[]{:S(2)}, u32[]{:S(2)}) %collective-permute-start.1) | collective-permute-done | bytes 262176 | tf_op jit(solution)/shard_map/while/body/eval_jaxpr/ppermute | solution.py:12
  396.3 12.1 %collective-permute-done.1 = f32[4,128,128]{2,1,0:T(8,128)S(1)} collective-permute-done((f32[4,128,128]{2,1,0:T(8,128)S(1)}, f32[4,128,128]{2,1,0:T(8,128)S(1)}, u32[]{:S(2)}, u32[]{:S(2)}) %collective-permute-start.1) | collective-permute-done | bytes 262176 | tf_op jit(solution)/shard_map/while/body/eval_jaxpr/ppermute | solution.py:12
  410.4 7.9 %collective-permute-done.1 = f32[4,128,128]{2,1,0:T(8,128)S(1)} collective-permute-done((f32[4,128,128]{2,1,0:T(8,128)S(1)}, f32[4,128,128]{2,1,0:T(8,128)S(1)}, u32[]{:S(2)}, u32[]{:S(2)}) %collective-permute-start.1) | collective-permute-done | bytes 262176 | tf_op jit(solution)/shard_map/while/body/eval_jaxpr/ppermute | solution.py:12
  420.3 8.2 %collective-permute-done.1 = f32[4,128,128]{2,1,0:T(8,128)S(1)} collective-permute-done((f32[4,128,128]{2,1,0:T(8,128)S(1)}, f32[4,128,128]{2,1,0:T(8,128)S(1)}, u32[]{:S(2)}, u32[]{:S(2)}) %collective-permute-start.1) | collective-permute-done | bytes 262176 | tf_op jit(solution)/shard_map/while/body/eval_jaxpr/ppermute | solution.py:12
  430.5 7.9 %collective-permute-done.1 = f32[4,128,128]{2,1,0:T(8,128)S(1)} collective-permute-done((f32[4,128,128]{2,1,0:T(8,128)S(1)}, f32[4,128,128]{2,1,0:T(8,128)S(1)}, u32[]{:S(2)}, u32[]{:S(2)}) %collective-permute-start.1) | collective-permute-done | bytes 262176 | tf_op jit(solution)/shard_map/while/body/eval_jaxpr/ppermute | solution.py:12
  440.4 7.9 %collective-permute-done.1 = f32[4,128,128]{2,1,0:T(8,128)S(1)} collective-permute-done((f32[4,128,128]{2,1,0:T(8,128)S(1)}, f32[4,128,128]{2,1,0:T(8,128)S(1)}, u32[]{:S(2)}, u32[]{:S(2)}) %collective-permute-start.1) | collective-permute-done | bytes 262176 | tf_op jit(solution)/shard_map/while/body/eval_jaxpr/ppermute | solution.py:12
  450.3 7.9 %collective-permute-done.1 = f32[4,128,128]{2,1,0:T(8,128)S(1)} collective-permute-done((f32[4,128,128]{2,1,0:T(8,128)S(1)}, f32[4,128,128]{2,1,0:T(8,128)S(1)}, u32[]{:S(2)}, u32[]{:S(2)}) %collective-permute-start.1) | collective-permute-done | bytes 262176 | tf_op jit(solution)/shard_map/while/body/eval_jaxpr/ppermute | solution.py:12
  460.2 7.9 %collective-permute-done.1 = f32[4,128,128]{2,1,0:T(8,128)S(1)} collective-permute-done((f32[4,128,128]{2,1,0:T(8,128)S(1)}, f32[4,128,128]{2,1,0:T(8,128)S(1)}, u32[]{:S(2)}, u32[]{:S(2)}) %collective-permute-start.1) | collective-permute-done | bytes 262176 | tf_op jit(solution)/shard_map/while/body/eval_jaxpr/ppermute | solution.py:12
  470.1 7.9 %collective-permute-done.1 = f32[4,128,128]{2,1,0:T(8,128)S(1)} collective-permute-done((f32[4,128,128]{2,1,0:T(8,128)S(1)}, f32[4,128,128]{2,1,0:T(8,128)S(1)}, u32[]{:S(2)}, u32[]{:S(2)}) %collective-permute-start.1) | collective-permute-done | bytes 262176 | tf_op jit(solution)/shard_map/while/body/eval_jaxpr/ppermute | solution.py:12
  480.0 7.9 %collective-permute-done.1 = f32[4,128,128]{2,1,0:T(8,128)S(1)} collective-permute-done((f32[4,128,128]{2,1,0:T(8,128)S(1)}, f32[4,128,128]{2,1,0:T(8,128)S(1)}, u32[]{:S(2)}, u32[]{:S(2)}) %collective-permute-start.1) | collective-permute-done | bytes 262176 | tf_op jit(solution)/shard_map/while/body/eval_jaxpr/ppermute | solution.py:12
  489.9 7.9 %collective-permute-done.1 = f32[4,128,128]{2,1,0:T(8,128)S(1)} collective-permute-done((f32[4,128,128]{2,1,0:T(8,128)S(1)}, f32[4,128,128]{2,1,0:T(8,128)S(1)}, u32[]{:S(2)}, u32[]{:S(2)}) %collective-permute-start.1) | collective-permute-done | bytes 262176 | tf_op jit(solution)/shard_map/while/body/eval_jaxpr/ppermute | solution.py:12
  499.8 7.9 %collective-permute-done.1 = f32[4,128,128]{2,1,0:T(8,128)S(1)} collective-permute-done((f32[4,128,128]{2,1,0:T(8,128)S(1)}, f32[4,128,128]{2,1,0:T(8,128)S(1)}, u32[]{:S(2)}, u32[]{:S(2)}) %collective-permute-start.1) | collective-permute-done | bytes 262176 | tf_op jit(solution)/shard_map/while/body/eval_jaxpr/ppermute | solution.py:12
  509.7 7.9 %collective-permute-done.1 = f32[4,128,128]{2,1,0:T(8,128)S(1)} collective-permute-done((f32[4,128,128]{2,1,0:T(8,128)S(1)}, f32[4,128,128]{2,1,0:T(8,128)S(1)}, u32[]{:S(2)}, u32[]{:S(2)}) %collective-permute-start.1) | collective-permute-done | bytes 262176 | tf_op jit(solution)/shard_map/while/body/eval_jaxpr/ppermute | solution.py:12
  519.6 7.9 %collective-permute-done.1 = f32[4,128,128]{2,1,0:T(8,128)S(1)} collective-permute-done((f32[4,128,128]{2,1,0:T(8,128)S(1)}, f32[4,128,128]{2,1,0:T(8,128)S(1)}, u32[]{:S(2)}, u32[]{:S(2)}) %collective-permute-start.1) | collective-permute-done | bytes 262176 | tf_op jit(solution)/shard_map/while/body/eval_jaxpr/ppermute | solution.py:12
  529.5 7.9 %collective-permute-done.1 = f32[4,128,128]{2,1,0:T(8,128)S(1)} collective-permute-done((f32[4,128,128]{2,1,0:T(8,128)S(1)}, f32[4,128,128]{2,1,0:T(8,128)S(1)}, u32[]{:S(2)}, u32[]{:S(2)}) %collective-permute-start.1) | collective-permute-done | bytes 262176 | tf_op jit(solution)/shard_map/while/body/eval_jaxpr/ppermute | solution.py:12
  539.4 7.9 %collective-permute-done.1 = f32[4,128,128]{2,1,0:T(8,128)S(1)} collective-permute-done((f32[4,128,128]{2,1,0:T(8,128)S(1)}, f32[4,128,128]{2,1,0:T(8,128)S(1)}, u32[]{:S(2)}, u32[]{:S(2)}) %collective-permute-start.1) | collective-permute-done | bytes 262176 | tf_op jit(solution)/shard_map/while/body/eval_jaxpr/ppermute | solution.py:12
  549.3 7.9 %collective-permute-done.1 = f32[4,128,128]{2,1,0:T(8,128)S(1)} collective-permute-done((f32[4,128,128]{2,1,0:T(8,128)S(1)}, f32[4,128,128]{2,1,0:T(8,128)S(1)}, u32[]{:S(2)}, u32[]{:S(2)}) %collective-permute-start.1) | collective-permute-done | bytes 262176 | tf_op jit(solution)/shard_map/while/body/eval_jaxpr/ppermute | solution.py:12
  559.2 7.9 %collective-permute-done.1 = f32[4,128,128]{2,1,0:T(8,128)S(1)} collective-permute-done((f32[4,128,128]{2,1,0:T(8,128)S(1)}, f32[4,128,128]{2,1,0:T(8,128)S(1)}, u32[]{:S(2)}, u32[]{:S(2)}) %collective-permute-start.1) | collective-permute-done | bytes 262176 | tf_op jit(solution)/shard_map/while/body/eval_jaxpr/ppermute | solution.py:12
  569.1 7.9 %collective-permute-done.1 = f32[4,128,128]{2,1,0:T(8,128)S(1)} collective-permute-done((f32[4,128,128]{2,1,0:T(8,128)S(1)}, f32[4,128,128]{2,1,0:T(8,128)S(1)}, u32[]{:S(2)}, u32[]{:S(2)}) %collective-permute-start.1) | collective-permute-done | bytes 262176 | tf_op jit(solution)/shard_map/while/body/eval_jaxpr/ppermute | solution.py:12
  579.0 7.9 %collective-permute-done.1 = f32[4,128,128]{2,1,0:T(8,128)S(1)} collective-permute-done((f32[4,128,128]{2,1,0:T(8,128)S(1)}, f32[4,128,128]{2,1,0:T(8,128)S(1)}, u32[]{:S(2)}, u32[]{:S(2)}) %collective-permute-start.1) | collective-permute-done | bytes 262176 | tf_op jit(solution)/shard_map/while/body/eval_jaxpr/ppermute | solution.py:12
  588.9 7.9 %collective-permute-done.1 = f32[4,128,128]{2,1,0:T(8,128)S(1)} collective-permute-done((f32[4,128,128]{2,1,0:T(8,128)S(1)}, f32[4,128,128]{2,1,0:T(8,128)S(1)}, u32[]{:S(2)}, u32[]{:S(2)}) %collective-permute-start.1) | collective-permute-done | bytes 262176 | tf_op jit(solution)/shard_map/while/body/eval_jaxpr/ppermute | solution.py:12
  598.8 7.9 %collective-permute-done.1 = f32[4,128,128]{2,1,0:T(8,128)S(1)} collective-permute-done((f32[4,128,128]{2,1,0:T(8,128)S(1)}, f32[4,128,128]{2,1,0:T(8,128)S(1)}, u32[]{:S(2)}, u32[]{:S(2)}) %collective-permute-start.1) | collective-permute-done | bytes 262176 | tf_op jit(solution)/shard_map/while/body/eval_jaxpr/ppermute | solution.py:12
  608.7 7.9 %collective-permute-done.1 = f32[4,128,128]{2,1,0:T(8,128)S(1)} collective-permute-done((f32[4,128,128]{2,1,0:T(8,128)S(1)}, f32[4,128,128]{2,1,0:T(8,128)S(1)}, u32[]{:S(2)}, u32[]{:S(2)}) %collective-permute-start.1) | collective-permute-done | bytes 262176 | tf_op jit(solution)/shard_map/while/body/eval_jaxpr/ppermute | solution.py:12
  618.6 7.9 %collective-permute-done.1 = f32[4,128,128]{2,1,0:T(8,128)S(1)} collective-permute-done((f32[4,128,128]{2,1,0:T(8,128)S(1)}, f32[4,128,128]{2,1,0:T(8,128)S(1)}, u32[]{:S(2)}, u32[]{:S(2)}) %collective-permute-start.1) | collective-permute-done | bytes 262176 | tf_op jit(solution)/shard_map/while/body/eval_jaxpr/ppermute | solution.py:12
  628.5 7.9 %collective-permute-done.1 = f32[4,128,128]{2,1,0:T(8,128)S(1)} collective-permute-done((f32[4,128,128]{2,1,0:T(8,128)S(1)}, f32[4,128,128]{2,1,0:T(8,128)S(1)}, u32[]{:S(2)}, u32[]{:S(2)}) %collective-permute-start.1) | collective-permute-done | bytes 262176 | tf_op jit(solution)/shard_map/while/body/eval_jaxpr/ppermute | solution.py:12
  638.4 7.9 %collective-permute-done.1 = f32[4,128,128]{2,1,0:T(8,128)S(1)} collective-permute-done((f32[4,128,128]{2,1,0:T(8,128)S(1)}, f32[4,128,128]{2,1,0:T(8,128)S(1)}, u32[]{:S(2)}, u32[]{:S(2)}) %collective-permute-start.1) | collective-permute-done | bytes 262176 | tf_op jit(solution)/shard_map/while/body/eval_jaxpr/ppermute | solution.py:12
  (227 shorter events, 420.8 us)
Async XLA Ops:
  7.2 324.4 %all-gather.5.cloned.1.call-start = ((), (), s32[]{:S(2)}) async-start(), calls=%async_computation.4 | async-start | bytes 2359296 | tf_op jit(solution)/shard_map/all_gather | solution.py:82
  7.9 335.0 %all-gather.3.cloned.1.call-start = ((), (), s32[]{:S(2)}) async-start(), calls=%async_computation.2 | async-start | bytes 4325376 | tf_op jit(solution)/shard_map/all_gather | solution.py:75
  8.7 660.1 %reduce-scatter.7.cloned.1.call-start = ((), (), s32[]{:S(2)}) async-start(), calls=%async_computation.5 | async-start | bytes 4325376
  28.7 9.8 %collective-permute-start = (f32[4,128,128]{2,1,0:T(8,128)S(1)}, f32[4,128,128]{2,1,0:T(8,128)S(1)}, u32[]{:S(2)}, u32[]{:S(2)}) collective-permute-start(f32[4,128,128]{2,1,0:T(8,128)S(1)} %multiply_add_fusion.4), channel_id=1, source_target_pairs={{0,8},{8,16},{16,24},{24,32},{32,40},{40,48},{48,56},{56,64},{64,7... | collective-permute-start | bytes 786440 | tf_op jit(solution)/shard_map/while/body/eval_jaxpr/ppermute | solution.py:12
  38.6 9.8 %collective-permute-start = (f32[4,128,128]{2,1,0:T(8,128)S(1)}, f32[4,128,128]{2,1,0:T(8,128)S(1)}, u32[]{:S(2)}, u32[]{:S(2)}) collective-permute-start(f32[4,128,128]{2,1,0:T(8,128)S(1)} %multiply_add_fusion.4), channel_id=1, source_target_pairs={{0,8},{8,16},{16,24},{24,32},{32,40},{40,48},{48,56},{56,64},{64,7... | collective-permute-start | bytes 786440 | tf_op jit(solution)/shard_map/while/body/eval_jaxpr/ppermute | solution.py:12
  48.5 9.8 %collective-permute-start = (f32[4,128,128]{2,1,0:T(8,128)S(1)}, f32[4,128,128]{2,1,0:T(8,128)S(1)}, u32[]{:S(2)}, u32[]{:S(2)}) collective-permute-start(f32[4,128,128]{2,1,0:T(8,128)S(1)} %multiply_add_fusion.4), channel_id=1, source_target_pairs={{0,8},{8,16},{16,24},{24,32},{32,40},{40,48},{48,56},{56,64},{64,7... | collective-permute-start | bytes 786440 | tf_op jit(solution)/shard_map/while/body/eval_jaxpr/ppermute | solution.py:12
  58.4 9.8 %collective-permute-start = (f32[4,128,128]{2,1,0:T(8,128)S(1)}, f32[4,128,128]{2,1,0:T(8,128)S(1)}, u32[]{:S(2)}, u32[]{:S(2)}) collective-permute-start(f32[4,128,128]{2,1,0:T(8,128)S(1)} %multiply_add_fusion.4), channel_id=1, source_target_pairs={{0,8},{8,16},{16,24},{24,32},{32,40},{40,48},{48,56},{56,64},{64,7... | collective-permute-start | bytes 786440 | tf_op jit(solution)/shard_map/while/body/eval_jaxpr/ppermute | solution.py:12
  68.3 10.2 %collective-permute-start = (f32[4,128,128]{2,1,0:T(8,128)S(1)}, f32[4,128,128]{2,1,0:T(8,128)S(1)}, u32[]{:S(2)}, u32[]{:S(2)}) collective-permute-start(f32[4,128,128]{2,1,0:T(8,128)S(1)} %multiply_add_fusion.4), channel_id=1, source_target_pairs={{0,8},{8,16},{16,24},{24,32},{32,40},{40,48},{48,56},{56,64},{64,7... | collective-permute-start | bytes 786440 | tf_op jit(solution)/shard_map/while/body/eval_jaxpr/ppermute | solution.py:12
  78.6 9.9 %collective-permute-start = (f32[4,128,128]{2,1,0:T(8,128)S(1)}, f32[4,128,128]{2,1,0:T(8,128)S(1)}, u32[]{:S(2)}, u32[]{:S(2)}) collective-permute-start(f32[4,128,128]{2,1,0:T(8,128)S(1)} %multiply_add_fusion.4), channel_id=1, source_target_pairs={{0,8},{8,16},{16,24},{24,32},{32,40},{40,48},{48,56},{56,64},{64,7... | collective-permute-start | bytes 786440 | tf_op jit(solution)/shard_map/while/body/eval_jaxpr/ppermute | solution.py:12
  88.5 15.0 %collective-permute-start = (f32[4,128,128]{2,1,0:T(8,128)S(1)}, f32[4,128,128]{2,1,0:T(8,128)S(1)}, u32[]{:S(2)}, u32[]{:S(2)}) collective-permute-start(f32[4,128,128]{2,1,0:T(8,128)S(1)} %multiply_add_fusion.4), channel_id=1, source_target_pairs={{0,8},{8,16},{16,24},{24,32},{32,40},{40,48},{48,56},{56,64},{64,7... | collective-permute-start | bytes 786440 | tf_op jit(solution)/shard_map/while/body/eval_jaxpr/ppermute | solution.py:12
  103.6 9.8 %collective-permute-start = (f32[4,128,128]{2,1,0:T(8,128)S(1)}, f32[4,128,128]{2,1,0:T(8,128)S(1)}, u32[]{:S(2)}, u32[]{:S(2)}) collective-permute-start(f32[4,128,128]{2,1,0:T(8,128)S(1)} %multiply_add_fusion.4), channel_id=1, source_target_pairs={{0,8},{8,16},{16,24},{24,32},{32,40},{40,48},{48,56},{56,64},{64,7... | collective-permute-start | bytes 786440 | tf_op jit(solution)/shard_map/while/body/eval_jaxpr/ppermute | solution.py:12
  113.5 9.8 %collective-permute-start = (f32[4,128,128]{2,1,0:T(8,128)S(1)}, f32[4,128,128]{2,1,0:T(8,128)S(1)}, u32[]{:S(2)}, u32[]{:S(2)}) collective-permute-start(f32[4,128,128]{2,1,0:T(8,128)S(1)} %multiply_add_fusion.4), channel_id=1, source_target_pairs={{0,8},{8,16},{16,24},{24,32},{32,40},{40,48},{48,56},{56,64},{64,7... | collective-permute-start | bytes 786440 | tf_op jit(solution)/shard_map/while/body/eval_jaxpr/ppermute | solution.py:12
  123.4 9.8 %collective-permute-start = (f32[4,128,128]{2,1,0:T(8,128)S(1)}, f32[4,128,128]{2,1,0:T(8,128)S(1)}, u32[]{:S(2)}, u32[]{:S(2)}) collective-permute-start(f32[4,128,128]{2,1,0:T(8,128)S(1)} %multiply_add_fusion.4), channel_id=1, source_target_pairs={{0,8},{8,16},{16,24},{24,32},{32,40},{40,48},{48,56},{56,64},{64,7... | collective-permute-start | bytes 786440 | tf_op jit(solution)/shard_map/while/body/eval_jaxpr/ppermute | solution.py:12
  133.3 9.8 %collective-permute-start = (f32[4,128,128]{2,1,0:T(8,128)S(1)}, f32[4,128,128]{2,1,0:T(8,128)S(1)}, u32[]{:S(2)}, u32[]{:S(2)}) collective-permute-start(f32[4,128,128]{2,1,0:T(8,128)S(1)} %multiply_add_fusion.4), channel_id=1, source_target_pairs={{0,8},{8,16},{16,24},{24,32},{32,40},{40,48},{48,56},{56,64},{64,7... | collective-permute-start | bytes 786440 | tf_op jit(solution)/shard_map/while/body/eval_jaxpr/ppermute | solution.py:12
  143.2 9.8 %collective-permute-start = (f32[4,128,128]{2,1,0:T(8,128)S(1)}, f32[4,128,128]{2,1,0:T(8,128)S(1)}, u32[]{:S(2)}, u32[]{:S(2)}) collective-permute-start(f32[4,128,128]{2,1,0:T(8,128)S(1)} %multiply_add_fusion.4), channel_id=1, source_target_pairs={{0,8},{8,16},{16,24},{24,32},{32,40},{40,48},{48,56},{56,64},{64,7... | collective-permute-start | bytes 786440 | tf_op jit(solution)/shard_map/while/body/eval_jaxpr/ppermute | solution.py:12
  153.1 9.8 %collective-permute-start = (f32[4,128,128]{2,1,0:T(8,128)S(1)}, f32[4,128,128]{2,1,0:T(8,128)S(1)}, u32[]{:S(2)}, u32[]{:S(2)}) collective-permute-start(f32[4,128,128]{2,1,0:T(8,128)S(1)} %multiply_add_fusion.4), channel_id=1, source_target_pairs={{0,8},{8,16},{16,24},{24,32},{32,40},{40,48},{48,56},{56,64},{64,7... | collective-permute-start | bytes 786440 | tf_op jit(solution)/shard_map/while/body/eval_jaxpr/ppermute | solution.py:12
  162.9 9.8 %collective-permute-start = (f32[4,128,128]{2,1,0:T(8,128)S(1)}, f32[4,128,128]{2,1,0:T(8,128)S(1)}, u32[]{:S(2)}, u32[]{:S(2)}) collective-permute-start(f32[4,128,128]{2,1,0:T(8,128)S(1)} %multiply_add_fusion.4), channel_id=1, source_target_pairs={{0,8},{8,16},{16,24},{24,32},{32,40},{40,48},{48,56},{56,64},{64,7... | collective-permute-start | bytes 786440 | tf_op jit(solution)/shard_map/while/body/eval_jaxpr/ppermute | solution.py:12
  172.8 9.8 %collective-permute-start = (f32[4,128,128]{2,1,0:T(8,128)S(1)}, f32[4,128,128]{2,1,0:T(8,128)S(1)}, u32[]{:S(2)}, u32[]{:S(2)}) collective-permute-start(f32[4,128,128]{2,1,0:T(8,128)S(1)} %multiply_add_fusion.4), channel_id=1, source_target_pairs={{0,8},{8,16},{16,24},{24,32},{32,40},{40,48},{48,56},{56,64},{64,7... | collective-permute-start | bytes 786440 | tf_op jit(solution)/shard_map/while/body/eval_jaxpr/ppermute | solution.py:12
  182.7 9.8 %collective-permute-start = (f32[4,128,128]{2,1,0:T(8,128)S(1)}, f32[4,128,128]{2,1,0:T(8,128)S(1)}, u32[]{:S(2)}, u32[]{:S(2)}) collective-permute-start(f32[4,128,128]{2,1,0:T(8,128)S(1)} %multiply_add_fusion.4), channel_id=1, source_target_pairs={{0,8},{8,16},{16,24},{24,32},{32,40},{40,48},{48,56},{56,64},{64,7... | collective-permute-start | bytes 786440 | tf_op jit(solution)/shard_map/while/body/eval_jaxpr/ppermute | solution.py:12
  192.6 9.8 %collective-permute-start = (f32[4,128,128]{2,1,0:T(8,128)S(1)}, f32[4,128,128]{2,1,0:T(8,128)S(1)}, u32[]{:S(2)}, u32[]{:S(2)}) collective-permute-start(f32[4,128,128]{2,1,0:T(8,128)S(1)} %multiply_add_fusion.4), channel_id=1, source_target_pairs={{0,8},{8,16},{16,24},{24,32},{32,40},{40,48},{48,56},{56,64},{64,7... | collective-permute-start | bytes 786440 | tf_op jit(solution)/shard_map/while/body/eval_jaxpr/ppermute | solution.py:12
  202.5 9.8 %collective-permute-start = (f32[4,128,128]{2,1,0:T(8,128)S(1)}, f32[4,128,128]{2,1,0:T(8,128)S(1)}, u32[]{:S(2)}, u32[]{:S(2)}) collective-permute-start(f32[4,128,128]{2,1,0:T(8,128)S(1)} %multiply_add_fusion.4), channel_id=1, source_target_pairs={{0,8},{8,16},{16,24},{24,32},{32,40},{40,48},{48,56},{56,64},{64,7... | collective-permute-start | bytes 786440 | tf_op jit(solution)/shard_map/while/body/eval_jaxpr/ppermute | solution.py:12
  212.4 9.8 %collective-permute-start = (f32[4,128,128]{2,1,0:T(8,128)S(1)}, f32[4,128,128]{2,1,0:T(8,128)S(1)}, u32[]{:S(2)}, u32[]{:S(2)}) collective-permute-start(f32[4,128,128]{2,1,0:T(8,128)S(1)} %multiply_add_fusion.4), channel_id=1, source_target_pairs={{0,8},{8,16},{16,24},{24,32},{32,40},{40,48},{48,56},{56,64},{64,7... | collective-permute-start | bytes 786440 | tf_op jit(solution)/shard_map/while/body/eval_jaxpr/ppermute | solution.py:12
  232.2 9.8 %collective-permute-start = (f32[4,128,128]{2,1,0:T(8,128)S(1)}, f32[4,128,128]{2,1,0:T(8,128)S(1)}, u32[]{:S(2)}, u32[]{:S(2)}) collective-permute-start(f32[4,128,128]{2,1,0:T(8,128)S(1)} %multiply_add_fusion.4), channel_id=1, source_target_pairs={{0,8},{8,16},{16,24},{24,32},{32,40},{40,48},{48,56},{56,64},{64,7... | collective-permute-start | bytes 786440 | tf_op jit(solution)/shard_map/while/body/eval_jaxpr/ppermute | solution.py:12
  242.1 9.8 %collective-permute-start = (f32[4,128,128]{2,1,0:T(8,128)S(1)}, f32[4,128,128]{2,1,0:T(8,128)S(1)}, u32[]{:S(2)}, u32[]{:S(2)}) collective-permute-start(f32[4,128,128]{2,1,0:T(8,128)S(1)} %multiply_add_fusion.4), channel_id=1, source_target_pairs={{0,8},{8,16},{16,24},{24,32},{32,40},{40,48},{48,56},{56,64},{64,7... | collective-permute-start | bytes 786440 | tf_op jit(solution)/shard_map/while/body/eval_jaxpr/ppermute | solution.py:12
  252.0 9.8 %collective-permute-start = (f32[4,128,128]{2,1,0:T(8,128)S(1)}, f32[4,128,128]{2,1,0:T(8,128)S(1)}, u32[]{:S(2)}, u32[]{:S(2)}) collective-permute-start(f32[4,128,128]{2,1,0:T(8,128)S(1)} %multiply_add_fusion.4), channel_id=1, source_target_pairs={{0,8},{8,16},{16,24},{24,32},{32,40},{40,48},{48,56},{56,64},{64,7... | collective-permute-start | bytes 786440 | tf_op jit(solution)/shard_map/while/body/eval_jaxpr/ppermute | solution.py:12
  281.7 9.8 %collective-permute-start = (f32[4,128,128]{2,1,0:T(8,128)S(1)}, f32[4,128,128]{2,1,0:T(8,128)S(1)}, u32[]{:S(2)}, u32[]{:S(2)}) collective-permute-start(f32[4,128,128]{2,1,0:T(8,128)S(1)} %multiply_add_fusion.4), channel_id=1, source_target_pairs={{0,8},{8,16},{16,24},{24,32},{32,40},{40,48},{48,56},{56,64},{64,7... | collective-permute-start | bytes 786440 | tf_op jit(solution)/shard_map/while/body/eval_jaxpr/ppermute | solution.py:12
  291.6 9.8 %collective-permute-start = (f32[4,128,128]{2,1,0:T(8,128)S(1)}, f32[4,128,128]{2,1,0:T(8,128)S(1)}, u32[]{:S(2)}, u32[]{:S(2)}) collective-permute-start(f32[4,128,128]{2,1,0:T(8,128)S(1)} %multiply_add_fusion.4), channel_id=1, source_target_pairs={{0,8},{8,16},{16,24},{24,32},{32,40},{40,48},{48,56},{56,64},{64,7... | collective-permute-start | bytes 786440 | tf_op jit(solution)/shard_map/while/body/eval_jaxpr/ppermute | solution.py:12
  301.5 9.8 %collective-permute-start = (f32[4,128,128]{2,1,0:T(8,128)S(1)}, f32[4,128,128]{2,1,0:T(8,128)S(1)}, u32[]{:S(2)}, u32[]{:S(2)}) collective-permute-start(f32[4,128,128]{2,1,0:T(8,128)S(1)} %multiply_add_fusion.4), channel_id=1, source_target_pairs={{0,8},{8,16},{16,24},{24,32},{32,40},{40,48},{48,56},{56,64},{64,7... | collective-permute-start | bytes 786440 | tf_op jit(solution)/shard_map/while/body/eval_jaxpr/ppermute | solution.py:12
  342.9 327.8 %reduce-scatter.5.cloned.1.call-start = ((), (), s32[]{:S(2)}) async-start(), calls=%async_computation.3 | async-start | bytes 4718592 | tf_op jit(solution)/shard_map/reduce_scatter | solution.py:79
  354.0 10.5 %collective-permute-start.1 = (f32[4,128,128]{2,1,0:T(8,128)S(1)}, f32[4,128,128]{2,1,0:T(8,128)S(1)}, u32[]{:S(2)}, u32[]{:S(2)}) collective-permute-start(f32[4,128,128]{2,1,0:T(8,128)S(1)} %multiply_add_fusion.5), channel_id=1, source_target_pairs={{8,0},{16,8},{24,16},{32,24},{40,32},{48,40},{56,48},{64,56},{72,6... | collective-permute-start | bytes 786440 | tf_op jit(solution)/shard_map/while/body/eval_jaxpr/ppermute | solution.py:12
  394.4 14.0 %collective-permute-start.1 = (f32[4,128,128]{2,1,0:T(8,128)S(1)}, f32[4,128,128]{2,1,0:T(8,128)S(1)}, u32[]{:S(2)}, u32[]{:S(2)}) collective-permute-start(f32[4,128,128]{2,1,0:T(8,128)S(1)} %multiply_add_fusion.5), channel_id=1, source_target_pairs={{8,0},{16,8},{24,16},{32,24},{40,32},{48,40},{56,48},{64,56},{72,6... | collective-permute-start | bytes 786440 | tf_op jit(solution)/shard_map/while/body/eval_jaxpr/ppermute | solution.py:12
  418.4 10.2 %collective-permute-start.1 = (f32[4,128,128]{2,1,0:T(8,128)S(1)}, f32[4,128,128]{2,1,0:T(8,128)S(1)}, u32[]{:S(2)}, u32[]{:S(2)}) collective-permute-start(f32[4,128,128]{2,1,0:T(8,128)S(1)} %multiply_add_fusion.5), channel_id=1, source_target_pairs={{8,0},{16,8},{24,16},{32,24},{40,32},{48,40},{56,48},{64,56},{72,6... | collective-permute-start | bytes 786440 | tf_op jit(solution)/shard_map/while/body/eval_jaxpr/ppermute | solution.py:12
  (37 other events, 661.0 us)
Sparse Core Ops, SparseCore 0:
  9.8 39.0 all-gather.4
  51.5 55.7 all-gather.2
  343.0 88.8 reduce-scatter.6
  434.5 55.5 reduce-scatter.4
where the time goes:
time: 681 us; the launch traced here: 679 us
  waiting for transfers between devices  358 us (53%)
  starting transfers between devices  259 us (38%)
  matrix products  17.5 us (3%)
  local copies, waits for them, and re-layouts  16.5 us (2%)
  between operations  15.3 us (2%)
  other arithmetic  12.1 us (2%)
    ppermute x62, waiting for transfers between devices, shifted(): lax.ppermute(value, axis, [(source, source + steps) for source in range(i...  357 us
    ppermute x62, starting transfers between devices, shifted(): lax.ppermute(value, axis, [(source, source + steps) for source in range(i...  258 us
  transfers between devices with their start and end apart: 66, of which 62 were waited for; matrix products, arithmetic and copies ran while one was open for 6% of the time, Pallas kernels for 0%

commit v1 on v0

v1 whole, which is shorter than its diff:
```python
import functools

import jax
import jax.numpy as jnp
from jax import lax
from jax.experimental import pallas as pl
from jax.experimental.pallas import tpu as pltpu
from jax.sharding import Mesh, PartitionSpec as P

F32 = jnp.float32
BF16 = jnp.bfloat16
HIGH = lax.Precision.HIGHEST
SIDE = 4
LONG = 8
HEADS = 4
HD = 128
ROWS = 256
HALF = 256
STATE = HEADS * HD
PAY = STATE + 16
DOCS = 16
VMEM = pl.BlockSpec(memory_space=pltpu.VMEM)
SMEM = pl.BlockSpec(memory_space=pltpu.SMEM)


def call(kernel, outs, specs, flops):
    return pl.pallas_call(
        kernel,
        out_shape=[jax.ShapeDtypeStruct(s, d) for s, d in outs],
        in_specs=specs,
        out_specs=[VMEM] * len(outs),
        compiler_params=pltpu.CompilerParams(vmem_limit_bytes=48 * 2**20),
        cost_estimate=pl.CostEstimate(flops=flops, bytes_accessed=2**20, transcendentals=0),
    )


def dot(a, b, dims, precision=None):
    return lax.dot_general(a, b, (dims, ((), ())), precision=precision, preferred_element_type=F32)


NN = ((1,), (0,))
NT = ((1,), (1,))
TN = ((0,), (0,))


class Masks:
    def __init__(self, len_ref, at_ref, ld_ref):
        first = at_ref[0]
        pos_r = first + lax.broadcasted_iota(jnp.int32, (1, ROWS), 1)
        pos_c = first + lax.broadcasted_iota(jnp.int32, (ROWS, 1), 0)
        doc_r = jnp.full((1, ROWS), -1, jnp.int32)
        doc_c = jnp.full((ROWS, 1), -1, jnp.int32)
        edge = [jnp.int32(-1)] * 3
        start = jnp.int32(0)
        for j in range(DOCS):
            doc_r = doc_r + jnp.where(pos_r >= start, 1, 0)
            doc_c = doc_c + jnp.where(pos_c >= start, 1, 0)
            for n, p in enumerate((first - 1, first + ROWS - 1, first + ROWS)):
                edge[n] = edge[n] + jnp.where(p >= start, 1, 0)
            start = start + len_ref[j]
        prev, last, after = edge
        row = lax.broadcasted_iota(jnp.int32, (ROWS, ROWS), 0)
        col = lax.broadcasted_iota(jnp.int32, (ROWS, ROWS), 1)
        ld = ld_ref[...]
        self.cum_r = dot(ld, jnp.where(row <= col, 1.0, 0.0).astype(F32), NN, HIGH)
        self.cum_c = dot(jnp.where(col <= row, 1.0, 0.0).astype(F32), ld, NT, HIGH)
        self.joint = jnp.logical_and(row >= col, doc_c == doc_r)
        self.first_doc, self.last_doc, self.next_doc = doc_c == prev, doc_c == last, doc_c == after
        self.whole = prev == last

    def decay(self, h):
        gap = self.cum_c[:, h : h + 1] - self.cum_r[h : h + 1, :]
        return jnp.where(self.joint, jnp.exp(jnp.where(self.joint, gap, 0.0)), 0.0)

    def total(self, h):
        return self.cum_r[h : h + 1, ROWS - 1 : ROWS]

    def enter(self, h):
        return jnp.where(self.first_doc, jnp.exp(self.cum_c[:, h : h + 1]), 0.0)

    def tail(self, h):
        return jnp.exp(self.total(h) - self.cum_c[:, h : h + 1])

    def keep(self, h):
        return jnp.where(self.last_doc, self.tail(h), 0.0)

    def leave(self, h):
        return jnp.where(self.next_doc, self.tail(h), 0.0)

    def through(self, h):
        return jnp.where(self.whole, jnp.exp(self.total(h)), 0.0)


def head(h):
    return slice(h * HD, (h + 1) * HD)


def put_factors(ref, factors):
    row = lax.broadcasted_iota(jnp.int32, (16, HD), 0)
    block = jnp.zeros((16, HD), F32)
    for h, f in enumerate(factors):
        high = f.astype(BF16).astype(F32)
        block = block + jnp.where(row == h, high, 0.0) + jnp.where(row == HEADS + h, f - high, 0.0)
    ref[STATE:PAY, :] = block.astype(BF16)


def take(ref):
    tail = ref[STATE:PAY, :].astype(F32)
    states = [ref[head(h), :].astype(F32) for h in range(HEADS)]
    factors = [tail[h : h + 1, 0:1] + tail[HEADS + h : HEADS + h + 1, 0:1] for h in range(HEADS)]
    return states, factors


def chain(a_ref, b_ref, c_ref):
    (sa, fa), (sb, fb), (sc, fc) = take(a_ref), take(b_ref), take(c_ref)
    states = [sa[h] + fa[h] * (sb[h] + fb[h] * sc[h]) for h in range(HEADS)]
    return states, [fa[h] * fb[h] * fc[h] for h in range(HEADS)]


def first_kernel(len_ref, at_ref, ld_ref, q_ref, k_ref, v_ref, pay_ref, local_ref):
    m = Masks(len_ref, at_ref, ld_ref)
    for h in range(HEADS):
        k, v = k_ref[:, head(h)], v_ref[:, head(h)]
        kept = (k.astype(F32) * m.keep(h)).astype(BF16)
        pay_ref[head(h), :] = dot(kept, v, TN).astype(BF16)
        attn = (dot(q_ref[:, head(h)], k, NT) * m.decay(h)).astype(BF16)
        local_ref[:, head(h)] = dot(attn, v, NN)
    put_factors(pay_ref, [m.through(h) for h in range(HEADS)])


def window_kernel(a_ref, b_ref, c_ref, pay_ref):
    states, factors = chain(a_ref, b_ref, c_ref)
    for h in range(HEADS):
        pay_ref[head(h), :] = states[h].astype(BF16)
    put_factors(pay_ref, factors)


def attend_kernel(len_ref, at_ref, ld_ref, q_ref, local_ref, a_ref, b_ref, c_ref, att_ref, state_ref):
    m = Masks(len_ref, at_ref, ld_ref)
    states, _ = chain(a_ref, b_ref, c_ref)
    for h in range(HEADS):
        state = states[h].astype(BF16)
        state_ref[head(h), :] = state
        carried = dot(q_ref[:, head(h)], state, NN) * m.enter(h)
        att_ref[:, head(h)] = (local_ref[:, head(h)] + carried).astype(BF16)


def back_kernel(len_ref, at_ref, ld_ref, q_ref, own_ref, other_ref, pay_ref, g_ref):
    m = Masks(len_ref, at_ref, ld_ref)
    for h in range(HEADS):
        g = (own_ref[:, head(h)] + other_ref[:, head(h)].astype(F32)).astype(BF16)
        g_ref[:, head(h)] = g
        entered = (q_ref[:, head(h)].astype(F32) * m.enter(h)).astype(BF16)
        pay_ref[head(h), :] = dot(entered, g, TN).astype(BF16)
    put_factors(pay_ref, [m.through(h) for h in range(HEADS)])


def grads_kernel(
    len_ref, at_ref, ld_ref, q_ref, k_ref, v_ref, g_ref, state_ref, a_ref, b_ref, c_ref, dq_ref, dk_ref, dv_ref
):
    m = Masks(len_ref, at_ref, ld_ref)
    carries, _ = chain(a_ref, b_ref, c_ref)
    for h in range(HEADS):
        q, k, v, g = (r[:, head(h)] for r in (q_ref, k_ref, v_ref, g_ref))
        decay, leave, carry = m.decay(h), m.leave(h), carries[h].astype(BF16)
        attn = (dot(q, k, NT) * decay).astype(BF16)
        back = (dot(g, v, NT) * decay).astype(BF16)
        dq = dot(back, k, NN) + dot(g, state_ref[head(h), :], NT) * m.enter(h)
        dk = dot(back, q, TN) + dot(v, carry, NT) * leave
        dv = dot(attn, g, TN) + dot(k, carry, NN) * leave
        dq_ref[:, head(h)] = dq.astype(BF16)
        dk_ref[:, head(h)] = dk.astype(BF16)
        dv_ref[:, head(h)] = dv.astype(BF16)


def chip_of(j, y, x, sign):
    far, near = j // 2, 2 * (j % 2)
    dy = lax.rem(sign * (far - y) + SIDE, SIDE)
    return dy, [lax.rem(sign * (near + e - x) + SIDE, SIDE) for e in range(2)]


def weight_part(wa_ref, wb_ref, j, at_ref):
    ry, rx = chip_of(j, at_ref[1], at_ref[2], -1)
    left = jnp.concatenate([wa_ref[ry, r] for r in rx], axis=0)
    right = jnp.concatenate([wb_ref[r, ry] for r in rx], axis=0)
    return jnp.concatenate([left, right], axis=1)


def pull_kernel(at_ref, g_ref, wa_ref, wb_ref, own_ref, send_ref):
    total = jnp.zeros((2 * ROWS, STATE), F32)
    for j in range(LONG):
        slot = lax.rem(at_ref[3] - j + LONG, LONG)
        total = total + dot(g_ref[slot], weight_part(wa_ref, wb_ref, j, at_ref), NN)
    own_ref[...] = total[:ROWS]
    send_ref[...] = total[ROWS:].astype(BF16)


def mix_kernel(at_ref, own_ref, other_ref, wa_ref, wb_ref, out_ref):
    for j in range(LONG):
        w = weight_part(wa_ref, wb_ref, j, at_ref)
        out_ref[j, :ROWS] = dot(own_ref[...], w, NT).astype(BF16)
        out_ref[j, ROWS:] = dot(other_ref[...], w, NT).astype(BF16)


def weight_grad_kernel(at_ref, g_ref, own_ref, other_ref, ra_ref, rb_ref):
    for j in range(LONG):
        slot = lax.rem(at_ref[3] - j + LONG, LONG)
        dy, dx = chip_of(j, at_ref[1], at_ref[2], 1)
        part = dot(g_ref[slot, :ROWS], own_ref[...], TN) + dot(g_ref[slot, ROWS:], other_ref[...], TN)
        part = part.astype(BF16)
        for e in range(2):
            rows = slice(e * HD, (e + 1) * HD)
            ra_ref[dy, dx[e]] = part[rows, :HALF]
            rb_ref[dx[e], dy] = part[rows, HALF:]


def ring(value, axis, steps):
    count = lax.axis_size(axis)
    return lax.ppermute(value, axis, [(i, (i + steps) % count) for i in range(count)])


def line(value, steps):
    count = SIDE * SIDE * 2
    pairs = [(i, i + steps) for i in range(count) if 0 <= i + steps < count]
    return lax.ppermute(value, ("y", "x", "core"), pairs)


def gather_side(value, axis):
    return jnp.stack([value] + [ring(value, axis, s) for s in (1, 2, -1)])


def scatter_side(value, axis):
    parts = [value[0]] + [ring(value[s], axis, s if s < 3 else -1) for s in (1, 2, 3)]
    return functools.reduce(jnp.add, [p.astype(F32) for p in parts])


def gather_long(value):
    found = {0: value}
    right = left = value
    for s in range(1, LONG // 2 + 1):
        right = ring(right, "z", 1)
        found[s] = right
        if s < LONG // 2:
            left = ring(left, "z", -1)
            found[LONG - s] = left
    return jnp.stack([found[s] for s in range(LONG)])


def swap(value):
    return ring(value, "core", 1)


def parity(value):
    return [jnp.concatenate([value[:, (2 * e + c) * HD : (2 * e + c + 1) * HD] for e in range(2)], 1) for c in range(2)]


def body(q, k, v, log_decay, lengths, weight, out_grad):
    y, x, c, z = (lax.axis_index(a) for a in ("y", "x", "core", "z"))
    at = jnp.stack([((y * SIDE + x) * 2 + c) * ROWS, y, x, z]).astype(jnp.int32)
    lead = (lengths, at, log_decay)
    lead_specs = [SMEM, SMEM, VMEM]
    even, odd = parity(out_grad)
    mine, yours = jnp.where(c == 0, even, odd), jnp.where(c == 0, odd, even)
    grads = gather_long(jnp.concatenate([mine, swap(yours)], axis=0))
    wa = gather_side(gather_side(weight[:, :HALF], "x"), "y")
    wb = gather_side(gather_side(weight[:, HALF:], "y"), "x")
    wide = ((ROWS, STATE), BF16)
    pay, local = call(
        first_kernel, [((PAY, HD), BF16), ((ROWS, STATE), F32)], lead_specs + [VMEM] * 3, 2**28
    )(*lead, q, k, v)
    window = call(window_kernel, [((PAY, HD), BF16)], [VMEM] * 3, 2**20)
    [pay] = window(pay, line(pay, 1), line(pay, 2))
    att, state = call(attend_kernel, [wide, ((STATE, HD), BF16)], lead_specs + [VMEM] * 5, 2**26)(
        *lead, q, local, line(pay, 1), line(pay, 4), line(pay, 7)
    )
    att_other = swap(att)
    [mixed] = call(mix_kernel, [((LONG, 2 * ROWS, HALF), BF16)], [SMEM] + [VMEM] * 4, 2**30)(
        at, att, att_other, wa, wb
    )
    mixed = lax.psum_scatter(mixed, "z", scatter_dimension=0)
    mixed_other = swap(mixed[ROWS:])
    mixed = mixed[:ROWS]
    even, odd = jnp.where(c == 0, mixed, mixed_other), jnp.where(c == 0, mixed_other, mixed)
    mixed = jnp.concatenate([even[:, :HD], odd[:, :HD], even[:, HD:], odd[:, HD:]], axis=1)
    own, send = call(pull_kernel, [((ROWS, STATE), F32), wide], [SMEM] + [VMEM] * 3, 2**30)(at, grads, wa, wb)
    back, g = call(back_kernel, [((PAY, HD), BF16), wide], lead_specs + [VMEM] * 3, 2**26)(
        *lead, q, own, swap(send)
    )
    [back] = window(back, line(back, -1), line(back, -2))
    grid = ((SIDE, SIDE, HD, HALF), BF16)
    ra, rb = call(weight_grad_kernel, [grid, grid], [SMEM] + [VMEM] * 3, 2**30)(at, grads, att, att_other)
    ra = scatter_side(scatter_side(ra, "y").astype(BF16), "x")
    rb = scatter_side(scatter_side(rb, "x").astype(BF16), "y")
    dq, dk, dv = call(grads_kernel, [wide] * 3, lead_specs + [VMEM] * 8, 2**29)(
        *lead, q, k, v, g, state, line(back, -1), line(back, -4), line(back, -7)
    )
    return mixed, dq, dk, dv, jnp.concatenate([ra, rb], axis=1)


def solution(mesh):
    fine = Mesh(mesh.devices.reshape(SIDE, SIDE, 2, LONG), ("y", "x", "core", "z"))
    seq = ("y", "x", "core")
    wide = P(seq, "z")
    return jax.shard_map(
        body,
        mesh=fine,
        in_specs=(wide, wide, wide, P("z", seq), P(), wide, wide),
        out_specs=(wide,) * 5,
        check_vma=False,
    )
```

time: 681 us -> 183 us (0.27)
  the two profiles are of different devices: /device:TPU:39 before, /device:TPU:103 now
where the time goes in v1:
time: 183 us
  starting transfers between devices  80.8 us (44%)
  waiting for transfers between devices  59.5 us (33%)
  between operations  14.6 us (8%)
  Pallas kernels  14 us (8%)
  local copies, waits for them, and re-layouts  11.5 us (6%)
  other arithmetic  2.37 us (1%)
    ppermute x35, waiting for transfers between devices, ring(): lax.ppermute(value, axis, [(i, (i + steps) % count) for i in range(count)])  50.2 us
    ppermute x35, starting transfers between devices, ring(): lax.ppermute(value, axis, [(i, (i + steps) % count) for i in range(count)])  48.8 us
    ppermute x10, starting transfers between devices, line(): return lax.ppermute(value, ('y', 'x', 'core'), pairs)  32 us
    ppermute x10, waiting for transfers between devices, line(): return lax.ppermute(value, ('y', 'x', 'core'), pairs)  9.26 us
    unnamed x34, local copies, waits for them, and re-layouts  8.51 us
  transfers between devices with their start and end apart: 46, of which 16 were waited for; matrix products, arithmetic and copies ran while one was open for 4% of the time, Pallas kernels for 6%

profile of v1, /device:TPU:103, one launch (start us, length us, event | category | flops | bytes accessed | tf_op | source)
XLA Modules:
  0.0 182.7 jit_solution(16343182749167003272)
XLA Ops:
  11.5 2.3 %shard_map.110 = (bf16[528,128]{1,0:T(8,128)(2,1)S(1)}, f32[256,512]{1,0:T(8,128)S(1)}) custom-call(s32[16]{0:T(128)S(1)} %copy-done.5, s32[4]{0:T(128)S(1)} %pad_add_fusion.at_ref, f32[4,256]{1,0:T(4,128)S(1)} %copy-done.3, bf16[256,512]{1,0:T(8,128)(2,1)S(1)} %copy-done.1, bf16[256,512]{1,0:T(8,128)(2,1)S(1)} %copy-done.7, bf16[256,512]{1,0:T(8,128)(2,1)S(1)} %copy-done.9), custom_call_target="tpu_custom_call" | custom-call | flops 268435456 | bytes 1048576 | tf_op jit(solution)/shard_map/pallas_call | solution.py:268
  13.8 3.8 %collective-permute-start = (bf16[528,128]{1,0:T(8,128)(2,1)S(1)}, bf16[528,128]{1,0:T(8,128)(2,1)S(1)}, u32[]{:S(2)}, u32[]{:S(2)}) collective-permute-start(bf16[528,128]{1,0:T(8,128)(2,1)S(1)} %get-tuple-element.19.a_ref), channel_id=1, source_target_pairs={{0,8},{8,16},{16,24},{24,32},{32,40},{40,48},{48,56},{56,64},{64,7... | collective-permute-start | bytes 405512 | tf_op jit(solution)/shard_map/ppermute | solution.py:225
  17.6 3.1 %collective-permute-start.1 = (bf16[528,128]{1,0:T(8,128)(2,1)S(1)}, bf16[528,128]{1,0:T(8,128)(2,1)S(1)}, u32[]{:S(2)}, u32[]{:S(2)}) collective-permute-start(bf16[528,128]{1,0:T(8,128)(2,1)S(1)} %get-tuple-element.19.a_ref), channel_id=1, source_target_pairs={{0,16},{8,24},{16,32},{24,40},{32,48},{40,56},{48,64},{56,72},{64,... | collective-permute-start | bytes 405512 | tf_op jit(solution)/shard_map/ppermute | solution.py:225
  24.5 2.0 %collective-permute-start.14 = (bf16[128,256]{1,0:T(8,128)(2,1)S(1)}, bf16[128,256]{1,0:T(8,128)(2,1)S(1)}, u32[]{:S(2)}, u32[]{:S(2)}) collective-permute-start(bf16[128,256]{1,0:T(8,128)(2,1)S(1)} %get-tuple-element.61), channel_id=1, source_target_pairs={{0,192},{64,0},{128,64},{192,128},{1,193},{65,1},{129,65},{193,129... | collective-permute-start | bytes 196616 | tf_op jit(solution)/shard_map/ppermute | solution.py:219
  28.3 3.5 %collective-permute-start.2 = (bf16[528,128]{1,0:T(8,128)(2,1)S(1)}, bf16[528,128]{1,0:T(8,128)(2,1)S(1)}, u32[]{:S(2)}, u32[]{:S(2)}) collective-permute-start(bf16[528,128]{1,0:T(8,128)(2,1)S(1)} %shard_map.111), channel_id=1, source_target_pairs={{0,8},{8,16},{16,24},{24,32},{32,40},{40,48},{48,56},{56,64},{64,7... | collective-permute-start | bytes 405512 | tf_op jit(solution)/shard_map/ppermute | solution.py:225
  34.6 3.4 %collective-permute-done.7 = bf16[128,256]{1,0:T(8,128)(2,1)S(1)} collective-permute-done((bf16[128,256]{1,0:T(8,128)(2,1)S(1)}, bf16[128,256]{1,0:T(8,128)(2,1)S(1)}, u32[]{:S(2)}, u32[]{:S(2)}) %collective-permute-start.7) | collective-permute-done | bytes 65568 | tf_op jit(solution)/shard_map/ppermute | solution.py:219
  39.5 5.1 %collective-permute-start.17 = (bf16[4,128,256]{2,1,0:T(8,128)(2,1)S(1)}, bf16[4,128,256]{2,1,0:T(8,128)(2,1)S(1)}, u32[]{:S(2)}, u32[]{:S(2)}) collective-permute-start(bf16[4,128,256]{2,1,0:T(8,128)(2,1)S(1)} %get-tuple-element.52), channel_id=1, source_target_pairs={{0,48},{16,0},{32,16},{48,32},{1,49},{17,1},{33,17},{49,33},{2,50}... | collective-permute-start | bytes 786440 | tf_op jit(solution)/shard_map/ppermute | solution.py:219
  44.6 3.5 %collective-permute-start.3 = (bf16[528,128]{1,0:T(8,128)(2,1)S(1)}, bf16[528,128]{1,0:T(8,128)(2,1)S(1)}, u32[]{:S(2)}, u32[]{:S(2)}) collective-permute-start(bf16[528,128]{1,0:T(8,128)(2,1)S(1)} %shard_map.111), channel_id=1, source_target_pairs={{0,32},{8,40},{16,48},{24,56},{32,64},{40,72},{48,80},{56,88},{64,... | collective-permute-start | bytes 405512 | tf_op jit(solution)/shard_map/ppermute | solution.py:225
  48.1 3.8 %collective-permute-start.4 = (bf16[528,128]{1,0:T(8,128)(2,1)S(1)}, bf16[528,128]{1,0:T(8,128)(2,1)S(1)}, u32[]{:S(2)}, u32[]{:S(2)}) collective-permute-start(bf16[528,128]{1,0:T(8,128)(2,1)S(1)} %shard_map.111), channel_id=1, source_target_pairs={{0,56},{8,64},{16,72},{24,80},{32,88},{40,96},{48,104},{56,112},{6... | collective-permute-start | bytes 405512 | tf_op jit(solution)/shard_map/ppermute | solution.py:225
  52.0 3.9 %collective-permute-done.3.b_ref = bf16[528,128]{1,0:T(8,128)(2,1)S(1)} collective-permute-done((bf16[528,128]{1,0:T(8,128)(2,1)S(1)}, bf16[528,128]{1,0:T(8,128)(2,1)S(1)}, u32[]{:S(2)}, u32[]{:S(2)}) %collective-permute-start.3) | collective-permute-done | bytes 135200 | tf_op jit(solution)/shard_map/ppermute | solution.py:225
  60.2 3.1 %collective-permute-start.20 = (bf16[512,256]{1,0:T(8,128)(2,1)S(1)}, bf16[512,256]{1,0:T(8,128)(2,1)}, u32[]{:S(2)}, u32[]{:S(2)}) collective-permute-start(bf16[512,256]{1,0:T(8,128)(2,1)S(1)} %pad_maximum_fusion.5), channel_id=1, source_target_pairs={{0,1},{1,2},{2,3},{3,4},{4,5},{5,6},{6,7},{7,0},{8,9},{9,10},{10,1... | collective-permute-start | bytes 786440 | tf_op jit(solution)/shard_map/ppermute | solution.py:219
  65.3 2.2 %collective-permute-done.11 = bf16[4,128,256]{2,1,0:T(8,128)(2,1)S(1)} collective-permute-done((bf16[4,128,256]{2,1,0:T(8,128)(2,1)S(1)}, bf16[4,128,256]{2,1,0:T(8,128)(2,1)S(1)}, u32[]{:S(2)}, u32[]{:S(2)}) %collective-permute-start.11) | collective-permute-done | bytes 262176 | tf_op jit(solution)/shard_map/ppermute | solution.py:219
  67.5 3.6 %collective-permute-done.9 = bf16[4,128,256]{2,1,0:T(8,128)(2,1)S(1)} collective-permute-done((bf16[4,128,256]{2,1,0:T(8,128)(2,1)S(1)}, bf16[4,128,256]{2,1,0:T(8,128)(2,1)S(1)}, u32[]{:S(2)}, u32[]{:S(2)}) %collective-permute-start.9) | collective-permute-done | bytes 262176 | tf_op jit(solution)/shard_map/ppermute | solution.py:219
  71.3 2.9 %collective-permute-start.21 = (bf16[512,256]{1,0:T(8,128)(2,1)}, bf16[512,256]{1,0:T(8,128)(2,1)}, u32[]{:S(2)}, u32[]{:S(2)}) collective-permute-start(bf16[512,256]{1,0:T(8,128)(2,1)} %collective-permute-done.20), channel_id=1, source_target_pairs={{0,1},{1,2},{2,3},{3,4},{4,5},{5,6},{6,7},{7,0},{8,9},{9,10},{10,1... | collective-permute-start | bytes 786440 | tf_op jit(solution)/shard_map/ppermute | solution.py:219
  79.5 3.4 %collective-permute-start.22 = (bf16[512,256]{1,0:T(8,128)(2,1)}, bf16[512,256]{1,0:T(8,128)(2,1)S(1)}, u32[]{:S(2)}, u32[]{:S(2)}) collective-permute-start(bf16[512,256]{1,0:T(8,128)(2,1)} %collective-permute-done.21), channel_id=1, source_target_pairs={{0,1},{1,2},{2,3},{3,4},{4,5},{5,6},{6,7},{7,0},{8,9},{9,10},{10,1... | collective-permute-start | bytes 786440 | tf_op jit(solution)/shard_map/ppermute | solution.py:219
  83.0 3.5 %collective-permute-done.24 = bf16[512,256]{1,0:T(8,128)(2,1)S(1)} collective-permute-done((bf16[512,256]{1,0:T(8,128)(2,1)S(1)}, bf16[512,256]{1,0:T(8,128)(2,1)S(1)}, u32[]{:S(2)}, u32[]{:S(2)}) %collective-permute-start.24) | collective-permute-done | bytes 262176 | tf_op jit(solution)/shard_map/ppermute | solution.py:219
  87.7 3.4 %collective-permute-start.23 = (bf16[512,256]{1,0:T(8,128)(2,1)S(1)}, bf16[512,256]{1,0:T(8,128)(2,1)S(1)}, u32[]{:S(2)}, u32[]{:S(2)}) collective-permute-start(bf16[512,256]{1,0:T(8,128)(2,1)S(1)} %collective-permute-done.22), channel_id=1, source_target_pairs={{0,1},{1,2},{2,3},{3,4},{4,5},{5,6},{6,7},{7,0},{8,9},{9,10},{10,1... | collective-permute-start | bytes 786440 | tf_op jit(solution)/shard_map/ppermute | solution.py:219
  92.1 8.5 %collective-permute-done.25 = bf16[512,256]{1,0:T(8,128)(2,1)S(1)} collective-permute-done((bf16[512,256]{1,0:T(8,128)(2,1)S(1)}, bf16[512,256]{1,0:T(8,128)(2,1)S(1)}, u32[]{:S(2)}, u32[]{:S(2)}) %collective-permute-start.25) | collective-permute-done | bytes 262176 | tf_op jit(solution)/shard_map/ppermute | solution.py:219
  100.7 13.5 %collective-permute-done.26 = bf16[512,256]{1,0:T(8,128)(2,1)S(1)} collective-permute-done((bf16[512,256]{1,0:T(8,128)(2,1)S(1)}, bf16[512,256]{1,0:T(8,128)(2,1)S(1)}, u32[]{:S(2)}, u32[]{:S(2)}) %collective-permute-start.26) | collective-permute-done | bytes 262176 | tf_op jit(solution)/shard_map/ppermute | solution.py:219
  116.1 3.9 %collective-permute-start.27 = (bf16[256,512]{1,0:T(8,128)(2,1)S(1)}, bf16[256,512]{1,0:T(8,128)(2,1)S(1)}, u32[]{:S(2)}, u32[]{:S(2)}) collective-permute-start(bf16[256,512]{1,0:T(8,128)(2,1)S(1)} %get-tuple-element.22), channel_id=1, source_target_pairs={{0,8},{8,0},{1,9},{9,1},{2,10},{10,2},{3,11},{11,3},{4,12},{12,4},... | collective-permute-start | bytes 786440 | tf_op jit(solution)/shard_map/ppermute | solution.py:219
  122.7 2.5 %collective-permute-start.35 = (bf16[4,128,256]{2,1,0:T(8,128)(2,1)S(1)}, bf16[4,128,256]{2,1,0:T(8,128)(2,1)S(1)}, u32[]{:S(2)}, u32[]{:S(2)}) collective-permute-start(bf16[4,128,256]{2,1,0:T(8,128)(2,1)S(1)} %get-tuple-element.32), channel_id=1, source_target_pairs={{0,192},{64,0},{128,64},{192,128},{1,193},{65,1},{129,65},{193,129... | collective-permute-start | bytes 786440 | tf_op jit(solution)/shard_map/ppermute | solution.py:219
  129.9 6.9 %collective-permute-done.33 = bf16[4,128,256]{2,1,0:T(8,128)(2,1)S(1)} collective-permute-done((bf16[4,128,256]{2,1,0:T(8,128)(2,1)S(1)}, bf16[4,128,256]{2,1,0:T(8,128)(2,1)S(1)}, u32[]{:S(2)}, u32[]{:S(2)}) %collective-permute-start.33) | collective-permute-done | bytes 262176 | tf_op jit(solution)/shard_map/ppermute | solution.py:219
  136.7 2.7 %collective-permute-start.28 = (bf16[528,128]{1,0:T(8,128)(2,1)S(1)}, bf16[528,128]{1,0:T(8,128)(2,1)S(1)}, u32[]{:S(2)}, u32[]{:S(2)}) collective-permute-start(bf16[528,128]{1,0:T(8,128)(2,1)S(1)} %get-tuple-element.25.a_ref), channel_id=1, source_target_pairs={{8,0},{16,8},{24,16},{32,24},{40,32},{48,40},{56,48},{64,56},{72,6... | collective-permute-start | bytes 405512 | tf_op jit(solution)/shard_map/ppermute | solution.py:225
  139.5 1.9 %collective-permute-start.29 = (bf16[528,128]{1,0:T(8,128)(2,1)S(1)}, bf16[528,128]{1,0:T(8,128)(2,1)S(1)}, u32[]{:S(2)}, u32[]{:S(2)}) collective-permute-start(bf16[528,128]{1,0:T(8,128)(2,1)S(1)} %get-tuple-element.25.a_ref), channel_id=1, source_target_pairs={{16,0},{24,8},{32,16},{40,24},{48,32},{56,40},{64,48},{72,56},{80,... | collective-permute-start | bytes 405512 | tf_op jit(solution)/shard_map/ppermute | solution.py:225
  141.6 2.4 %collective-permute-start.36 = (bf16[128,256]{1,0:T(8,128)(2,1)S(1)}, bf16[128,256]{1,0:T(8,128)(2,1)S(1)}, u32[]{:S(2)}, u32[]{:S(2)}) collective-permute-start(bf16[128,256]{1,0:T(8,128)(2,1)S(1)} %get-tuple-element.39), channel_id=1, source_target_pairs={{0,16},{16,32},{32,48},{48,0},{1,17},{17,33},{33,49},{49,1},{2,18}... | collective-permute-start | bytes 196616 | tf_op jit(solution)/shard_map/ppermute | solution.py:219
  146.9 3.8 %collective-permute-done.37 = bf16[128,256]{1,0:T(8,128)(2,1)S(1)} collective-permute-done((bf16[128,256]{1,0:T(8,128)(2,1)S(1)}, bf16[128,256]{1,0:T(8,128)(2,1)S(1)}, u32[]{:S(2)}, u32[]{:S(2)}) %collective-permute-start.37) | collective-permute-done | bytes 65568 | tf_op jit(solution)/shard_map/ppermute | solution.py:219
  152.7 2.7 %collective-permute-done.43 = bf16[128,256]{1,0:T(8,128)(2,1)S(1)} collective-permute-done((bf16[128,256]{1,0:T(8,128)(2,1)S(1)}, bf16[128,256]{1,0:T(8,128)(2,1)S(1)}, u32[]{:S(2)}, u32[]{:S(2)}) %collective-permute-start.43) | collective-permute-done | bytes 65568 | tf_op jit(solution)/shard_map/ppermute | solution.py:219
  155.5 3.7 %collective-permute-start.30 = (bf16[528,128]{1,0:T(8,128)(2,1)S(1)}, bf16[528,128]{1,0:T(8,128)(2,1)S(1)}, u32[]{:S(2)}, u32[]{:S(2)}) collective-permute-start(bf16[528,128]{1,0:T(8,128)(2,1)S(1)} %shard_map.116), channel_id=1, source_target_pairs={{8,0},{16,8},{24,16},{32,24},{40,32},{48,40},{56,48},{64,56},{72,6... | collective-permute-start | bytes 405512 | tf_op jit(solution)/shard_map/ppermute | solution.py:225
  159.3 3.9 %collective-permute-start.31 = (bf16[528,128]{1,0:T(8,128)(2,1)S(1)}, bf16[528,128]{1,0:T(8,128)(2,1)S(1)}, u32[]{:S(2)}, u32[]{:S(2)}) collective-permute-start(bf16[528,128]{1,0:T(8,128)(2,1)S(1)} %shard_map.116), channel_id=1, source_target_pairs={{32,0},{40,8},{48,16},{56,24},{64,32},{72,40},{80,48},{88,56},{96,... | collective-permute-start | bytes 405512 | tf_op jit(solution)/shard_map/ppermute | solution.py:225
  163.2 1.9 %collective-permute-start.32 = (bf16[528,128]{1,0:T(8,128)(2,1)S(1)}, bf16[528,128]{1,0:T(8,128)(2,1)S(1)}, u32[]{:S(2)}, u32[]{:S(2)}) collective-permute-start(bf16[528,128]{1,0:T(8,128)(2,1)S(1)} %shard_map.116), channel_id=1, source_target_pairs={{56,0},{64,8},{72,16},{80,24},{88,32},{96,40},{104,48},{112,56},{1... | collective-permute-start | bytes 405512 | tf_op jit(solution)/shard_map/ppermute | solution.py:225
  168.8 3.0 %collective-permute-done.32.c_ref = bf16[528,128]{1,0:T(8,128)(2,1)S(1)} collective-permute-done((bf16[528,128]{1,0:T(8,128)(2,1)S(1)}, bf16[528,128]{1,0:T(8,128)(2,1)S(1)}, u32[]{:S(2)}, u32[]{:S(2)}) %collective-permute-start.32) | collective-permute-done | bytes 135200 | tf_op jit(solution)/shard_map/ppermute | solution.py:225
  171.8 3.3 %shard_map.117 = (bf16[256,512]{1,0:T(8,128)(2,1)}, bf16[256,512]{1,0:T(8,128)(2,1)}, bf16[256,512]{1,0:T(8,128)(2,1)}) custom-call(s32[16]{0:T(128)S(1)} %copy-done.6, s32[4]{0:T(128)S(1)} %pad_add_fusion.at_ref, f32[4,256]{1,0:T(4,128)S(1)} %copy-done.4, bf16[256,512]{1,0:T(8,128)(2,1)S(1)} %copy-done.2, bf16[256,512]{1,0:T(8,128)(2,1)S(1)} %copy-done.8, ...), custom_call_target="tpu_custom_call" | custom-call | flops 536870912 | bytes 1048576 | tf_op jit(solution)/shard_map/pallas_call | solution.py:294
  (128 shorter events, 46.9 us)
Async XLA Ops:
  7.2 158.0 %reduce-scatter.2.cloned.1.call-start = ((), (), s32[]{:S(2)}) async-start(), calls=%async_computation.1 | async-start | bytes 2359296 | tf_op jit(solution)/shard_map/reduce_scatter | solution.py:280
  13.8 13.7 %collective-permute-start = (bf16[528,128]{1,0:T(8,128)(2,1)S(1)}, bf16[528,128]{1,0:T(8,128)(2,1)S(1)}, u32[]{:S(2)}, u32[]{:S(2)}) collective-permute-start(bf16[528,128]{1,0:T(8,128)(2,1)S(1)} %get-tuple-element.19.a_ref), channel_id=1, source_target_pairs={{0,8},{8,16},{16,24},{24,32},{32,40},{40,48},{48,56},{56,64},{64,7... | collective-permute-start | bytes 405512 | tf_op jit(solution)/shard_map/ppermute | solution.py:225
  17.6 10.0 %collective-permute-start.1 = (bf16[528,128]{1,0:T(8,128)(2,1)S(1)}, bf16[528,128]{1,0:T(8,128)(2,1)S(1)}, u32[]{:S(2)}, u32[]{:S(2)}) collective-permute-start(bf16[528,128]{1,0:T(8,128)(2,1)S(1)} %get-tuple-element.19.a_ref), channel_id=1, source_target_pairs={{0,16},{8,24},{16,32},{24,40},{32,48},{40,56},{48,64},{56,72},{64,... | collective-permute-start | bytes 405512 | tf_op jit(solution)/shard_map/ppermute | solution.py:225
  23.0 8.8 %collective-permute-start.13 = (bf16[128,256]{1,0:T(8,128)(2,1)S(1)}, bf16[128,256]{1,0:T(8,128)(2,1)S(1)}, u32[]{:S(2)}, u32[]{:S(2)}) collective-permute-start(bf16[128,256]{1,0:T(8,128)(2,1)S(1)} %get-tuple-element.61), channel_id=1, source_target_pairs={{0,128},{64,192},{128,0},{192,64},{1,129},{65,193},{129,1},{193,65... | collective-permute-start | bytes 196616 | tf_op jit(solution)/shard_map/ppermute | solution.py:219
  27.5 17.1 %collective-permute-start.19 = (bf16[256,256]{1,0:T(8,128)(2,1)S(1)}, bf16[256,256]{1,0:T(8,128)(2,1)S(1)}, u32[]{:S(2)}, u32[]{:S(2)}) collective-permute-start(bf16[256,256]{1,0:T(8,128)(2,1)S(1)} %get-tuple-element.46), channel_id=1, source_target_pairs={{0,8},{8,0},{1,9},{9,1},{2,10},{10,2},{3,11},{11,3},{4,12},{12,4},... | collective-permute-start | bytes 393224 | tf_op jit(solution)/shard_map/ppermute | solution.py:219
  28.3 19.8 %collective-permute-start.2 = (bf16[528,128]{1,0:T(8,128)(2,1)S(1)}, bf16[528,128]{1,0:T(8,128)(2,1)S(1)}, u32[]{:S(2)}, u32[]{:S(2)}) collective-permute-start(bf16[528,128]{1,0:T(8,128)(2,1)S(1)} %shard_map.111), channel_id=1, source_target_pairs={{0,8},{8,16},{16,24},{24,32},{32,40},{40,48},{48,56},{56,64},{64,7... | collective-permute-start | bytes 405512 | tf_op jit(solution)/shard_map/ppermute | solution.py:225
  31.9 26.8 %collective-permute-start.15 = (bf16[4,128,256]{2,1,0:T(8,128)(2,1)S(1)}, bf16[4,128,256]{2,1,0:T(8,128)(2,1)S(1)}, u32[]{:S(2)}, u32[]{:S(2)}) collective-permute-start(bf16[4,128,256]{2,1,0:T(8,128)(2,1)S(1)} %get-tuple-element.52), channel_id=1, source_target_pairs={{0,16},{16,32},{32,48},{48,0},{1,17},{17,33},{33,49},{49,1},{2,18}... | collective-permute-start | bytes 786440 | tf_op jit(solution)/shard_map/ppermute | solution.py:219
  38.0 22.2 %collective-permute-start.16 = (bf16[4,128,256]{2,1,0:T(8,128)(2,1)S(1)}, bf16[4,128,256]{2,1,0:T(8,128)(2,1)S(1)}, u32[]{:S(2)}, u32[]{:S(2)}) collective-permute-start(bf16[4,128,256]{2,1,0:T(8,128)(2,1)S(1)} %get-tuple-element.52), channel_id=1, source_target_pairs={{0,32},{16,48},{32,0},{48,16},{1,33},{17,49},{33,1},{49,17},{2,34}... | collective-permute-start | bytes 786440 | tf_op jit(solution)/shard_map/ppermute | solution.py:219
  39.5 23.8 %collective-permute-start.17 = (bf16[4,128,256]{2,1,0:T(8,128)(2,1)S(1)}, bf16[4,128,256]{2,1,0:T(8,128)(2,1)S(1)}, u32[]{:S(2)}, u32[]{:S(2)}) collective-permute-start(bf16[4,128,256]{2,1,0:T(8,128)(2,1)S(1)} %get-tuple-element.52), channel_id=1, source_target_pairs={{0,48},{16,0},{32,16},{48,32},{1,49},{17,1},{33,17},{49,33},{2,50}... | collective-permute-start | bytes 786440 | tf_op jit(solution)/shard_map/ppermute | solution.py:219
  44.6 11.3 %collective-permute-start.3 = (bf16[528,128]{1,0:T(8,128)(2,1)S(1)}, bf16[528,128]{1,0:T(8,128)(2,1)S(1)}, u32[]{:S(2)}, u32[]{:S(2)}) collective-permute-start(bf16[528,128]{1,0:T(8,128)(2,1)S(1)} %shard_map.111), channel_id=1, source_target_pairs={{0,32},{8,40},{16,48},{24,56},{32,64},{40,72},{48,80},{56,88},{64,... | collective-permute-start | bytes 405512 | tf_op jit(solution)/shard_map/ppermute | solution.py:225
  48.1 9.3 %collective-permute-start.4 = (bf16[528,128]{1,0:T(8,128)(2,1)S(1)}, bf16[528,128]{1,0:T(8,128)(2,1)S(1)}, u32[]{:S(2)}, u32[]{:S(2)}) collective-permute-start(bf16[528,128]{1,0:T(8,128)(2,1)S(1)} %shard_map.111), channel_id=1, source_target_pairs={{0,56},{8,64},{16,72},{24,80},{32,88},{40,96},{48,104},{56,112},{6... | collective-permute-start | bytes 405512 | tf_op jit(solution)/shard_map/ppermute | solution.py:225
  55.9 9.4 %collective-permute-start.10 = (bf16[4,128,256]{2,1,0:T(8,128)(2,1)S(1)}, bf16[4,128,256]{2,1,0:T(8,128)(2,1)S(1)}, u32[]{:S(2)}, u32[]{:S(2)}) collective-permute-start(bf16[4,128,256]{2,1,0:T(8,128)(2,1)S(1)} %get-tuple-element.54), channel_id=1, source_target_pairs={{0,128},{64,192},{128,0},{192,64},{1,129},{65,193},{129,1},{193,65... | collective-permute-start | bytes 786440 | tf_op jit(solution)/shard_map/ppermute | solution.py:219
  57.5 10.0 %collective-permute-start.11 = (bf16[4,128,256]{2,1,0:T(8,128)(2,1)S(1)}, bf16[4,128,256]{2,1,0:T(8,128)(2,1)S(1)}, u32[]{:S(2)}, u32[]{:S(2)}) collective-permute-start(bf16[4,128,256]{2,1,0:T(8,128)(2,1)S(1)} %get-tuple-element.54), channel_id=1, source_target_pairs={{0,192},{64,0},{128,64},{192,128},{1,193},{65,1},{129,65},{193,129... | collective-permute-start | bytes 786440 | tf_op jit(solution)/shard_map/ppermute | solution.py:219
  58.7 12.4 %collective-permute-start.9 = (bf16[4,128,256]{2,1,0:T(8,128)(2,1)S(1)}, bf16[4,128,256]{2,1,0:T(8,128)(2,1)S(1)}, u32[]{:S(2)}, u32[]{:S(2)}) collective-permute-start(bf16[4,128,256]{2,1,0:T(8,128)(2,1)S(1)} %get-tuple-element.54), channel_id=1, source_target_pairs={{0,64},{64,128},{128,192},{192,0},{1,65},{65,129},{129,193},{193,1... | collective-permute-start | bytes 786440 | tf_op jit(solution)/shard_map/ppermute | solution.py:219
  60.2 11.1 %collective-permute-start.20 = (bf16[512,256]{1,0:T(8,128)(2,1)S(1)}, bf16[512,256]{1,0:T(8,128)(2,1)}, u32[]{:S(2)}, u32[]{:S(2)}) collective-permute-start(bf16[512,256]{1,0:T(8,128)(2,1)S(1)} %pad_maximum_fusion.5), channel_id=1, source_target_pairs={{0,1},{1,2},{2,3},{3,4},{4,5},{5,6},{6,7},{7,0},{8,9},{9,10},{10,1... | collective-permute-start | bytes 786440 | tf_op jit(solution)/shard_map/ppermute | solution.py:219
  63.3 10.9 %collective-permute-start.5 = (bf16[256,512]{1,0:T(8,128)(2,1)S(1)}, bf16[256,512]{1,0:T(8,128)(2,1)S(1)}, u32[]{:S(2)}, u32[]{:S(2)}) collective-permute-start(bf16[256,512]{1,0:T(8,128)(2,1)S(1)} %get-tuple-element.20.own_ref), channel_id=1, source_target_pairs={{0,8},{8,0},{1,9},{9,1},{2,10},{10,2},{3,11},{11,3},{4,12},{12,4},... | collective-permute-start | bytes 786440 | tf_op jit(solution)/shard_map/ppermute | solution.py:219
  86.4 14.2 %collective-permute-start.25 = (bf16[512,256]{1,0:T(8,128)(2,1)S(1)}, bf16[512,256]{1,0:T(8,128)(2,1)S(1)}, u32[]{:S(2)}, u32[]{:S(2)}) collective-permute-start(bf16[512,256]{1,0:T(8,128)(2,1)S(1)} %collective-permute-done.24), channel_id=1, source_target_pairs={{0,7},{1,0},{2,1},{3,2},{4,3},{5,4},{6,5},{7,6},{8,15},{9,8},{10,9... | collective-permute-start | bytes 786440 | tf_op jit(solution)/shard_map/ppermute | solution.py:219
  87.7 12.9 %collective-permute-start.23 = (bf16[512,256]{1,0:T(8,128)(2,1)S(1)}, bf16[512,256]{1,0:T(8,128)(2,1)S(1)}, u32[]{:S(2)}, u32[]{:S(2)}) collective-permute-start(bf16[512,256]{1,0:T(8,128)(2,1)S(1)} %collective-permute-done.22), channel_id=1, source_target_pairs={{0,1},{1,2},{2,3},{3,4},{4,5},{5,6},{6,7},{7,0},{8,9},{9,10},{10,1... | collective-permute-start | bytes 786440 | tf_op jit(solution)/shard_map/ppermute | solution.py:219
  100.6 13.6 %collective-permute-start.26 = (bf16[512,256]{1,0:T(8,128)(2,1)S(1)}, bf16[512,256]{1,0:T(8,128)(2,1)S(1)}, u32[]{:S(2)}, u32[]{:S(2)}) collective-permute-start(bf16[512,256]{1,0:T(8,128)(2,1)S(1)} %collective-permute-done.25), channel_id=1, source_target_pairs={{0,7},{1,0},{2,1},{3,2},{4,3},{5,4},{6,5},{7,6},{8,15},{9,8},{10,9... | collective-permute-start | bytes 786440 | tf_op jit(solution)/shard_map/ppermute | solution.py:219
  116.1 11.1 %collective-permute-start.27 = (bf16[256,512]{1,0:T(8,128)(2,1)S(1)}, bf16[256,512]{1,0:T(8,128)(2,1)S(1)}, u32[]{:S(2)}, u32[]{:S(2)}) collective-permute-start(bf16[256,512]{1,0:T(8,128)(2,1)S(1)} %get-tuple-element.22), channel_id=1, source_target_pairs={{0,8},{8,0},{1,9},{9,1},{2,10},{10,2},{3,11},{11,3},{4,12},{12,4},... | collective-permute-start | bytes 786440 | tf_op jit(solution)/shard_map/ppermute | solution.py:219
  121.9 14.8 %collective-permute-start.33 = (bf16[4,128,256]{2,1,0:T(8,128)(2,1)S(1)}, bf16[4,128,256]{2,1,0:T(8,128)(2,1)S(1)}, u32[]{:S(2)}, u32[]{:S(2)}) collective-permute-start(bf16[4,128,256]{2,1,0:T(8,128)(2,1)S(1)} %get-tuple-element.31), channel_id=1, source_target_pairs={{0,64},{64,128},{128,192},{192,0},{1,65},{65,129},{129,193},{193,1... | collective-permute-start | bytes 786440 | tf_op jit(solution)/shard_map/ppermute | solution.py:219
  122.7 14.0 %collective-permute-start.34 = (bf16[4,128,256]{2,1,0:T(8,128)(2,1)S(1)}, bf16[4,128,256]{2,1,0:T(8,128)(2,1)S(1)}, u32[]{:S(2)}, u32[]{:S(2)}) collective-permute-start(bf16[4,128,256]{2,1,0:T(8,128)(2,1)S(1)} %get-tuple-element.33), channel_id=1, source_target_pairs={{0,128},{64,192},{128,0},{192,64},{1,129},{65,193},{129,1},{193,65... | collective-permute-start | bytes 786440 | tf_op jit(solution)/shard_map/ppermute | solution.py:219
  122.7 16.7 %collective-permute-start.35 = (bf16[4,128,256]{2,1,0:T(8,128)(2,1)S(1)}, bf16[4,128,256]{2,1,0:T(8,128)(2,1)S(1)}, u32[]{:S(2)}, u32[]{:S(2)}) collective-permute-start(bf16[4,128,256]{2,1,0:T(8,128)(2,1)S(1)} %get-tuple-element.32), channel_id=1, source_target_pairs={{0,192},{64,0},{128,64},{192,128},{1,193},{65,1},{129,65},{193,129... | collective-permute-start | bytes 786440 | tf_op jit(solution)/shard_map/ppermute | solution.py:219
  125.3 16.3 %collective-permute-start.39 = (bf16[4,128,256]{2,1,0:T(8,128)(2,1)S(1)}, bf16[4,128,256]{2,1,0:T(8,128)(2,1)S(1)}, u32[]{:S(2)}, u32[]{:S(2)}) collective-permute-start(bf16[4,128,256]{2,1,0:T(8,128)(2,1)S(1)} %get-tuple-element.34), channel_id=1, source_target_pairs={{0,16},{16,32},{32,48},{48,0},{1,17},{17,33},{33,49},{49,1},{2,18}... | collective-permute-start | bytes 786440 | tf_op jit(solution)/shard_map/ppermute | solution.py:219
  127.2 16.8 %collective-permute-start.40 = (bf16[4,128,256]{2,1,0:T(8,128)(2,1)S(1)}, bf16[4,128,256]{2,1,0:T(8,128)(2,1)S(1)}, u32[]{:S(2)}, u32[]{:S(2)}) collective-permute-start(bf16[4,128,256]{2,1,0:T(8,128)(2,1)S(1)} %get-tuple-element.36), channel_id=1, source_target_pairs={{0,32},{16,48},{32,0},{48,16},{1,33},{17,49},{33,1},{49,17},{2,34}... | collective-permute-start | bytes 786440 | tf_op jit(solution)/shard_map/ppermute | solution.py:219
  136.7 9.2 %collective-permute-start.41 = (bf16[4,128,256]{2,1,0:T(8,128)(2,1)S(1)}, bf16[4,128,256]{2,1,0:T(8,128)(2,1)S(1)}, u32[]{:S(2)}, u32[]{:S(2)}) collective-permute-start(bf16[4,128,256]{2,1,0:T(8,128)(2,1)S(1)} %get-tuple-element.35), channel_id=1, source_target_pairs={{0,48},{16,0},{32,16},{48,32},{1,49},{17,1},{33,17},{49,33},{2,50}... | collective-permute-start | bytes 786440 | tf_op jit(solution)/shard_map/ppermute | solution.py:219
  136.7 18.6 %collective-permute-start.28 = (bf16[528,128]{1,0:T(8,128)(2,1)S(1)}, bf16[528,128]{1,0:T(8,128)(2,1)S(1)}, u32[]{:S(2)}, u32[]{:S(2)}) collective-permute-start(bf16[528,128]{1,0:T(8,128)(2,1)S(1)} %get-tuple-element.25.a_ref), channel_id=1, source_target_pairs={{8,0},{16,8},{24,16},{32,24},{40,32},{48,40},{56,48},{64,56},{72,6... | collective-permute-start | bytes 405512 | tf_op jit(solution)/shard_map/ppermute | solution.py:225
  139.5 15.9 %collective-permute-start.29 = (bf16[528,128]{1,0:T(8,128)(2,1)S(1)}, bf16[528,128]{1,0:T(8,128)(2,1)S(1)}, u32[]{:S(2)}, u32[]{:S(2)}) collective-permute-start(bf16[528,128]{1,0:T(8,128)(2,1)S(1)} %get-tuple-element.25.a_ref), channel_id=1, source_target_pairs={{16,0},{24,8},{32,16},{40,24},{48,32},{56,40},{64,48},{72,56},{80,... | collective-permute-start | bytes 405512 | tf_op jit(solution)/shard_map/ppermute | solution.py:225
  155.5 11.5 %collective-permute-start.30 = (bf16[528,128]{1,0:T(8,128)(2,1)S(1)}, bf16[528,128]{1,0:T(8,128)(2,1)S(1)}, u32[]{:S(2)}, u32[]{:S(2)}) collective-permute-start(bf16[528,128]{1,0:T(8,128)(2,1)S(1)} %shard_map.116), channel_id=1, source_target_pairs={{8,0},{16,8},{24,16},{32,24},{40,32},{48,40},{56,48},{64,56},{72,6... | collective-permute-start | bytes 405512 | tf_op jit(solution)/shard_map/ppermute | solution.py:225
  159.3 9.5 %collective-permute-start.31 = (bf16[528,128]{1,0:T(8,128)(2,1)S(1)}, bf16[528,128]{1,0:T(8,128)(2,1)S(1)}, u32[]{:S(2)}, u32[]{:S(2)}) collective-permute-start(bf16[528,128]{1,0:T(8,128)(2,1)S(1)} %shard_map.116), channel_id=1, source_target_pairs={{32,0},{40,8},{48,16},{56,24},{64,32},{72,40},{80,48},{88,56},{96,... | collective-permute-start | bytes 405512 | tf_op jit(solution)/shard_map/ppermute | solution.py:225
  163.2 8.6 %collective-permute-start.32 = (bf16[528,128]{1,0:T(8,128)(2,1)S(1)}, bf16[528,128]{1,0:T(8,128)(2,1)S(1)}, u32[]{:S(2)}, u32[]{:S(2)}) collective-permute-start(bf16[528,128]{1,0:T(8,128)(2,1)S(1)} %shard_map.116), channel_id=1, source_target_pairs={{56,0},{64,8},{72,16},{80,24},{88,32},{96,40},{104,48},{112,56},{1... | collective-permute-start | bytes 405512 | tf_op jit(solution)/shard_map/ppermute | solution.py:225
  166.2 8.9 %collective-permute-start.18 = (bf16[256,256]{1,0:T(8,128)(2,1)S(1)}, bf16[256,256]{1,0:T(8,128)(2,1)S(1)}, u32[]{:S(2)}, u32[]{:S(2)}) collective-permute-start(bf16[256,256]{1,0:T(8,128)(2,1)S(1)} %slice_bitcast_fusion.6), channel_id=1, source_target_pairs={{0,8},{8,0},{1,9},{9,1},{2,10},{10,2},{3,11},{11,3},{4,12},{12,4},... | collective-permute-start | bytes 393224 | tf_op jit(solution)/shard_map/ppermute | solution.py:219
  (28 other events, 312.2 us)
Sparse Core Ops, SparseCore 0:
  77.5 43.6 reduce-scatter.1

commit v2 on v1

--- a/solution.py
+++ b/solution.py
@@ -111,10 +111,41 @@
     return states, factors
 
 
-def chain(a_ref, b_ref, c_ref):
-    (sa, fa), (sb, fb), (sc, fc) = take(a_ref), take(b_ref), take(c_ref)
-    states = [sa[h] + fa[h] * (sb[h] + fb[h] * sc[h]) for h in range(HEADS)]
-    return states, [fa[h] * fb[h] * fc[h] for h in range(HEADS)]
+def pick(flag, a, b):
+    return jnp.where(flag, a, b)
+
+
+def fold(outer, inner):
+    (so, fo), (si, fi) = outer, inner
+    return [so[h] + fo[h] * si[h] for h in range(HEADS)], [fo[h] * fi[h] for h in range(HEADS)]
+
+
+def ordered(flag, a_ref, b_ref):
+    (sa, fa), (sb, fb) = take(a_ref), take(b_ref)
+    one = [pick(flag, p, q) for p, q in zip(sa, sb)], [pick(flag, p, q) for p, q in zip(fa, fb)]
+    two = [pick(flag, q, p) for p, q in zip(sa, sb)], [pick(flag, q, p) for p, q in zip(fa, fb)]
+    return one, two
+
+
+def put(ref, folded):
+    states, factors = folded
+    for h in range(HEADS):
+        ref[head(h), :] = states[h].astype(BF16)
+    put_factors(ref, factors)
+
+
+def chip_kernel(outer, at_ref, own_ref, other_ref, pay_ref):
+    put(pay_ref, fold(*ordered(at_ref[4] == outer, own_ref, other_ref)))
+
+
+def pair_kernel(a_ref, b_ref, pay_ref):
+    put(pay_ref, fold(take(a_ref), take(b_ref)))
+
+
+def entering(outer, at_ref, own_ref, other_ref, sibling_ref):
+    states, _ = fold(*ordered(at_ref[4] == 0, own_ref, other_ref))
+    near, factors = take(sibling_ref)
+    return [pick(at_ref[4] == outer, near[h] + factors[h] * states[h], states[h]) for h in range(HEADS)]
 
 
 def first_kernel(len_ref, at_ref, ld_ref, q_ref, k_ref, v_ref, pay_ref, local_ref):
@@ -128,16 +159,9 @@
     put_factors(pay_ref, [m.through(h) for h in range(HEADS)])
 
 
-def window_kernel(a_ref, b_ref, c_ref, pay_ref):
-    states, factors = chain(a_ref, b_ref, c_ref)
-    for h in range(HEADS):
-        pay_ref[head(h), :] = states[h].astype(BF16)
-    put_factors(pay_ref, factors)
-
-
 def attend_kernel(len_ref, at_ref, ld_ref, q_ref, local_ref, a_ref, b_ref, c_ref, att_ref, state_ref):
     m = Masks(len_ref, at_ref, ld_ref)
-    states, _ = chain(a_ref, b_ref, c_ref)
+    states = entering(1, at_ref, a_ref, b_ref, c_ref)
     for h in range(HEADS):
         state = states[h].astype(BF16)
         state_ref[head(h), :] = state
@@ -159,7 +183,7 @@
     len_ref, at_ref, ld_ref, q_ref, k_ref, v_ref, g_ref, state_ref, a_ref, b_ref, c_ref, dq_ref, dk_ref, dv_ref
 ):
     m = Masks(len_ref, at_ref, ld_ref)
-    carries, _ = chain(a_ref, b_ref, c_ref)
+    carries = entering(0, at_ref, a_ref, b_ref, c_ref)
     for h in range(HEADS):
         q, k, v, g = (r[:, head(h)] for r in (q_ref, k_ref, v_ref, g_ref))
         decay, leave, carry = m.decay(h), m.leave(h), carries[h].astype(BF16)
@@ -179,39 +203,39 @@
     return dy, [lax.rem(sign * (near + e - x) + SIDE, SIDE) for e in range(2)]
 
 
-def weight_part(wa_ref, wb_ref, j, at_ref):
+def place(at_ref, along_y, along_x):
+    flip = at_ref[4] == 0
+    return pick(flip, along_y, along_x), pick(flip, along_x, along_y)
+
+
+def weight_part(w_ref, j, at_ref):
     ry, rx = chip_of(j, at_ref[1], at_ref[2], -1)
-    left = jnp.concatenate([wa_ref[ry, r] for r in rx], axis=0)
-    right = jnp.concatenate([wb_ref[r, ry] for r in rx], axis=0)
-    return jnp.concatenate([left, right], axis=1)
-
-
-def pull_kernel(at_ref, g_ref, wa_ref, wb_ref, own_ref, send_ref):
+    return jnp.concatenate([w_ref[place(at_ref, ry, r)] for r in rx], axis=0)
+
+
+def pull_kernel(at_ref, g_ref, w_ref, own_ref, send_ref):
     total = jnp.zeros((2 * ROWS, STATE), F32)
     for j in range(LONG):
-        slot = lax.rem(at_ref[3] - j + LONG, LONG)
-        total = total + dot(g_ref[slot], weight_part(wa_ref, wb_ref, j, at_ref), NN)
+        total = total + dot(g_ref[j], weight_part(w_ref, j, at_ref), NN)
     own_ref[...] = total[:ROWS]
     send_ref[...] = total[ROWS:].astype(BF16)
 
 
-def mix_kernel(at_ref, own_ref, other_ref, wa_ref, wb_ref, out_ref):
+def mix_kernel(at_ref, own_ref, other_ref, w_ref, out_ref):
     for j in range(LONG):
-        w = weight_part(wa_ref, wb_ref, j, at_ref)
+        w = weight_part(w_ref, j, at_ref)
         out_ref[j, :ROWS] = dot(own_ref[...], w, NT).astype(BF16)
         out_ref[j, ROWS:] = dot(other_ref[...], w, NT).astype(BF16)
 
 
-def weight_grad_kernel(at_ref, g_ref, own_ref, other_ref, ra_ref, rb_ref):
+def weight_grad_kernel(at_ref, g_ref, own_ref, other_ref, r_ref):
     for j in range(LONG):
-        slot = lax.rem(at_ref[3] - j + LONG, LONG)
         dy, dx = chip_of(j, at_ref[1], at_ref[2], 1)
-        part = dot(g_ref[slot, :ROWS], own_ref[...], TN) + dot(g_ref[slot, ROWS:], other_ref[...], TN)
+        part = dot(g_ref[j, :ROWS], own_ref[...], TN) + dot(g_ref[j, ROWS:], other_ref[...], TN)
         part = part.astype(BF16)
         for e in range(2):
             rows = slice(e * HD, (e + 1) * HD)
-            ra_ref[dy, dx[e]] = part[rows, :HALF]
-            rb_ref[dx[e], dy] = part[rows, HALF:]
+            r_ref[place(at_ref, dy, dx[e])] = part[rows]
 
 
 def ring(value, axis, steps):
@@ -219,31 +243,44 @@
     return lax.ppermute(value, axis, [(i, (i + steps) % count) for i in range(count)])
 
 
-def line(value, steps):
-    count = SIDE * SIDE * 2
-    pairs = [(i, i + steps) for i in range(count) if 0 <= i + steps < count]
-    return lax.ppermute(value, ("y", "x", "core"), pairs)
-
-
-def gather_side(value, axis):
-    return jnp.stack([value] + [ring(value, axis, s) for s in (1, 2, -1)])
-
-
-def scatter_side(value, axis):
-    parts = [value[0]] + [ring(value[s], axis, s if s < 3 else -1) for s in (1, 2, 3)]
+SEQ = ("y", "x", "core")
+
+
+def cross(value, axes, steps):
+    pairs = []
+    for y in range(SIDE):
+        for x in range(SIDE):
+            for c in range(2):
+                up, on = ((y + steps) % SIDE, x) if axes[c] == "y" else (y, (x + steps) % SIDE)
+                pairs.append(((y * SIDE + x) * 2 + c, (up * SIDE + on) * 2 + c))
+    return lax.ppermute(value, SEQ, pairs)
+
+
+def line(value, near, far):
+    pairs = []
+    for c, steps in enumerate((near, far)):
+        pairs += [(2 * i + c, 2 * (i + steps) + c) for i in range(SIDE * SIDE) if 0 <= i + steps < SIDE * SIDE]
+    return lax.ppermute(value, SEQ, pairs)
+
+
+def gather_side(value, axes):
+    return jnp.stack([value] + [cross(value, axes, s) for s in (1, 2, 3)])
+
+
+def scatter_side(value, axes):
+    parts = [value[0]] + [cross(value[s], axes, s) for s in (1, 2, 3)]
     return functools.reduce(jnp.add, [p.astype(F32) for p in parts])
 
 
-def gather_long(value):
-    found = {0: value}
-    right = left = value
-    for s in range(1, LONG // 2 + 1):
-        right = ring(right, "z", 1)
-        found[s] = right
-        if s < LONG // 2:
-            left = ring(left, "z", -1)
-            found[LONG - s] = left
-    return jnp.stack([found[s] for s in range(LONG)])
+def relay(at, pay, way, outer):
+    sibling = swap(pay)
+    [chip] = call(functools.partial(chip_kernel, outer), [((PAY, HD), BF16)], [SMEM] + [VMEM] * 2, 2**20)(
+        at, pay, sibling
+    )
+    [share] = call(pair_kernel, [((PAY, HD), BF16)], [VMEM] * 2, 2**20)(
+        line(chip, way, 3 * way), line(chip, 2 * way, 4 * way)
+    )
+    return share, swap(share), sibling
 
 
 def swap(value):
@@ -256,45 +293,40 @@
 
 def body(q, k, v, log_decay, lengths, weight, out_grad):
     y, x, c, z = (lax.axis_index(a) for a in ("y", "x", "core", "z"))
-    at = jnp.stack([((y * SIDE + x) * 2 + c) * ROWS, y, x, z]).astype(jnp.int32)
+    at = jnp.stack([((y * SIDE + x) * 2 + c) * ROWS, y, x, z, c]).astype(jnp.int32)
     lead = (lengths, at, log_decay)
     lead_specs = [SMEM, SMEM, VMEM]
     even, odd = parity(out_grad)
     mine, yours = jnp.where(c == 0, even, odd), jnp.where(c == 0, odd, even)
-    grads = gather_long(jnp.concatenate([mine, swap(yours)], axis=0))
-    wa = gather_side(gather_side(weight[:, :HALF], "x"), "y")
-    wb = gather_side(gather_side(weight[:, HALF:], "y"), "x")
+    grads = lax.all_gather(jnp.concatenate([mine, swap(yours)], axis=0), "z")
+    w = gather_side(gather_side(weight, "xy"), "yx")
     wide = ((ROWS, STATE), BF16)
     pay, local = call(
         first_kernel, [((PAY, HD), BF16), ((ROWS, STATE), F32)], lead_specs + [VMEM] * 3, 2**28
     )(*lead, q, k, v)
-    window = call(window_kernel, [((PAY, HD), BF16)], [VMEM] * 3, 2**20)
-    [pay] = window(pay, line(pay, 1), line(pay, 2))
     att, state = call(attend_kernel, [wide, ((STATE, HD), BF16)], lead_specs + [VMEM] * 5, 2**26)(
-        *lead, q, local, line(pay, 1), line(pay, 4), line(pay, 7)
+        *lead, q, local, *relay(at, pay, 1, 1)
     )
     att_other = swap(att)
-    [mixed] = call(mix_kernel, [((LONG, 2 * ROWS, HALF), BF16)], [SMEM] + [VMEM] * 4, 2**30)(
-        at, att, att_other, wa, wb
+    [mixed] = call(mix_kernel, [((LONG, 2 * ROWS, HALF), BF16)], [SMEM] + [VMEM] * 3, 2**30)(
+        at, att, att_other, w
     )
     mixed = lax.psum_scatter(mixed, "z", scatter_dimension=0)
     mixed_other = swap(mixed[ROWS:])
     mixed = mixed[:ROWS]
     even, odd = jnp.where(c == 0, mixed, mixed_other), jnp.where(c == 0, mixed_other, mixed)
     mixed = jnp.concatenate([even[:, :HD], odd[:, :HD], even[:, HD:], odd[:, HD:]], axis=1)
-    own, send = call(pull_kernel, [((ROWS, STATE), F32), wide], [SMEM] + [VMEM] * 3, 2**30)(at, grads, wa, wb)
+    own, send = call(pull_kernel, [((ROWS, STATE), F32), wide], [SMEM] + [VMEM] * 2, 2**30)(at, grads, w)
     back, g = call(back_kernel, [((PAY, HD), BF16), wide], lead_specs + [VMEM] * 3, 2**26)(
         *lead, q, own, swap(send)
     )
-    [back] = window(back, line(back, -1), line(back, -2))
-    grid = ((SIDE, SIDE, HD, HALF), BF16)
-    ra, rb = call(weight_grad_kernel, [grid, grid], [SMEM] + [VMEM] * 3, 2**30)(at, grads, att, att_other)
-    ra = scatter_side(scatter_side(ra, "y").astype(BF16), "x")
-    rb = scatter_side(scatter_side(rb, "x").astype(BF16), "y")
+    grid = ((SIDE, SIDE, HD, STATE), BF16)
+    [r] = call(weight_grad_kernel, [grid], [SMEM] + [VMEM] * 3, 2**30)(at, grads, att, att_other)
+    r = scatter_side(scatter_side(r, "yx").astype(BF16), "xy")
     dq, dk, dv = call(grads_kernel, [wide] * 3, lead_specs + [VMEM] * 8, 2**29)(
-        *lead, q, k, v, g, state, line(back, -1), line(back, -4), line(back, -7)
-    )
-    return mixed, dq, dk, dv, jnp.concatenate([ra, rb], axis=1)
+        *lead, q, k, v, g, state, *relay(at, back, -1, 0)
+    )
+    return mixed, dq, dk, dv, r
 
 
 def solution(mesh):

time: 183 us -> 112 us (0.61)
  the two profiles are of different devices: /device:TPU:103 before, /device:TPU:1 now
where the time goes in v2:
time: 112 us
  starting transfers between devices  41.7 us (37%)
  waiting for transfers between devices  29.7 us (27%)
  Pallas kernels  15.1 us (13%)
  between operations  14.3 us (13%)
  other arithmetic  6 us (5%)
  local copies, waits for them, and re-layouts  5.21 us (5%)
    ppermute x8, starting transfers between devices, ring(): lax.ppermute(value, axis, [(i, (i + steps) % count) for i in range(count)])  19.1 us
    ppermute x12, starting transfers between devices, cross(): return lax.ppermute(value, SEQ, pairs)  14.2 us
    reduce_scatter x1, waiting for transfers between devices, body(): mixed = lax.psum_scatter(mixed, 'z', scatter_dimension=0)  10.2 us
    ppermute x4, starting transfers between devices, line(): return lax.ppermute(value, SEQ, pairs)  8.3 us
    ppermute x12, waiting for transfers between devices, cross(): return lax.ppermute(value, SEQ, pairs)  7.38 us
    ppermute x4, waiting for transfers between devices, line(): return lax.ppermute(value, SEQ, pairs)  6.58 us
    ppermute x8, waiting for transfers between devices, ring(): lax.ppermute(value, axis, [(i, (i + steps) % count) for i in range(count)])  5.48 us
    another operation x2, other arithmetic, gather_side(): return jnp.stack([value] + [cross(value, axes, s) for s in (1, 2, 3)])  3.42 us
  transfers between devices with their start and end apart: 26, of which 11 were waited for; matrix products, arithmetic and copies ran while one was open for 5% of the time, Pallas kernels for 14%

profile of v2, /device:TPU:1, one launch (start us, length us, event | category | flops | bytes accessed | tf_op | source)
XLA Modules:
  0.0 112.1 jit_solution(12100038534833974394)
XLA Ops:
  8.4 3.3 %collective-permute-start.12 = (bf16[256,256]{1,0:T(8,128)(2,1)S(1)}, bf16[256,256]{1,0:T(8,128)(2,1)S(1)}, u32[]{:S(2)}, u32[]{:S(2)}) collective-permute-start(bf16[256,256]{1,0:T(8,128)(2,1)S(1)} %get-tuple-element.38), channel_id=1, source_target_pairs={{0,8},{8,0},{1,9},{9,1},{2,10},{10,2},{3,11},{11,3},{4,12},{12,4},... | collective-permute-start | bytes 393224 | tf_op jit(solution)/shard_map/ppermute | solution.py:243
  13.5 1.1 collective-permute-start.7
  15.6 2.3 %collective-permute-done.7 = bf16[128,512]{1,0:T(8,128)(2,1)S(1)} collective-permute-done((bf16[128,512]{1,0:T(8,128)(2,1)}, bf16[128,512]{1,0:T(8,128)(2,1)S(1)}, u32[]{:S(2)}, u32[]{:S(2)}) %collective-permute-start.7) | collective-permute-done | bytes 131104 | tf_op jit(solution)/shard_map/ppermute | solution.py:256
  17.9 2.5 %collective-permute-done.6 = bf16[128,512]{1,0:T(8,128)(2,1)S(1)} collective-permute-done((bf16[128,512]{1,0:T(8,128)(2,1)}, bf16[128,512]{1,0:T(8,128)(2,1)S(1)}, u32[]{:S(2)}, u32[]{:S(2)}) %collective-permute-start.6) | collective-permute-done | bytes 131104 | tf_op jit(solution)/shard_map/ppermute | solution.py:256
  20.4 1.4 %collective-permute-done.5 = bf16[128,512]{1,0:T(8,128)(2,1)S(1)} collective-permute-done((bf16[128,512]{1,0:T(8,128)(2,1)}, bf16[128,512]{1,0:T(8,128)(2,1)S(1)}, u32[]{:S(2)}, u32[]{:S(2)}) %collective-permute-start.5) | collective-permute-done | bytes 131104 | tf_op jit(solution)/shard_map/ppermute | solution.py:256
  21.8 1.8 %fusion.5 = (bf16[1,4,128,512]{3,2,1,0:T(8,128)(2,1)}, bf16[4,128,512]{2,1,0:T(8,128)(2,1)S(1)}) fusion(bf16[1,128,512]{2,1,0:T(8,128)(2,1)S(1)} %bitcast.48, bf16[1,128,512]{2,1,0:T(8,128)(2,1)S(1)} %bitcast.49, bf16[1,128,512]{2,1,0:T(8,128)(2,1)S(1)} %bitcast.50, bf16[1,128,512]{2,1,0:T(8,128)(2,1)} %bitcast.47), kind=kLoop, calls=%fused_computation.27 | loop fusion | flops 786432 | bytes 1572864 | tf_op jit(solution)/shard_map/stack | solution.py:267
  23.6 2.2 %collective-permute-start.10 = (bf16[4,128,512]{2,1,0:T(8,128)(2,1)S(1)}, bf16[4,128,512]{2,1,0:T(8,128)(2,1)}, u32[]{:S(2)}, u32[]{:S(2)}) collective-permute-start(bf16[4,128,512]{2,1,0:T(8,128)(2,1)S(1)} %get-tuple-element.34), channel_id=1, source_target_pairs={{0,192},{8,56},{16,208},{24,8},{32,224},{40,24},{48,240},{56,40},{... | collective-permute-start | bytes 1572872 | tf_op jit(solution)/shard_map/ppermute | solution.py:256
  27.0 2.3 %shard_map.110 = (bf16[528,128]{1,0:T(8,128)(2,1)S(1)}, f32[256,512]{1,0:T(8,128)S(1)}) custom-call(s32[16]{0:T(128)S(1)} %copy-done.4, s32[5]{0:T(128)S(1)} %stack.53.at_ref, f32[4,256]{1,0:T(4,128)S(1)} %copy-done.3, bf16[256,512]{1,0:T(8,128)(2,1)S(1)} %copy-done.2, bf16[256,512]{1,0:T(8,128)(2,1)S(1)} %copy-done.5, bf16[256,512]{1,0:T(8,128)(2,1)S(1)} %copy-done.6), custom_call_target="tpu_custom_call" | custom-call | flops 268435456 | bytes 1048576 | tf_op jit(solution)/shard_map/pallas_call | solution.py:304
  29.3 2.6 %collective-permute-start = (bf16[528,128]{1,0:T(8,128)(2,1)S(1)}, bf16[528,128]{1,0:T(8,128)(2,1)S(1)}, u32[]{:S(2)}, u32[]{:S(2)}) collective-permute-start(bf16[528,128]{1,0:T(8,128)(2,1)S(1)} %get-tuple-element.17.own_ref), channel_id=1, source_target_pairs={{0,8},{8,0},{1,9},{9,1},{2,10},{10,2},{3,11},{11,3},{4,12},{12,4},... | collective-permute-start | bytes 405512 | tf_op jit(solution)/shard_map/ppermute | solution.py:243
  33.6 2.2 %collective-permute-start.1 = (bf16[528,128]{1,0:T(8,128)(2,1)S(1)}, bf16[528,128]{1,0:T(8,128)(2,1)S(1)}, u32[]{:S(2)}, u32[]{:S(2)}) collective-permute-start(bf16[528,128]{1,0:T(8,128)(2,1)S(1)} %shard_map.111), channel_id=1, source_target_pairs={{0,16},{16,32},{32,48},{48,64},{64,80},{80,96},{96,112},{112,128},... | collective-permute-start | bytes 405512 | tf_op jit(solution)/shard_map/ppermute | solution.py:263
  35.8 3.5 %collective-permute-start.2 = (bf16[528,128]{1,0:T(8,128)(2,1)S(1)}, bf16[528,128]{1,0:T(8,128)(2,1)S(1)}, u32[]{:S(2)}, u32[]{:S(2)}) collective-permute-start(bf16[528,128]{1,0:T(8,128)(2,1)S(1)} %shard_map.111), channel_id=1, source_target_pairs={{0,32},{16,48},{32,64},{48,80},{64,96},{80,112},{96,128},{112,144}... | collective-permute-start | bytes 405512 | tf_op jit(solution)/shard_map/ppermute | solution.py:263
  39.3 6.6 %collective-permute-done.2.b_ref = bf16[528,128]{1,0:T(8,128)(2,1)S(1)} collective-permute-done((bf16[528,128]{1,0:T(8,128)(2,1)S(1)}, bf16[528,128]{1,0:T(8,128)(2,1)S(1)}, u32[]{:S(2)}, u32[]{:S(2)}) %collective-permute-start.2) | collective-permute-done | bytes 135200 | tf_op jit(solution)/shard_map/ppermute | solution.py:263
  46.1 1.3 %collective-permute-done.3.b_ref = bf16[528,128]{1,0:T(8,128)(2,1)S(1)} collective-permute-done((bf16[528,128]{1,0:T(8,128)(2,1)S(1)}, bf16[528,128]{1,0:T(8,128)(2,1)S(1)}, u32[]{:S(2)}, u32[]{:S(2)}) %collective-permute-start.3) | collective-permute-done | bytes 135200 | tf_op jit(solution)/shard_map/ppermute | solution.py:243
  47.4 1.2 %shard_map.113 = (bf16[256,512]{1,0:T(8,128)(2,1)S(1)}, bf16[512,128]{1,0:T(8,128)(2,1)S(1)}) custom-call(s32[16]{0:T(128)S(1)} %copy-done.4, s32[5]{0:T(128)S(1)} %stack.53.at_ref, f32[4,256]{1,0:T(4,128)S(1)} %copy-done.3, bf16[256,512]{1,0:T(8,128)(2,1)S(1)} %copy-done.2, f32[256,512]{1,0:T(8,128)S(1)} %get-tuple-element.16.local_ref, ...), custom_call_target="tpu_custom_call" | custom-call | flops 67108864 | bytes 1048576 | tf_op jit(solution)/shard_map/pallas_call | solution.py:307
  48.9 1.6 %pad_maximum_fusion.w_ref = bf16[4,4,128,512]{3,2,1,0:T(8,128)(2,1)S(1)} fusion(bf16[1,4,128,512]{3,2,1,0:T(8,128)(2,1)} %bitcast.12, bf16[1,4,128,512]{3,2,1,0:T(8,128)(2,1)} %bitcast.11, bf16[1,4,128,512]{3,2,1,0:T(8,128)(2,1)} %bitcast.10, bf16[1,4,128,512]{3,2,1,0:T(8,128)(2,1)S(1)} %copy-done.7), kind=kLoop, calls=%fused_computation | loop fusion | flops 3145728 | bytes 4194304 | tf_op jit(solution)/shard_map/stack | solution.py:267
  50.5 1.8 %shard_map.114 = bf16[8,512,256]{2,1,0:T(8,128)(2,1)S(1)} custom-call(s32[5]{0:T(128)S(1)} %stack.53.at_ref, bf16[256,512]{1,0:T(8,128)(2,1)S(1)} %get-tuple-element.18.own_ref, bf16[256,512]{1,0:T(8,128)(2,1)S(1)} %collective-permute-done.4.other_ref, bf16[4,4,128,512]{3,2,1,0:T(8,128)(2,1)S(1)} %pad_maximum_fusion.w_ref), custom_call_target="tpu_custom_call" | custom-call | flops 1073741824 | bytes 1048576 | tf_op jit(solution)/shard_map/pallas_call | solution.py:311
  52.3 1.3 %copy-done.1 = bf16[8,512,256]{2,1,0:T(8,128)(2,1)} copy-done((bf16[8,512,256]{2,1,0:T(8,128)(2,1)}, bf16[8,512,256]{2,1,0:T(8,128)(2,1)S(1)}, u32[]{:S(2)}) %copy-start.1) | copy-done | bytes 2097176
  53.7 1.6 %copy-done = bf16[4096,256]{1,0:T(8,128)(2,1)S(1)} copy-done((bf16[4096,256]{1,0:T(8,128)(2,1)S(1)}, bf16[4096,256]{1,0:T(8,128)(2,1)}, u32[]{:S(2)}) %copy-start) | copy-done | bytes 2097176
  55.3 1.8 %shard_map.120 = bf16[4,4,128,512]{3,2,1,0:T(8,128)(2,1)S(1)} custom-call(s32[5]{0:T(128)S(1)} %stack.53.at_ref, bf16[8,512,256]{2,1,0:T(8,128)(2,1)S(1)} %bitcast.45, bf16[256,512]{1,0:T(8,128)(2,1)S(1)} %get-tuple-element.18.own_ref, bf16[256,512]{1,0:T(8,128)(2,1)S(1)} %collective-permute-done.4.other_ref), custom_call_target="tpu_custom_call" | custom-call | flops 1073741824 | bytes 1048576 | tf_op jit(solution)/shard_map/pallas_call | solution.py:324
  57.2 2.8 %collective-permute-start.20 = (bf16[4,128,512]{2,1,0:T(8,128)(2,1)S(1)}, bf16[4,128,512]{2,1,0:T(8,128)(2,1)S(1)}, u32[]{:S(2)}, u32[]{:S(2)}) collective-permute-start(bf16[4,128,512]{2,1,0:T(8,128)(2,1)S(1)} %get-tuple-element.28), channel_id=1, source_target_pairs={{0,192},{8,56},{16,208},{24,8},{32,224},{40,24},{48,240},{56,40},{... | collective-permute-start | bytes 1572872 | tf_op jit(solution)/shard_map/ppermute | solution.py:256
  60.7 1.8 %shard_map.115 = (f32[256,512]{1,0:T(8,128)S(1)}, bf16[256,512]{1,0:T(8,128)(2,1)S(1)}) custom-call(s32[5]{0:T(128)S(1)} %stack.53.at_ref, bf16[8,512,256]{2,1,0:T(8,128)(2,1)S(1)} %bitcast.46, bf16[4,4,128,512]{3,2,1,0:T(8,128)(2,1)S(1)} %pad_maximum_fusion.w_ref), custom_call_target="tpu_custom_call" | custom-call | flops 1073741824 | bytes 1048576 | tf_op jit(solution)/shard_map/pallas_call | solution.py:319
  62.5 4.1 %collective-permute-start.13 = (bf16[256,512]{1,0:T(8,128)(2,1)S(1)}, bf16[256,512]{1,0:T(8,128)(2,1)S(1)}, u32[]{:S(2)}, u32[]{:S(2)}) collective-permute-start(bf16[256,512]{1,0:T(8,128)(2,1)S(1)} %get-tuple-element.20), channel_id=1, source_target_pairs={{0,8},{8,0},{1,9},{9,1},{2,10},{10,2},{3,11},{11,3},{4,12},{12,4},... | collective-permute-start | bytes 786440 | tf_op jit(solution)/shard_map/ppermute | solution.py:243
  66.6 1.2 %collective-permute-done.13.other_ref = bf16[256,512]{1,0:T(8,128)(2,1)S(1)} collective-permute-done((bf16[256,512]{1,0:T(8,128)(2,1)S(1)}, bf16[256,512]{1,0:T(8,128)(2,1)S(1)}, u32[]{:S(2)}, u32[]{:S(2)}) %collective-permute-start.13) | collective-permute-done | bytes 262176 | tf_op jit(solution)/shard_map/ppermute | solution.py:243
  67.8 1.5 %shard_map.116 = (bf16[528,128]{1,0:T(8,128)(2,1)S(1)}, bf16[256,512]{1,0:T(8,128)(2,1)S(1)}) custom-call(s32[16]{0:T(128)S(1)} %copy-done.4, s32[5]{0:T(128)S(1)} %stack.53.at_ref, f32[4,256]{1,0:T(4,128)S(1)} %copy-done.3, bf16[256,512]{1,0:T(8,128)(2,1)S(1)} %copy-done.2, f32[256,512]{1,0:T(8,128)S(1)} %get-tuple-element.19.own_ref, ...), custom_call_target="tpu_custom_call" | custom-call | flops 67108864 | bytes 1048576 | tf_op jit(solution)/shard_map/pallas_call | solution.py:320
  71.4 1.3 %collective-permute-start.15 = (bf16[528,128]{1,0:T(8,128)(2,1)S(1)}, bf16[528,128]{1,0:T(8,128)(2,1)S(1)}, u32[]{:S(2)}, u32[]{:S(2)}) collective-permute-start(bf16[528,128]{1,0:T(8,128)(2,1)S(1)} %shard_map.117), channel_id=1, source_target_pairs={{16,0},{32,16},{48,32},{64,48},{80,64},{96,80},{112,96},{128,112},... | collective-permute-start | bytes 405512 | tf_op jit(solution)/shard_map/ppermute | solution.py:263
  72.7 1.3 %collective-permute-start.16 = (bf16[528,128]{1,0:T(8,128)(2,1)S(1)}, bf16[528,128]{1,0:T(8,128)(2,1)S(1)}, u32[]{:S(2)}, u32[]{:S(2)}) collective-permute-start(bf16[528,128]{1,0:T(8,128)(2,1)S(1)} %shard_map.117), channel_id=1, source_target_pairs={{32,0},{48,16},{64,32},{80,48},{96,64},{112,80},{128,96},{144,112}... | collective-permute-start | bytes 405512 | tf_op jit(solution)/shard_map/ppermute | solution.py:263
  74.0 1.2 %collective-permute-done.18 = bf16[4,128,512]{2,1,0:T(8,128)(2,1)S(1)} collective-permute-done((bf16[4,128,512]{2,1,0:T(8,128)(2,1)S(1)}, bf16[4,128,512]{2,1,0:T(8,128)(2,1)S(1)}, u32[]{:S(2)}, u32[]{:S(2)}) %collective-permute-start.18) | collective-permute-done | bytes 524320 | tf_op jit(solution)/shard_map/ppermute | solution.py:256
  75.5 4.7 %collective-permute-start.23 = (bf16[128,512]{1,0:T(8,128)(2,1)S(1)}, bf16[128,512]{1,0:T(8,128)(2,1)S(1)}, u32[]{:S(2)}, u32[]{:S(2)}) collective-permute-start(bf16[128,512]{1,0:T(8,128)(2,1)S(1)} %get-tuple-element.31), channel_id=1, source_target_pairs={{0,48},{8,200},{16,0},{24,216},{32,16},{40,232},{48,32},{56,248},{... | collective-permute-start | bytes 393224 | tf_op jit(solution)/shard_map/ppermute | solution.py:256
  81.0 3.4 %collective-permute-start.17 = (bf16[528,128]{1,0:T(8,128)(2,1)S(1)}, bf16[528,128]{1,0:T(8,128)(2,1)S(1)}, u32[]{:S(2)}, u32[]{:S(2)}) collective-permute-start(bf16[528,128]{1,0:T(8,128)(2,1)S(1)} %shard_map.118.a_ref), channel_id=1, source_target_pairs={{0,8},{8,0},{1,9},{9,1},{2,10},{10,2},{3,11},{11,3},{4,12},{12,4},... | collective-permute-start | bytes 405512 | tf_op jit(solution)/shard_map/ppermute | solution.py:243
  84.3 10.2 %reduce-scatter.2.cloned.1.call-done = bf16[1,512,256]{2,1,0:T(8,128)(2,1)} async-done(((bf16[8,512,256]{2,1,0:T(8,128)(2,1)}), bf16[1,512,256]{2,1,0:T(8,128)(2,1)}) %reduce-scatter.2.cloned.1.call-update) | async-done | bytes 262160 | tf_op jit(solution)/shard_map/reduce_scatter | solution.py:314
  95.5 4.8 %collective-permute-start.11 = (bf16[256,256]{1,0:T(8,128)(2,1)S(1)}, bf16[256,256]{1,0:T(8,128)(2,1)S(1)}, u32[]{:S(2)}, u32[]{:S(2)}) collective-permute-start(bf16[256,256]{1,0:T(8,128)(2,1)S(1)} %slice_bitcast_fusion.8), channel_id=1, source_target_pairs={{0,8},{8,0},{1,9},{9,1},{2,10},{10,2},{3,11},{11,3},{4,12},{12,4},... | collective-permute-start | bytes 393224 | tf_op jit(solution)/shard_map/ppermute | solution.py:243
  101.2 3.3 %shard_map.119 = (bf16[256,512]{1,0:T(8,128)(2,1)}, bf16[256,512]{1,0:T(8,128)(2,1)}, bf16[256,512]{1,0:T(8,128)(2,1)}) custom-call(s32[16]{0:T(128)S(1)} %copy-done.4, s32[5]{0:T(128)S(1)} %stack.53.at_ref, f32[4,256]{1,0:T(4,128)S(1)} %copy-done.3, bf16[256,512]{1,0:T(8,128)(2,1)S(1)} %copy-done.2, bf16[256,512]{1,0:T(8,128)(2,1)S(1)} %copy-done.5, ...), custom_call_target="tpu_custom_call" | custom-call | flops 536870912 | bytes 1048576 | tf_op jit(solution)/shard_map/pallas_call | solution.py:326
  (65 shorter events, 13.8 us)
Async XLA Ops:
  7.2 19.8 %copy-start.4 = (s32[16]{0:T(128)S(1)}, s32[16]{0:T(128)}, u32[]{:S(2)}) copy-start(s32[16]{0:T(128)} %len_ref.7) | copy-start | bytes 196
  7.2 19.8 %copy-start.3 = (f32[4,256]{1,0:T(4,128)S(1)}, f32[4,256]{1,0:T(4,128)}, u32[]{:S(2)}) copy-start(f32[4,256]{1,0:T(4,128)} %ld_ref.7) | copy-start | bytes 12292
  7.2 19.8 %copy-start.2 = (bf16[256,512]{1,0:T(8,128)(2,1)S(1)}, bf16[256,512]{1,0:T(8,128)(2,1)}, u32[]{:S(2)}) copy-start(bf16[256,512]{1,0:T(8,128)(2,1)} %q_ref.7) | copy-start | bytes 786436
  7.2 19.8 %copy-start.5 = (bf16[256,512]{1,0:T(8,128)(2,1)S(1)}, bf16[256,512]{1,0:T(8,128)(2,1)}, u32[]{:S(2)}) copy-start(bf16[256,512]{1,0:T(8,128)(2,1)} %k_ref.3) | copy-start | bytes 786436
  7.2 19.8 %copy-start.6 = (bf16[256,512]{1,0:T(8,128)(2,1)S(1)}, bf16[256,512]{1,0:T(8,128)(2,1)}, u32[]{:S(2)}) copy-start(bf16[256,512]{1,0:T(8,128)(2,1)} %v_ref.3) | copy-start | bytes 786436
  7.2 46.5 %all-gather.3.cloned.1.call-start = ((), (), s32[]{:S(2)}) async-start(), calls=%async_computation.2 | async-start | bytes 2359296 | tf_op jit(solution)/shard_map/all_gather | solution.py:301
  8.4 4.3 %collective-permute-start.12 = (bf16[256,256]{1,0:T(8,128)(2,1)S(1)}, bf16[256,256]{1,0:T(8,128)(2,1)S(1)}, u32[]{:S(2)}, u32[]{:S(2)}) collective-permute-start(bf16[256,256]{1,0:T(8,128)(2,1)S(1)} %get-tuple-element.38), channel_id=1, source_target_pairs={{0,8},{8,0},{1,9},{9,1},{2,10},{10,2},{3,11},{11,3},{4,12},{12,4},... | collective-permute-start | bytes 393224 | tf_op jit(solution)/shard_map/ppermute | solution.py:243
  13.4 81.1 %reduce-scatter.2.cloned.1.call-start = ((), (), s32[]{:S(2)}) async-start(), calls=%async_computation.1 | async-start | bytes 2359296 | tf_op jit(solution)/shard_map/reduce_scatter | solution.py:314
  13.5 4.4 %collective-permute-start.7 = (bf16[128,512]{1,0:T(8,128)(2,1)}, bf16[128,512]{1,0:T(8,128)(2,1)S(1)}, u32[]{:S(2)}, u32[]{:S(2)}) collective-permute-start(bf16[128,512]{1,0:T(8,128)(2,1)} %param.12), channel_id=1, source_target_pairs={{0,48},{8,200},{16,0},{24,216},{32,16},{40,232},{48,32},{56,248},{... | collective-permute-start | bytes 393224 | tf_op jit(solution)/shard_map/ppermute | solution.py:256
  14.6 5.8 %collective-permute-start.6 = (bf16[128,512]{1,0:T(8,128)(2,1)}, bf16[128,512]{1,0:T(8,128)(2,1)S(1)}, u32[]{:S(2)}, u32[]{:S(2)}) collective-permute-start(bf16[128,512]{1,0:T(8,128)(2,1)} %param.12), channel_id=1, source_target_pairs={{0,32},{8,136},{16,48},{24,152},{32,0},{40,168},{48,16},{56,184},{... | collective-permute-start | bytes 393224 | tf_op jit(solution)/shard_map/ppermute | solution.py:256
  14.9 6.9 %collective-permute-start.5 = (bf16[128,512]{1,0:T(8,128)(2,1)}, bf16[128,512]{1,0:T(8,128)(2,1)S(1)}, u32[]{:S(2)}, u32[]{:S(2)}) collective-permute-start(bf16[128,512]{1,0:T(8,128)(2,1)} %param.12), channel_id=1, source_target_pairs={{0,16},{8,72},{16,32},{24,88},{32,48},{40,104},{48,0},{56,120},{64... | collective-permute-start | bytes 393224 | tf_op jit(solution)/shard_map/ppermute | solution.py:256
  23.6 25.2 %collective-permute-start.10 = (bf16[4,128,512]{2,1,0:T(8,128)(2,1)S(1)}, bf16[4,128,512]{2,1,0:T(8,128)(2,1)}, u32[]{:S(2)}, u32[]{:S(2)}) collective-permute-start(bf16[4,128,512]{2,1,0:T(8,128)(2,1)S(1)} %get-tuple-element.34), channel_id=1, source_target_pairs={{0,192},{8,56},{16,208},{24,8},{32,224},{40,24},{48,240},{56,40},{... | collective-permute-start | bytes 1572872 | tf_op jit(solution)/shard_map/ppermute | solution.py:256
  25.8 23.1 %collective-permute-start.9 = (bf16[4,128,512]{2,1,0:T(8,128)(2,1)S(1)}, bf16[4,128,512]{2,1,0:T(8,128)(2,1)}, u32[]{:S(2)}, u32[]{:S(2)}) collective-permute-start(bf16[4,128,512]{2,1,0:T(8,128)(2,1)S(1)} %get-tuple-element.34), channel_id=1, source_target_pairs={{0,128},{8,40},{16,144},{24,56},{32,160},{40,8},{48,176},{56,24},{... | collective-permute-start | bytes 1572872 | tf_op jit(solution)/shard_map/ppermute | solution.py:256
  26.3 22.5 %collective-permute-start.8 = (bf16[4,128,512]{2,1,0:T(8,128)(2,1)S(1)}, bf16[4,128,512]{2,1,0:T(8,128)(2,1)}, u32[]{:S(2)}, u32[]{:S(2)}) collective-permute-start(bf16[4,128,512]{2,1,0:T(8,128)(2,1)S(1)} %get-tuple-element.34), channel_id=1, source_target_pairs={{0,64},{8,24},{16,80},{24,40},{32,96},{40,56},{48,112},{56,8},{64,... | collective-permute-start | bytes 1572872 | tf_op jit(solution)/shard_map/ppermute | solution.py:256
  27.0 21.8 %copy-start.7 = (bf16[1,4,128,512]{3,2,1,0:T(8,128)(2,1)S(1)}, bf16[1,4,128,512]{3,2,1,0:T(8,128)(2,1)}, u32[]{:S(2)}) copy-start(bf16[1,4,128,512]{3,2,1,0:T(8,128)(2,1)} %get-tuple-element.33) | copy-start | bytes 1572868
  29.3 3.6 %collective-permute-start = (bf16[528,128]{1,0:T(8,128)(2,1)S(1)}, bf16[528,128]{1,0:T(8,128)(2,1)S(1)}, u32[]{:S(2)}, u32[]{:S(2)}) collective-permute-start(bf16[528,128]{1,0:T(8,128)(2,1)S(1)} %get-tuple-element.17.own_ref), channel_id=1, source_target_pairs={{0,8},{8,0},{1,9},{9,1},{2,10},{10,2},{3,11},{11,3},{4,12},{12,4},... | collective-permute-start | bytes 405512 | tf_op jit(solution)/shard_map/ppermute | solution.py:243
  33.6 5.7 %collective-permute-start.1 = (bf16[528,128]{1,0:T(8,128)(2,1)S(1)}, bf16[528,128]{1,0:T(8,128)(2,1)S(1)}, u32[]{:S(2)}, u32[]{:S(2)}) collective-permute-start(bf16[528,128]{1,0:T(8,128)(2,1)S(1)} %shard_map.111), channel_id=1, source_target_pairs={{0,16},{16,32},{32,48},{48,64},{64,80},{80,96},{96,112},{112,128},... | collective-permute-start | bytes 405512 | tf_op jit(solution)/shard_map/ppermute | solution.py:263
  35.8 10.1 %collective-permute-start.2 = (bf16[528,128]{1,0:T(8,128)(2,1)S(1)}, bf16[528,128]{1,0:T(8,128)(2,1)S(1)}, u32[]{:S(2)}, u32[]{:S(2)}) collective-permute-start(bf16[528,128]{1,0:T(8,128)(2,1)S(1)} %shard_map.111), channel_id=1, source_target_pairs={{0,32},{16,48},{32,64},{48,80},{64,96},{80,112},{96,128},{112,144}... | collective-permute-start | bytes 405512 | tf_op jit(solution)/shard_map/ppermute | solution.py:263
  46.0 1.4 %collective-permute-start.3 = (bf16[528,128]{1,0:T(8,128)(2,1)S(1)}, bf16[528,128]{1,0:T(8,128)(2,1)S(1)}, u32[]{:S(2)}, u32[]{:S(2)}) collective-permute-start(bf16[528,128]{1,0:T(8,128)(2,1)S(1)} %shard_map.112.a_ref), channel_id=1, source_target_pairs={{0,8},{8,0},{1,9},{9,1},{2,10},{10,2},{3,11},{11,3},{4,12},{12,4},... | collective-permute-start | bytes 405512 | tf_op jit(solution)/shard_map/ppermute | solution.py:243
  48.6 1.9 %collective-permute-start.4 = (bf16[256,512]{1,0:T(8,128)(2,1)S(1)}, bf16[256,512]{1,0:T(8,128)(2,1)S(1)}, u32[]{:S(2)}, u32[]{:S(2)}) collective-permute-start(bf16[256,512]{1,0:T(8,128)(2,1)S(1)} %get-tuple-element.18.own_ref), channel_id=1, source_target_pairs={{0,8},{8,0},{1,9},{9,1},{2,10},{10,2},{3,11},{11,3},{4,12},{12,4},... | collective-permute-start | bytes 786440 | tf_op jit(solution)/shard_map/ppermute | solution.py:243
  57.2 16.7 %collective-permute-start.20 = (bf16[4,128,512]{2,1,0:T(8,128)(2,1)S(1)}, bf16[4,128,512]{2,1,0:T(8,128)(2,1)S(1)}, u32[]{:S(2)}, u32[]{:S(2)}) collective-permute-start(bf16[4,128,512]{2,1,0:T(8,128)(2,1)S(1)} %get-tuple-element.28), channel_id=1, source_target_pairs={{0,192},{8,56},{16,208},{24,8},{32,224},{40,24},{48,240},{56,40},{... | collective-permute-start | bytes 1572872 | tf_op jit(solution)/shard_map/ppermute | solution.py:256
  60.0 14.0 %collective-permute-start.19 = (bf16[4,128,512]{2,1,0:T(8,128)(2,1)S(1)}, bf16[4,128,512]{2,1,0:T(8,128)(2,1)S(1)}, u32[]{:S(2)}, u32[]{:S(2)}) collective-permute-start(bf16[4,128,512]{2,1,0:T(8,128)(2,1)S(1)} %get-tuple-element.29), channel_id=1, source_target_pairs={{0,128},{8,40},{16,144},{24,56},{32,160},{40,8},{48,176},{56,24},{... | collective-permute-start | bytes 1572872 | tf_op jit(solution)/shard_map/ppermute | solution.py:256
  60.0 15.2 %collective-permute-start.18 = (bf16[4,128,512]{2,1,0:T(8,128)(2,1)S(1)}, bf16[4,128,512]{2,1,0:T(8,128)(2,1)S(1)}, u32[]{:S(2)}, u32[]{:S(2)}) collective-permute-start(bf16[4,128,512]{2,1,0:T(8,128)(2,1)S(1)} %get-tuple-element.27), channel_id=1, source_target_pairs={{0,64},{8,24},{16,80},{24,40},{32,96},{40,56},{48,112},{56,8},{64,... | collective-permute-start | bytes 1572872 | tf_op jit(solution)/shard_map/ppermute | solution.py:256
  62.5 5.3 %collective-permute-start.13 = (bf16[256,512]{1,0:T(8,128)(2,1)S(1)}, bf16[256,512]{1,0:T(8,128)(2,1)S(1)}, u32[]{:S(2)}, u32[]{:S(2)}) collective-permute-start(bf16[256,512]{1,0:T(8,128)(2,1)S(1)} %get-tuple-element.20), channel_id=1, source_target_pairs={{0,8},{8,0},{1,9},{9,1},{2,10},{10,2},{3,11},{11,3},{4,12},{12,4},... | collective-permute-start | bytes 786440 | tf_op jit(solution)/shard_map/ppermute | solution.py:243
  69.3 1.5 %collective-permute-start.14 = (bf16[528,128]{1,0:T(8,128)(2,1)S(1)}, bf16[528,128]{1,0:T(8,128)(2,1)S(1)}, u32[]{:S(2)}, u32[]{:S(2)}) collective-permute-start(bf16[528,128]{1,0:T(8,128)(2,1)S(1)} %get-tuple-element.23.own_ref), channel_id=1, source_target_pairs={{0,8},{8,0},{1,9},{9,1},{2,10},{10,2},{3,11},{11,3},{4,12},{12,4},... | collective-permute-start | bytes 405512 | tf_op jit(solution)/shard_map/ppermute | solution.py:243
  71.4 9.5 %collective-permute-start.15 = (bf16[528,128]{1,0:T(8,128)(2,1)S(1)}, bf16[528,128]{1,0:T(8,128)(2,1)S(1)}, u32[]{:S(2)}, u32[]{:S(2)}) collective-permute-start(bf16[528,128]{1,0:T(8,128)(2,1)S(1)} %shard_map.117), channel_id=1, source_target_pairs={{16,0},{32,16},{48,32},{64,48},{80,64},{96,80},{112,96},{128,112},... | collective-permute-start | bytes 405512 | tf_op jit(solution)/shard_map/ppermute | solution.py:263
  72.7 8.2 %collective-permute-start.16 = (bf16[528,128]{1,0:T(8,128)(2,1)S(1)}, bf16[528,128]{1,0:T(8,128)(2,1)S(1)}, u32[]{:S(2)}, u32[]{:S(2)}) collective-permute-start(bf16[528,128]{1,0:T(8,128)(2,1)S(1)} %shard_map.117), channel_id=1, source_target_pairs={{32,0},{48,16},{64,32},{80,48},{96,64},{112,80},{128,96},{144,112}... | collective-permute-start | bytes 405512 | tf_op jit(solution)/shard_map/ppermute | solution.py:263
  75.5 24.9 %collective-permute-start.23 = (bf16[128,512]{1,0:T(8,128)(2,1)S(1)}, bf16[128,512]{1,0:T(8,128)(2,1)S(1)}, u32[]{:S(2)}, u32[]{:S(2)}) collective-permute-start(bf16[128,512]{1,0:T(8,128)(2,1)S(1)} %get-tuple-element.31), channel_id=1, source_target_pairs={{0,48},{8,200},{16,0},{24,216},{32,16},{40,232},{48,32},{56,248},{... | collective-permute-start | bytes 393224 | tf_op jit(solution)/shard_map/ppermute | solution.py:256
  80.2 20.2 %collective-permute-start.22 = (bf16[128,512]{1,0:T(8,128)(2,1)S(1)}, bf16[128,512]{1,0:T(8,128)(2,1)S(1)}, u32[]{:S(2)}, u32[]{:S(2)}) collective-permute-start(bf16[128,512]{1,0:T(8,128)(2,1)S(1)} %get-tuple-element.32), channel_id=1, source_target_pairs={{0,32},{8,136},{16,48},{24,152},{32,0},{40,168},{48,16},{56,184},{... | collective-permute-start | bytes 393224 | tf_op jit(solution)/shard_map/ppermute | solution.py:256
  80.2 20.2 %collective-permute-start.21 = (bf16[128,512]{1,0:T(8,128)(2,1)S(1)}, bf16[128,512]{1,0:T(8,128)(2,1)S(1)}, u32[]{:S(2)}, u32[]{:S(2)}) collective-permute-start(bf16[128,512]{1,0:T(8,128)(2,1)S(1)} %get-tuple-element.30), channel_id=1, source_target_pairs={{0,16},{8,72},{16,32},{24,88},{32,48},{40,104},{48,0},{56,120},{64... | collective-permute-start | bytes 393224 | tf_op jit(solution)/shard_map/ppermute | solution.py:256
  81.0 20.2 %collective-permute-start.17 = (bf16[528,128]{1,0:T(8,128)(2,1)S(1)}, bf16[528,128]{1,0:T(8,128)(2,1)S(1)}, u32[]{:S(2)}, u32[]{:S(2)}) collective-permute-start(bf16[528,128]{1,0:T(8,128)(2,1)S(1)} %shard_map.118.a_ref), channel_id=1, source_target_pairs={{0,8},{8,0},{1,9},{9,1},{2,10},{10,2},{3,11},{11,3},{4,12},{12,4},... | collective-permute-start | bytes 405512 | tf_op jit(solution)/shard_map/ppermute | solution.py:243
  95.5 8.9 %collective-permute-start.11 = (bf16[256,256]{1,0:T(8,128)(2,1)S(1)}, bf16[256,256]{1,0:T(8,128)(2,1)S(1)}, u32[]{:S(2)}, u32[]{:S(2)}) collective-permute-start(bf16[256,256]{1,0:T(8,128)(2,1)S(1)} %slice_bitcast_fusion.8), channel_id=1, source_target_pairs={{0,8},{8,0},{1,9},{9,1},{2,10},{10,2},{3,11},{11,3},{4,12},{12,4},... | collective-permute-start | bytes 393224 | tf_op jit(solution)/shard_map/ppermute | solution.py:243
  (3 other events, 12.8 us)
Sparse Core Ops, SparseCore 0:
  13.5 38.3 all-gather.2
  54.5 40.0 reduce-scatter.1

commit v3 on v2

--- a/solution.py
+++ b/solution.py
@@ -23,15 +23,17 @@
 SMEM = pl.BlockSpec(memory_space=pltpu.SMEM)
 
 
-def call(kernel, outs, specs, flops):
-    return pl.pallas_call(
-        kernel,
+def call(kernel, outs, specs, us, after=()):
+    gates = len(after)
+    made = pl.pallas_call(
+        lambda *refs: kernel(*refs[gates:]),
         out_shape=[jax.ShapeDtypeStruct(s, d) for s, d in outs],
-        in_specs=specs,
+        in_specs=[pl.BlockSpec(memory_space=pl.ANY)] * gates + specs,
         out_specs=[VMEM] * len(outs),
         compiler_params=pltpu.CompilerParams(vmem_limit_bytes=48 * 2**20),
-        cost_estimate=pl.CostEstimate(flops=flops, bytes_accessed=2**20, transcendentals=0),
-    )
+        cost_estimate=pl.CostEstimate(flops=int(us * 3 * 10**9), bytes_accessed=2**20, transcendentals=0),
+    )
+    return lambda *args: made(*after, *args)
 
 
 def dot(a, b, dims, precision=None):
@@ -213,29 +215,32 @@
     return jnp.concatenate([w_ref[place(at_ref, ry, r)] for r in rx], axis=0)
 
 
-def pull_kernel(at_ref, g_ref, w_ref, own_ref, send_ref):
+def pull_kernel(at_ref, w_ref, *refs):
+    g_refs, (own_ref, send_ref) = refs[:LONG], refs[LONG:]
     total = jnp.zeros((2 * ROWS, STATE), F32)
-    for j in range(LONG):
-        total = total + dot(g_ref[j], weight_part(w_ref, j, at_ref), NN)
+    for s, g_ref in enumerate(g_refs):
+        j = lax.rem(at_ref[3] - s + LONG, LONG)
+        total = total + dot(g_ref[...], weight_part(w_ref, j, at_ref), NN)
     own_ref[...] = total[:ROWS]
     send_ref[...] = total[ROWS:].astype(BF16)
 
 
-def mix_kernel(at_ref, own_ref, other_ref, w_ref, out_ref):
-    for j in range(LONG):
-        w = weight_part(w_ref, j, at_ref)
-        out_ref[j, :ROWS] = dot(own_ref[...], w, NT).astype(BF16)
-        out_ref[j, ROWS:] = dot(other_ref[...], w, NT).astype(BF16)
-
-
-def weight_grad_kernel(at_ref, g_ref, own_ref, other_ref, r_ref):
-    for j in range(LONG):
+def mix_kernel(at_ref, own_ref, other_ref, w_ref, *out_refs):
+    for s, out_ref in enumerate(out_refs):
+        w = weight_part(w_ref, lax.rem(at_ref[3] + s, LONG), at_ref)
+        out_ref[:ROWS] = dot(own_ref[...], w, NT).astype(BF16)
+        out_ref[ROWS:] = dot(other_ref[...], w, NT).astype(BF16)
+
+
+def weight_grad_kernel(at_ref, own_ref, other_ref, *refs):
+    g_refs, r_ref = refs[:LONG], refs[LONG]
+    for s, g_ref in enumerate(g_refs):
+        j = lax.rem(at_ref[3] - s + LONG, LONG)
         dy, dx = chip_of(j, at_ref[1], at_ref[2], 1)
-        part = dot(g_ref[j, :ROWS], own_ref[...], TN) + dot(g_ref[j, ROWS:], other_ref[...], TN)
+        part = dot(g_ref[:ROWS], own_ref[...], TN) + dot(g_ref[ROWS:], other_ref[...], TN)
         part = part.astype(BF16)
         for e in range(2):
-            rows = slice(e * HD, (e + 1) * HD)
-            r_ref[place(at_ref, dy, dx[e])] = part[rows]
+            r_ref[place(at_ref, dy, dx[e])] = part[e * HD : (e + 1) * HD]
 
 
 def ring(value, axis, steps):
@@ -263,8 +268,14 @@
     return lax.ppermute(value, SEQ, pairs)
 
 
-def gather_side(value, axes):
-    return jnp.stack([value] + [cross(value, axes, s) for s in (1, 2, 3)])
+def stack_kernel(*refs):
+    for n, ref in enumerate(refs[:-1]):
+        refs[-1][n] = ref[...]
+
+
+def gather_side(value, axes, after=()):
+    parts = [value] + [cross(value, axes, s) for s in (1, 2, 3)]
+    return call(stack_kernel, [((SIDE,) + value.shape, BF16)], [VMEM] * SIDE, 0.7, after)(*parts)[0]
 
 
 def scatter_side(value, axes):
@@ -272,15 +283,48 @@
     return functools.reduce(jnp.add, [p.astype(F32) for p in parts])
 
 
-def relay(at, pay, way, outer):
+def relay(at, pay, way, outer, chip_after, pair_after):
     sibling = swap(pay)
-    [chip] = call(functools.partial(chip_kernel, outer), [((PAY, HD), BF16)], [SMEM] + [VMEM] * 2, 2**20)(
+    [chip] = call(functools.partial(chip_kernel, outer), [((PAY, HD), BF16)], [SMEM] + [VMEM] * 2, 0.7, chip_after)(
         at, pay, sibling
     )
-    [share] = call(pair_kernel, [((PAY, HD), BF16)], [VMEM] * 2, 2**20)(
+    [share] = call(pair_kernel, [((PAY, HD), BF16)], [VMEM] * 2, 0.7, pair_after)(
         line(chip, way, 3 * way), line(chip, 2 * way, 4 * way)
     )
     return share, swap(share), sibling
+
+
+def long_cross(value, steps):
+    pairs = [(c * LONG + z, c * LONG + (z + (1 - 2 * c) * steps) % LONG) for c in range(2) for z in range(LONG)]
+    return lax.ppermute(value, ("core", "z"), pairs)
+
+
+def gather_long(value, even):
+    parts = [None] * LONG
+    parts[0] = right = left = value
+    for s in range(1, LONG // 2):
+        parts[s] = right = ring(right, "z", 1)
+        parts[LONG - s] = left = ring(left, "z", -1)
+    parts[LONG // 2] = long_cross(jnp.where(even, right, left), 1)
+    return parts
+
+
+def add(a, b):
+    return (a.astype(F32) + b.astype(F32)).astype(BF16)
+
+
+def scatter_long(value, even):
+    half = LONG // 2
+    far = long_cross(value[half], 1)
+    right = jnp.where(even, add(value[half - 1], far), value[half - 1])
+    left = jnp.where(even, value[half + 1], add(value[half + 1], far))
+    stages = [(right, left)]
+    for s in range(1, half - 1):
+        right = add(value[half - 1 - s], ring(right, "z", 1))
+        left = add(value[half + 1 + s], ring(left, "z", -1))
+        stages.append((right, left))
+    right, left = ring(right, "z", 1), ring(left, "z", -1)
+    return (value[0].astype(F32) + right.astype(F32) + left.astype(F32)).astype(BF16), stages
 
 
 def swap(value):
@@ -298,33 +342,38 @@
     lead_specs = [SMEM, SMEM, VMEM]
     even, odd = parity(out_grad)
     mine, yours = jnp.where(c == 0, even, odd), jnp.where(c == 0, odd, even)
-    grads = lax.all_gather(jnp.concatenate([mine, swap(yours)], axis=0), "z")
-    w = gather_side(gather_side(weight, "xy"), "yx")
+    grads = gather_long(jnp.concatenate([mine, swap(yours)], axis=0), c == 0)
+    near = gather_side(weight, "xy", (grads[1], grads[7]))
+    w = gather_side(near, "yx")
+    first_after = (near,)
     wide = ((ROWS, STATE), BF16)
     pay, local = call(
-        first_kernel, [((PAY, HD), BF16), ((ROWS, STATE), F32)], lead_specs + [VMEM] * 3, 2**28
+        first_kernel, [((PAY, HD), BF16), ((ROWS, STATE), F32)], lead_specs + [VMEM] * 3, 2.3, first_after
     )(*lead, q, k, v)
-    att, state = call(attend_kernel, [wide, ((STATE, HD), BF16)], lead_specs + [VMEM] * 5, 2**26)(
-        *lead, q, local, *relay(at, pay, 1, 1)
+    att, state = call(attend_kernel, [wide, ((STATE, HD), BF16)], lead_specs + [VMEM] * 5, 1.9)(
+        *lead, q, local, *relay(at, pay, 1, 1, (grads[2], grads[6]), (grads[3], grads[5]))
     )
     att_other = swap(att)
-    [mixed] = call(mix_kernel, [((LONG, 2 * ROWS, HALF), BF16)], [SMEM] + [VMEM] * 3, 2**30)(
+    mixed = call(mix_kernel, [((2 * ROWS, HALF), BF16)] * LONG, [SMEM] + [VMEM] * 3, 1.9, (grads[4],))(
         at, att, att_other, w
     )
-    mixed = lax.psum_scatter(mixed, "z", scatter_dimension=0)
+    mixed, stages = scatter_long(mixed, c == 0)
     mixed_other = swap(mixed[ROWS:])
     mixed = mixed[:ROWS]
     even, odd = jnp.where(c == 0, mixed, mixed_other), jnp.where(c == 0, mixed_other, mixed)
     mixed = jnp.concatenate([even[:, :HD], odd[:, :HD], even[:, HD:], odd[:, HD:]], axis=1)
-    own, send = call(pull_kernel, [((ROWS, STATE), F32), wide], [SMEM] + [VMEM] * 2, 2**30)(at, grads, w)
-    back, g = call(back_kernel, [((PAY, HD), BF16), wide], lead_specs + [VMEM] * 3, 2**26)(
+    own, send = call(pull_kernel, [((ROWS, STATE), F32), wide], [SMEM] + [VMEM] * (1 + LONG), 1.9)(at, w, *grads)
+    back, g = call(back_kernel, [((PAY, HD), BF16), wide], lead_specs + [VMEM] * 3, 1.6)(
         *lead, q, own, swap(send)
     )
     grid = ((SIDE, SIDE, HD, STATE), BF16)
-    [r] = call(weight_grad_kernel, [grid], [SMEM] + [VMEM] * 3, 2**30)(at, grads, att, att_other)
-    r = scatter_side(scatter_side(r, "yx").astype(BF16), "xy")
-    dq, dk, dv = call(grads_kernel, [wide] * 3, lead_specs + [VMEM] * 8, 2**29)(
-        *lead, q, k, v, g, state, *relay(at, back, -1, 0)
+    [r] = call(weight_grad_kernel, [grid], [SMEM] + [VMEM] * (2 + LONG), 1.9)(
+        at, att, att_other, *grads
+    )
+    r_near = scatter_side(r, "yx").astype(BF16)
+    r = scatter_side(r_near, "xy")
+    dq, dk, dv = call(grads_kernel, [wide] * 3, lead_specs + [VMEM] * 8, 3.3, (r_near, *stages[2]))(
+        *lead, q, k, v, g, state, *relay(at, back, -1, 0, stages[0], stages[1])
     )
     return mixed, dq, dk, dv, r
 

time: 112 us -> 107 us (0.955)
  starting transfers between devices: 41.7 us -> 68.4 us
  between operations: 14.3 us -> 1.03 us
  waiting for transfers between devices: 29.7 us -> 17.3 us
  other arithmetic: 6 us -> 2.44 us
  local copies, waits for them, and re-layouts: 5.21 us -> 2.15 us
    ppermute x8 -> x20, starting transfers between devices: 19.1 us -> 30.4 us  [ring(): lax.ppermute(value, axis, [(i, (i + steps) % count) for i in range(count)])]
    reduce_scatter x1 -> x0, waiting for transfers between devices: 10.2 us -> none  [body(): mixed = lax.psum_scatter(mixed, 'z', scatter_dimension=0)]
    ppermute x12, starting transfers between devices: 14.2 us -> 21.3 us  [cross(): return lax.ppermute(value, SEQ, pairs)]
    ppermute x0 -> x2, starting transfers between devices: none -> 6.69 us  [long_cross(): return lax.ppermute(value, ('core', 'z'), pairs)]
    ppermute x4, waiting for transfers between devices: 6.58 us -> 2 us  [line(): return lax.ppermute(value, SEQ, pairs)]
    ppermute x8 -> x20, waiting for transfers between devices: 5.48 us -> 9.21 us  [ring(): lax.ppermute(value, axis, [(i, (i + steps) % count) for i in range(count)])]
    another operation x2 -> x0, other arithmetic: 3.42 us -> none  [gather_side(): return jnp.stack([value] + [cross(value, axes, s) for s in (1, 2, 3)])]
    unnamed x18 -> x12, local copies, waits for them, and re-layouts: 2.94 us -> 0.92 us
  transfers between devices with their start and end apart: 26 -> 38, of which waited for: 11 -> 7; matrix products, arithmetic and copies ran while one was open for 5% -> 2% of each run, Pallas kernels for 14% -> 14%
where the time goes in v3:
time: 107 us
  starting transfers between devices  68.4 us (64%)
  waiting for transfers between devices  17.3 us (16%)
  Pallas kernels  15.4 us (14%)
  other arithmetic  2.44 us (2%)
  local copies, waits for them, and re-layouts  2.15 us (2%)
    ppermute x20, starting transfers between devices, ring(): lax.ppermute(value, axis, [(i, (i + steps) % count) for i in range(count)])  30.4 us
    ppermute x12, starting transfers between devices, cross(): return lax.ppermute(value, SEQ, pairs)  21.3 us
    pallas_call x13, Pallas kernels, call(): return lambda *args: made(*after, *args)  15.4 us
    ppermute x4, starting transfers between devices, line(): return lax.ppermute(value, SEQ, pairs)  10 us
    ppermute x20, waiting for transfers between devices, ring(): lax.ppermute(value, axis, [(i, (i + steps) % count) for i in range(count)])  9.21 us
    ppermute x2, starting transfers between devices, long_cross(): return lax.ppermute(value, ('core', 'z'), pairs)  6.69 us
    ppermute x12, waiting for transfers between devices, cross(): return lax.ppermute(value, SEQ, pairs)  6.07 us
  transfers between devices with their start and end apart: 38, of which 7 were waited for; matrix products, arithmetic and copies ran while one was open for 2% of the time, Pallas kernels for 14%

profile of v3, /device:TPU:1, one launch (start us, length us, event | category | flops | bytes accessed | tf_op | source)
XLA Modules:
  0.0 106.7 jit_solution(4705232560152119632)
XLA Ops:
  1.7 3.3 %collective-permute-start = (bf16[256,256]{1,0:T(8,128)(2,1)S(1)}, bf16[256,256]{1,0:T(8,128)(2,1)S(1)}, u32[]{:S(2)}, u32[]{:S(2)}) collective-permute-start(bf16[256,256]{1,0:T(8,128)(2,1)S(1)} %get-tuple-element.54), channel_id=1, source_target_pairs={{0,8},{8,0},{1,9},{9,1},{2,10},{10,2},{3,11},{11,3},{4,12},{12,4},... | collective-permute-start | bytes 393224 | tf_op jit(solution)/shard_map/ppermute | solution.py:248
  6.0 3.9 %collective-permute-start.4 = (bf16[512,256]{1,0:T(8,128)(2,1)S(1)}, bf16[512,256]{1,0:T(8,128)(2,1)S(1)}, u32[]{:S(2)}, u32[]{:S(2)}) collective-permute-start(bf16[512,256]{1,0:T(8,128)(2,1)S(1)} %pad_maximum_fusion.refs_3_.refs_2_), channel_id=1, source_target_pairs={{0,7},{1,0},{2,1},{3,2},{4,3},{5,4},{6,5},{7,6},{8,15},{9,8},{10,9... | collective-permute-start | bytes 786440 | tf_op jit(solution)/shard_map/ppermute | solution.py:248
  9.9 2.9 %collective-permute-start.9 = (bf16[128,512]{1,0:T(8,128)(2,1)}, bf16[128,512]{1,0:T(8,128)(2,1)S(1)}, u32[]{:S(2)}, u32[]{:S(2)}) collective-permute-start(bf16[128,512]{1,0:T(8,128)(2,1)} %refs_2_.3), channel_id=1, source_target_pairs={{0,32},{8,136},{16,48},{24,152},{32,0},{40,168},{48,16},{56,184},{... | collective-permute-start | bytes 393224 | tf_op jit(solution)/shard_map/ppermute | solution.py:261
  13.2 2.3 %collective-permute-start.10 = (bf16[128,512]{1,0:T(8,128)(2,1)}, bf16[128,512]{1,0:T(8,128)(2,1)S(1)}, u32[]{:S(2)}, u32[]{:S(2)}) collective-permute-start(bf16[128,512]{1,0:T(8,128)(2,1)} %refs_2_.3), channel_id=1, source_target_pairs={{0,48},{8,200},{16,0},{24,216},{32,16},{40,232},{48,32},{56,248},{... | collective-permute-start | bytes 393224 | tf_op jit(solution)/shard_map/ppermute | solution.py:261
  15.6 3.0 %collective-permute-start.5 = (bf16[512,256]{1,0:T(8,128)(2,1)S(1)}, bf16[512,256]{1,0:T(8,128)(2,1)S(1)}, u32[]{:S(2)}, u32[]{:S(2)}) collective-permute-start(bf16[512,256]{1,0:T(8,128)(2,1)S(1)} %collective-permute-done.4.refs_1_.refs_10_.refs_9_), channel_id=1, source_target_pairs={{0,7},{1,0},{2,1},{3,2},{4,3},{5,4},{6,5},{7,6},{8,15},{9,8},{10,9... | collective-permute-start | bytes 786440 | tf_op jit(solution)/shard_map/ppermute | solution.py:248
  19.7 2.3 %shard_map.111 = (bf16[528,128]{1,0:T(8,128)(2,1)S(1)}, f32[256,512]{1,0:T(8,128)S(1)}) custom-call(bf16[4,128,512]{2,1,0:T(8,128)(2,1)S(1)} %shard_map.110.refs_0_, s32[16]{0:T(128)S(1)} %copy-done.5, s32[5]{0:T(128)S(1)} %stack.23.refs_2_.refs_1_.refs_0_.refs_4_, f32[4,256]{1,0:T(4,128)S(1)} %copy-done.4, bf16[256,512]{1,0:T(8,128)(2,1)S(1)} %copy-done, ...), custom_call_target="tpu_custom_call" | custom-call | flops 6899999744 | bytes 1048576 | tf_op jit(solution)/shard_map/pallas_call | solution.py:36
  22.0 1.7 %collective-permute-start.11 = (bf16[528,128]{1,0:T(8,128)(2,1)S(1)}, bf16[528,128]{1,0:T(8,128)(2,1)S(1)}, u32[]{:S(2)}, u32[]{:S(2)}) collective-permute-start(bf16[528,128]{1,0:T(8,128)(2,1)S(1)} %get-tuple-element.25.refs_3_), channel_id=1, source_target_pairs={{0,8},{8,0},{1,9},{9,1},{2,10},{10,2},{3,11},{11,3},{4,12},{12,4},... | collective-permute-start | bytes 405512 | tf_op jit(solution)/shard_map/ppermute | solution.py:248
  23.7 2.9 %collective-permute-start.6 = (bf16[512,256]{1,0:T(8,128)(2,1)S(1)}, bf16[512,256]{1,0:T(8,128)(2,1)S(1)}, u32[]{:S(2)}, u32[]{:S(2)}) collective-permute-start(bf16[512,256]{1,0:T(8,128)(2,1)S(1)} %collective-permute-done.5.refs_1_.refs_9_.refs_8_), channel_id=1, source_target_pairs={{0,7},{1,0},{2,1},{3,2},{4,3},{5,4},{6,5},{7,6},{8,15},{9,8},{10,9... | collective-permute-start | bytes 786440 | tf_op jit(solution)/shard_map/ppermute | solution.py:248
  26.6 2.7 %collective-permute-start.18 = (bf16[4,128,512]{2,1,0:T(8,128)(2,1)S(1)}, bf16[4,128,512]{2,1,0:T(8,128)(2,1)S(1)}, u32[]{:S(2)}, u32[]{:S(2)}) collective-permute-start(bf16[4,128,512]{2,1,0:T(8,128)(2,1)S(1)} %shard_map.110.refs_0_), channel_id=1, source_target_pairs={{0,192},{8,56},{16,208},{24,8},{32,224},{40,24},{48,240},{56,40},{... | collective-permute-start | bytes 1572872 | tf_op jit(solution)/shard_map/ppermute | solution.py:261
  30.8 3.2 %collective-permute-start.13 = (bf16[528,128]{1,0:T(8,128)(2,1)S(1)}, bf16[528,128]{1,0:T(8,128)(2,1)S(1)}, u32[]{:S(2)}, u32[]{:S(2)}) collective-permute-start(bf16[528,128]{1,0:T(8,128)(2,1)S(1)} %shard_map.112), channel_id=1, source_target_pairs={{0,32},{16,48},{32,64},{48,80},{64,96},{80,112},{96,128},{112,144}... | collective-permute-start | bytes 405512 | tf_op jit(solution)/shard_map/ppermute | solution.py:268
  34.0 4.2 %collective-permute-start.12 = (bf16[528,128]{1,0:T(8,128)(2,1)S(1)}, bf16[528,128]{1,0:T(8,128)(2,1)S(1)}, u32[]{:S(2)}, u32[]{:S(2)}) collective-permute-start(bf16[528,128]{1,0:T(8,128)(2,1)S(1)} %shard_map.112), channel_id=1, source_target_pairs={{0,16},{16,32},{32,48},{48,64},{64,80},{80,96},{96,112},{112,128},... | collective-permute-start | bytes 405512 | tf_op jit(solution)/shard_map/ppermute | solution.py:268
  38.3 3.7 %collective-permute-start.7 = (bf16[512,256]{1,0:T(8,128)(2,1)S(1)}, bf16[512,256]{1,0:T(8,128)(2,1)S(1)}, u32[]{:S(2)}, u32[]{:S(2)}) collective-permute-start(bf16[512,256]{1,0:T(8,128)(2,1)S(1)} %broadcast_select_fusion), channel_id=1, source_target_pairs={{0,1},{1,2},{2,3},{3,4},{4,5},{5,6},{6,7},{7,0},{8,15},{9,8},{10,9... | collective-permute-start | bytes 786440 | tf_op jit(solution)/shard_map/ppermute | solution.py:299
  41.9 2.0 %collective-permute-done.12.refs_2_ = bf16[528,128]{1,0:T(8,128)(2,1)S(1)} collective-permute-done((bf16[528,128]{1,0:T(8,128)(2,1)S(1)}, bf16[528,128]{1,0:T(8,128)(2,1)S(1)}, u32[]{:S(2)}, u32[]{:S(2)}) %collective-permute-start.12) | collective-permute-done | bytes 135200 | tf_op jit(solution)/shard_map/ppermute | solution.py:268
  44.8 1.3 %collective-permute-done.16.refs_1_ = bf16[4,128,512]{2,1,0:T(8,128)(2,1)S(1)} collective-permute-done((bf16[4,128,512]{2,1,0:T(8,128)(2,1)S(1)}, bf16[4,128,512]{2,1,0:T(8,128)(2,1)S(1)}, u32[]{:S(2)}, u32[]{:S(2)}) %collective-permute-start.16) | collective-permute-done | bytes 524320 | tf_op jit(solution)/shard_map/ppermute | solution.py:261
  47.4 4.7 %collective-permute-start.15 = (bf16[256,512]{1,0:T(8,128)(2,1)S(1)}, bf16[256,512]{1,0:T(8,128)(2,1)S(1)}, u32[]{:S(2)}, u32[]{:S(2)}) collective-permute-start(bf16[256,512]{1,0:T(8,128)(2,1)S(1)} %get-tuple-element.26.refs_2_.refs_1_), channel_id=1, source_target_pairs={{0,8},{8,0},{1,9},{9,1},{2,10},{10,2},{3,11},{11,3},{4,12},{12,4},... | collective-permute-start | bytes 786440 | tf_op jit(solution)/shard_map/ppermute | solution.py:248
  52.1 1.8 %shard_map.118 = (f32[256,512]{1,0:T(8,128)S(1)}, bf16[256,512]{1,0:T(8,128)(2,1)S(1)}) custom-call(s32[5]{0:T(128)S(1)} %stack.23.refs_2_.refs_1_.refs_0_.refs_4_, bf16[4,4,128,512]{3,2,1,0:T(8,128)(2,1)S(1)} %shard_map.115.refs_4_.refs_1_, bf16[512,256]{1,0:T(8,128)(2,1)S(1)} %pad_maximum_fusion.refs_3_.refs_2_, ...), custom_call_target="tpu_custom_call" | custom-call | flops 5699999744 | bytes 1048576 | tf_op jit(solution)/shard_map/pallas_call | solution.py:36
  54.0 1.9 %shard_map.116 = (bf16[512,256]{1,0:T(8,128)(2,1)S(1)}, bf16[512,256]{1,0:T(8,128)(2,1)S(1)}, bf16[512,256]{1,0:T(8,128)(2,1)S(1)}, bf16[512,256]{1,0:T(8,128)(2...) custom-call(bf16[512,256]{1,0:T(8,128)(2,1)S(1)} %collective-permute, ...), custom_call_target="tpu_custom_call" | custom-call | flops 5699999744 | bytes 1048576 | tf_op jit(solution)/shard_map/pallas_call | solution.py:36
  55.9 3.0 %collective-permute-start.19 = (bf16[512,256]{1,0:T(8,128)(2,1)S(1)}, bf16[512,256]{1,0:T(8,128)(2,1)S(1)}, u32[]{:S(2)}, u32[]{:S(2)}) collective-permute-start(bf16[512,256]{1,0:T(8,128)(2,1)S(1)} %get-tuple-element.31), channel_id=1, source_target_pairs={{0,1},{1,2},{2,3},{3,4},{4,5},{5,6},{6,7},{7,0},{8,15},{9,8},{10,9... | collective-permute-start | bytes 786440 | tf_op jit(solution)/shard_map/ppermute | solution.py:299
  59.0 1.8 %shard_map.117 = bf16[4,4,128,512]{3,2,1,0:T(8,128)(2,1)S(1)} custom-call(s32[5]{0:T(128)S(1)} %stack.23.refs_2_.refs_1_.refs_0_.refs_4_, bf16[256,512]{1,0:T(8,128)(2,1)S(1)} %get-tuple-element.26.refs_2_.refs_1_, bf16[256,512]{1,0:T(8,128)(2,1)S(1)} %collective-permute-done.15.refs_3_.refs_2_, bf16[512,256]{1,0:T(8,128)(2,1)S(1)} %pad_maximum_fusion.refs_3_.refs_2_, ...), custom_call_target="tpu_custom_call" | custom-call | flops 5699999744 | bytes 1048576 | tf_op jit(solution)/shard_map/pallas_call | solution.py:36
  60.8 1.6 %shard_map.119 = (bf16[528,128]{1,0:T(8,128)(2,1)S(1)}, bf16[256,512]{1,0:T(8,128)(2,1)S(1)}) custom-call(s32[16]{0:T(128)S(1)} %copy-done.5, s32[5]{0:T(128)S(1)} %stack.23.refs_2_.refs_1_.refs_0_.refs_4_, f32[4,256]{1,0:T(4,128)S(1)} %copy-done.4, bf16[256,512]{1,0:T(8,128)(2,1)S(1)} %copy-done, f32[256,512]{1,0:T(8,128)S(1)} %get-tuple-element.35.refs_4_, ...), custom_call_target="tpu_custom_call" | custom-call | flops 4800000000 | bytes 1048576 | tf_op jit(solution)/shard_map/pallas_call | solution.py:36
  62.9 2.7 %collective-permute-start.29 = (bf16[4,128,512]{2,1,0:T(8,128)(2,1)S(1)}, bf16[4,128,512]{2,1,0:T(8,128)(2,1)S(1)}, u32[]{:S(2)}, u32[]{:S(2)}) collective-permute-start(bf16[4,128,512]{2,1,0:T(8,128)(2,1)S(1)} %get-tuple-element.44), channel_id=1, source_target_pairs={{0,192},{8,56},{16,208},{24,8},{32,224},{40,24},{48,240},{56,40},{... | collective-permute-start | bytes 1572872 | tf_op jit(solution)/shard_map/ppermute | solution.py:261
  65.7 2.8 %collective-permute-start.23 = (bf16[512,256]{1,0:T(8,128)(2,1)S(1)}, bf16[512,256]{1,0:T(8,128)(2,1)S(1)}, u32[]{:S(2)}, u32[]{:S(2)}) collective-permute-start(bf16[512,256]{1,0:T(8,128)(2,1)S(1)} %get-tuple-element.52.refs_1_), channel_id=1, source_target_pairs={{0,7},{1,0},{2,1},{3,2},{4,3},{5,4},{6,5},{7,6},{8,15},{9,8},{10,9... | collective-permute-start | bytes 786440 | tf_op jit(solution)/shard_map/ppermute | solution.py:248
  69.1 1.5 %collective-permute-done.20 = bf16[512,256]{1,0:T(8,128)(2,1)S(1)} collective-permute-done((bf16[512,256]{1,0:T(8,128)(2,1)S(1)}, bf16[512,256]{1,0:T(8,128)(2,1)S(1)}, u32[]{:S(2)}, u32[]{:S(2)}) %collective-permute-start.20) | collective-permute-done | bytes 262176 | tf_op jit(solution)/shard_map/ppermute | solution.py:248
  73.3 4.7 %collective-permute-done.27 = bf16[4,128,512]{2,1,0:T(8,128)(2,1)S(1)} collective-permute-done((bf16[4,128,512]{2,1,0:T(8,128)(2,1)S(1)}, bf16[4,128,512]{2,1,0:T(8,128)(2,1)S(1)}, u32[]{:S(2)}, u32[]{:S(2)}) %collective-permute-start.27) | collective-permute-done | bytes 524320 | tf_op jit(solution)/shard_map/ppermute | solution.py:261
  78.5 2.5 %collective-permute-start.24 = (bf16[512,256]{1,0:T(8,128)(2,1)S(1)}, bf16[512,256]{1,0:T(8,128)(2,1)S(1)}, u32[]{:S(2)}, u32[]{:S(2)}) collective-permute-start(bf16[512,256]{1,0:T(8,128)(2,1)S(1)} %add_convert_fusion.2.refs_1_), channel_id=1, source_target_pairs={{0,7},{1,0},{2,1},{3,2},{4,3},{5,4},{6,5},{7,6},{8,15},{9,8},{10,9... | collective-permute-start | bytes 786440 | tf_op jit(solution)/shard_map/ppermute | solution.py:248
  81.3 3.0 %collective-permute-start.35 = (bf16[128,512]{1,0:T(8,128)(2,1)S(1)}, bf16[128,512]{1,0:T(8,128)(2,1)S(1)}, u32[]{:S(2)}, u32[]{:S(2)}) collective-permute-start(bf16[128,512]{1,0:T(8,128)(2,1)S(1)} %get-tuple-element.46), channel_id=1, source_target_pairs={{0,16},{8,72},{16,32},{24,88},{32,48},{40,104},{48,0},{56,120},{64... | collective-permute-start | bytes 393224 | tf_op jit(solution)/shard_map/ppermute | solution.py:261
  84.3 1.5 %collective-permute-done.21 = bf16[512,256]{1,0:T(8,128)(2,1)S(1)} collective-permute-done((bf16[512,256]{1,0:T(8,128)(2,1)S(1)}, bf16[512,256]{1,0:T(8,128)(2,1)S(1)}, u32[]{:S(2)}, u32[]{:S(2)}) %collective-permute-start.21) | collective-permute-done | bytes 262176 | tf_op jit(solution)/shard_map/ppermute | solution.py:248
  85.8 3.2 %collective-permute-start.37 = (bf16[128,512]{1,0:T(8,128)(2,1)S(1)}, bf16[128,512]{1,0:T(8,128)(2,1)S(1)}, u32[]{:S(2)}, u32[]{:S(2)}) collective-permute-start(bf16[128,512]{1,0:T(8,128)(2,1)S(1)} %get-tuple-element.47), channel_id=1, source_target_pairs={{0,48},{8,200},{16,0},{24,216},{32,16},{40,232},{48,32},{56,248},{... | collective-permute-start | bytes 393224 | tf_op jit(solution)/shard_map/ppermute | solution.py:261
  89.1 3.2 %collective-permute-start.36 = (bf16[128,512]{1,0:T(8,128)(2,1)S(1)}, bf16[128,512]{1,0:T(8,128)(2,1)S(1)}, u32[]{:S(2)}, u32[]{:S(2)}) collective-permute-start(bf16[128,512]{1,0:T(8,128)(2,1)S(1)} %get-tuple-element.48), channel_id=1, source_target_pairs={{0,32},{8,136},{16,48},{24,152},{32,0},{40,168},{48,16},{56,184},{... | collective-permute-start | bytes 393224 | tf_op jit(solution)/shard_map/ppermute | solution.py:261
  93.4 1.8 %collective-permute-start.25 = (bf16[512,256]{1,0:T(8,128)(2,1)S(1)}, bf16[512,256]{1,0:T(8,128)(2,1)S(1)}, u32[]{:S(2)}, u32[]{:S(2)}) collective-permute-start(bf16[512,256]{1,0:T(8,128)(2,1)S(1)} %add_convert_fusion.1.refs_2_), channel_id=1, source_target_pairs={{0,7},{1,0},{2,1},{3,2},{4,3},{5,4},{6,5},{7,6},{8,15},{9,8},{10,9... | collective-permute-start | bytes 786440 | tf_op jit(solution)/shard_map/ppermute | solution.py:248
  96.6 5.2 %collective-permute-done.22 = bf16[512,256]{1,0:T(8,128)(2,1)S(1)} collective-permute-done((bf16[512,256]{1,0:T(8,128)(2,1)S(1)}, bf16[512,256]{1,0:T(8,128)(2,1)S(1)}, u32[]{:S(2)}, u32[]{:S(2)}) %collective-permute-start.22) | collective-permute-done | bytes 262176 | tf_op jit(solution)/shard_map/ppermute | solution.py:248
  102.6 3.3 %shard_map.122 = (bf16[256,512]{1,0:T(8,128)(2,1)}, bf16[256,512]{1,0:T(8,128)(2,1)}, bf16[256,512]{1,0:T(8,128)(2,1)}) custom-call(bf16[4,128,512]{2,1,0:T(8,128)(2,1)S(1)} %fusion.2.refs_0_, bf16[512,256]{1,0:T(8,128)(2,1)S(1)} %add_convert_fusion.3.refs_1_, bf16[512,256]{1,0:T(8,128)(2,1)S(1)} %add_convert_fusion.1.refs_2_, s32[16]{0:T(128)S(1)} %copy-done.5, ...), custom_call_target="tpu_custom_call" | custom-call | flops 9900000256 | bytes 1048576 | tf_op jit(solution)/shard_map/pallas_call | solution.py:36
  (88 shorter events, 16.2 us)
Async XLA Ops:
  6.0 9.6 %collective-permute-start.4 = (bf16[512,256]{1,0:T(8,128)(2,1)S(1)}, bf16[512,256]{1,0:T(8,128)(2,1)S(1)}, u32[]{:S(2)}, u32[]{:S(2)}) collective-permute-start(bf16[512,256]{1,0:T(8,128)(2,1)S(1)} %pad_maximum_fusion.refs_3_.refs_2_), channel_id=1, source_target_pairs={{0,7},{1,0},{2,1},{3,2},{4,3},{5,4},{6,5},{7,6},{8,15},{9,8},{10,9... | collective-permute-start | bytes 786440 | tf_op jit(solution)/shard_map/ppermute | solution.py:248
  9.9 8.7 %collective-permute-start.1 = (bf16[512,256]{1,0:T(8,128)(2,1)S(1)}, bf16[512,256]{1,0:T(8,128)(2,1)S(1)}, u32[]{:S(2)}, u32[]{:S(2)}) collective-permute-start(bf16[512,256]{1,0:T(8,128)(2,1)S(1)} %pad_maximum_fusion.refs_3_.refs_2_), channel_id=1, source_target_pairs={{0,1},{1,2},{2,3},{3,4},{4,5},{5,6},{6,7},{7,0},{8,9},{9,10},{10,1... | collective-permute-start | bytes 786440 | tf_op jit(solution)/shard_map/ppermute | solution.py:248
  9.9 8.7 %collective-permute-start.9 = (bf16[128,512]{1,0:T(8,128)(2,1)}, bf16[128,512]{1,0:T(8,128)(2,1)S(1)}, u32[]{:S(2)}, u32[]{:S(2)}) collective-permute-start(bf16[128,512]{1,0:T(8,128)(2,1)} %refs_2_.3), channel_id=1, source_target_pairs={{0,32},{8,136},{16,48},{24,152},{32,0},{40,168},{48,16},{56,184},{... | collective-permute-start | bytes 393224 | tf_op jit(solution)/shard_map/ppermute | solution.py:261
  15.6 8.0 %collective-permute-start.5 = (bf16[512,256]{1,0:T(8,128)(2,1)S(1)}, bf16[512,256]{1,0:T(8,128)(2,1)S(1)}, u32[]{:S(2)}, u32[]{:S(2)}) collective-permute-start(bf16[512,256]{1,0:T(8,128)(2,1)S(1)} %collective-permute-done.4.refs_1_.refs_10_.refs_9_), channel_id=1, source_target_pairs={{0,7},{1,0},{2,1},{3,2},{4,3},{5,4},{6,5},{7,6},{8,15},{9,8},{10,9... | collective-permute-start | bytes 786440 | tf_op jit(solution)/shard_map/ppermute | solution.py:248
  18.7 7.9 %collective-permute-start.2 = (bf16[512,256]{1,0:T(8,128)(2,1)S(1)}, bf16[512,256]{1,0:T(8,128)(2,1)S(1)}, u32[]{:S(2)}, u32[]{:S(2)}) collective-permute-start(bf16[512,256]{1,0:T(8,128)(2,1)S(1)} %collective-permute-done.1.refs_0_.refs_4_.refs_3_), channel_id=1, source_target_pairs={{0,1},{1,2},{2,3},{3,4},{4,5},{5,6},{6,7},{7,0},{8,9},{9,10},{10,1... | collective-permute-start | bytes 786440 | tf_op jit(solution)/shard_map/ppermute | solution.py:248
  22.0 7.5 %collective-permute-start.11 = (bf16[528,128]{1,0:T(8,128)(2,1)S(1)}, bf16[528,128]{1,0:T(8,128)(2,1)S(1)}, u32[]{:S(2)}, u32[]{:S(2)}) collective-permute-start(bf16[528,128]{1,0:T(8,128)(2,1)S(1)} %get-tuple-element.25.refs_3_), channel_id=1, source_target_pairs={{0,8},{8,0},{1,9},{9,1},{2,10},{10,2},{3,11},{11,3},{4,12},{12,4},... | collective-permute-start | bytes 405512 | tf_op jit(solution)/shard_map/ppermute | solution.py:248
  23.7 7.1 %collective-permute-start.6 = (bf16[512,256]{1,0:T(8,128)(2,1)S(1)}, bf16[512,256]{1,0:T(8,128)(2,1)S(1)}, u32[]{:S(2)}, u32[]{:S(2)}) collective-permute-start(bf16[512,256]{1,0:T(8,128)(2,1)S(1)} %collective-permute-done.5.refs_1_.refs_9_.refs_8_), channel_id=1, source_target_pairs={{0,7},{1,0},{2,1},{3,2},{4,3},{5,4},{6,5},{7,6},{8,15},{9,8},{10,9... | collective-permute-start | bytes 786440 | tf_op jit(solution)/shard_map/ppermute | solution.py:248
  26.6 7.4 %collective-permute-start.3 = (bf16[512,256]{1,0:T(8,128)(2,1)S(1)}, bf16[512,256]{1,0:T(8,128)(2,1)S(1)}, u32[]{:S(2)}, u32[]{:S(2)}) collective-permute-start(bf16[512,256]{1,0:T(8,128)(2,1)S(1)} %collective-permute-done.2.refs_0_.refs_5_.refs_4_), channel_id=1, source_target_pairs={{0,1},{1,2},{2,3},{3,4},{4,5},{5,6},{6,7},{7,0},{8,9},{9,10},{10,1... | collective-permute-start | bytes 786440 | tf_op jit(solution)/shard_map/ppermute | solution.py:248
  26.6 18.2 %collective-permute-start.18 = (bf16[4,128,512]{2,1,0:T(8,128)(2,1)S(1)}, bf16[4,128,512]{2,1,0:T(8,128)(2,1)S(1)}, u32[]{:S(2)}, u32[]{:S(2)}) collective-permute-start(bf16[4,128,512]{2,1,0:T(8,128)(2,1)S(1)} %shard_map.110.refs_0_), channel_id=1, source_target_pairs={{0,192},{8,56},{16,208},{24,8},{32,224},{40,24},{48,240},{56,40},{... | collective-permute-start | bytes 1572872 | tf_op jit(solution)/shard_map/ppermute | solution.py:261
  29.3 15.5 %collective-permute-start.17 = (bf16[4,128,512]{2,1,0:T(8,128)(2,1)S(1)}, bf16[4,128,512]{2,1,0:T(8,128)(2,1)S(1)}, u32[]{:S(2)}, u32[]{:S(2)}) collective-permute-start(bf16[4,128,512]{2,1,0:T(8,128)(2,1)S(1)} %shard_map.110.refs_0_), channel_id=1, source_target_pairs={{0,128},{8,40},{16,144},{24,56},{32,160},{40,8},{48,176},{56,24},{... | collective-permute-start | bytes 1572872 | tf_op jit(solution)/shard_map/ppermute | solution.py:261
  29.5 16.6 %collective-permute-start.16 = (bf16[4,128,512]{2,1,0:T(8,128)(2,1)S(1)}, bf16[4,128,512]{2,1,0:T(8,128)(2,1)S(1)}, u32[]{:S(2)}, u32[]{:S(2)}) collective-permute-start(bf16[4,128,512]{2,1,0:T(8,128)(2,1)S(1)} %shard_map.110.refs_0_), channel_id=1, source_target_pairs={{0,64},{8,24},{16,80},{24,40},{32,96},{40,56},{48,112},{56,8},{64,... | collective-permute-start | bytes 1572872 | tf_op jit(solution)/shard_map/ppermute | solution.py:261
  30.8 7.5 %collective-permute-start.13 = (bf16[528,128]{1,0:T(8,128)(2,1)S(1)}, bf16[528,128]{1,0:T(8,128)(2,1)S(1)}, u32[]{:S(2)}, u32[]{:S(2)}) collective-permute-start(bf16[528,128]{1,0:T(8,128)(2,1)S(1)} %shard_map.112), channel_id=1, source_target_pairs={{0,32},{16,48},{32,64},{48,80},{64,96},{80,112},{96,128},{112,144}... | collective-permute-start | bytes 405512 | tf_op jit(solution)/shard_map/ppermute | solution.py:268
  34.0 9.9 %collective-permute-start.12 = (bf16[528,128]{1,0:T(8,128)(2,1)S(1)}, bf16[528,128]{1,0:T(8,128)(2,1)S(1)}, u32[]{:S(2)}, u32[]{:S(2)}) collective-permute-start(bf16[528,128]{1,0:T(8,128)(2,1)S(1)} %shard_map.112), channel_id=1, source_target_pairs={{0,16},{16,32},{32,48},{48,64},{64,80},{80,96},{96,112},{112,128},... | collective-permute-start | bytes 405512 | tf_op jit(solution)/shard_map/ppermute | solution.py:268
  38.3 13.8 %collective-permute-start.7 = (bf16[512,256]{1,0:T(8,128)(2,1)S(1)}, bf16[512,256]{1,0:T(8,128)(2,1)S(1)}, u32[]{:S(2)}, u32[]{:S(2)}) collective-permute-start(bf16[512,256]{1,0:T(8,128)(2,1)S(1)} %broadcast_select_fusion), channel_id=1, source_target_pairs={{0,1},{1,2},{2,3},{3,4},{4,5},{5,6},{6,7},{7,0},{8,15},{9,8},{10,9... | collective-permute-start | bytes 786440 | tf_op jit(solution)/shard_map/ppermute | solution.py:299
  47.4 6.6 %collective-permute-start.15 = (bf16[256,512]{1,0:T(8,128)(2,1)S(1)}, bf16[256,512]{1,0:T(8,128)(2,1)S(1)}, u32[]{:S(2)}, u32[]{:S(2)}) collective-permute-start(bf16[256,512]{1,0:T(8,128)(2,1)S(1)} %get-tuple-element.26.refs_2_.refs_1_), channel_id=1, source_target_pairs={{0,8},{8,0},{1,9},{9,1},{2,10},{10,2},{3,11},{11,3},{4,12},{12,4},... | collective-permute-start | bytes 786440 | tf_op jit(solution)/shard_map/ppermute | solution.py:248
  53.9 6.9 %collective-permute-start.30 = (bf16[256,512]{1,0:T(8,128)(2,1)S(1)}, bf16[256,512]{1,0:T(8,128)(2,1)S(1)}, u32[]{:S(2)}, u32[]{:S(2)}) collective-permute-start(bf16[256,512]{1,0:T(8,128)(2,1)S(1)} %get-tuple-element.36), channel_id=1, source_target_pairs={{0,8},{8,0},{1,9},{9,1},{2,10},{10,2},{3,11},{11,3},{4,12},{12,4},... | collective-permute-start | bytes 786440 | tf_op jit(solution)/shard_map/ppermute | solution.py:248
  55.9 6.5 %collective-permute-start.19 = (bf16[512,256]{1,0:T(8,128)(2,1)S(1)}, bf16[512,256]{1,0:T(8,128)(2,1)S(1)}, u32[]{:S(2)}, u32[]{:S(2)}) collective-permute-start(bf16[512,256]{1,0:T(8,128)(2,1)S(1)} %get-tuple-element.31), channel_id=1, source_target_pairs={{0,1},{1,2},{2,3},{3,4},{4,5},{5,6},{6,7},{7,0},{8,15},{9,8},{10,9... | collective-permute-start | bytes 786440 | tf_op jit(solution)/shard_map/ppermute | solution.py:299
  62.6 8.0 %collective-permute-start.20 = (bf16[512,256]{1,0:T(8,128)(2,1)S(1)}, bf16[512,256]{1,0:T(8,128)(2,1)S(1)}, u32[]{:S(2)}, u32[]{:S(2)}) collective-permute-start(bf16[512,256]{1,0:T(8,128)(2,1)S(1)} %get-tuple-element.51.refs_0_), channel_id=1, source_target_pairs={{0,1},{1,2},{2,3},{3,4},{4,5},{5,6},{6,7},{7,0},{8,9},{9,10},{10,1... | collective-permute-start | bytes 786440 | tf_op jit(solution)/shard_map/ppermute | solution.py:248
  62.8 15.2 %collective-permute-start.27 = (bf16[4,128,512]{2,1,0:T(8,128)(2,1)S(1)}, bf16[4,128,512]{2,1,0:T(8,128)(2,1)S(1)}, u32[]{:S(2)}, u32[]{:S(2)}) collective-permute-start(bf16[4,128,512]{2,1,0:T(8,128)(2,1)S(1)} %get-tuple-element.43), channel_id=1, source_target_pairs={{0,64},{8,24},{16,80},{24,40},{32,96},{40,56},{48,112},{56,8},{64,... | collective-permute-start | bytes 1572872 | tf_op jit(solution)/shard_map/ppermute | solution.py:261
  62.9 15.6 %collective-permute-start.29 = (bf16[4,128,512]{2,1,0:T(8,128)(2,1)S(1)}, bf16[4,128,512]{2,1,0:T(8,128)(2,1)S(1)}, u32[]{:S(2)}, u32[]{:S(2)}) collective-permute-start(bf16[4,128,512]{2,1,0:T(8,128)(2,1)S(1)} %get-tuple-element.44), channel_id=1, source_target_pairs={{0,192},{8,56},{16,208},{24,8},{32,224},{40,24},{48,240},{56,40},{... | collective-permute-start | bytes 1572872 | tf_op jit(solution)/shard_map/ppermute | solution.py:261
  65.6 15.4 %collective-permute-start.28 = (bf16[4,128,512]{2,1,0:T(8,128)(2,1)S(1)}, bf16[4,128,512]{2,1,0:T(8,128)(2,1)S(1)}, u32[]{:S(2)}, u32[]{:S(2)}) collective-permute-start(bf16[4,128,512]{2,1,0:T(8,128)(2,1)S(1)} %get-tuple-element.45), channel_id=1, source_target_pairs={{0,128},{8,40},{16,144},{24,56},{32,160},{40,8},{48,176},{56,24},{... | collective-permute-start | bytes 1572872 | tf_op jit(solution)/shard_map/ppermute | solution.py:261
  65.7 6.3 %collective-permute-start.23 = (bf16[512,256]{1,0:T(8,128)(2,1)S(1)}, bf16[512,256]{1,0:T(8,128)(2,1)S(1)}, u32[]{:S(2)}, u32[]{:S(2)}) collective-permute-start(bf16[512,256]{1,0:T(8,128)(2,1)S(1)} %get-tuple-element.52.refs_1_), channel_id=1, source_target_pairs={{0,7},{1,0},{2,1},{3,2},{4,3},{5,4},{6,5},{7,6},{8,15},{9,8},{10,9... | collective-permute-start | bytes 786440 | tf_op jit(solution)/shard_map/ppermute | solution.py:248
  70.6 21.8 %collective-permute-start.33 = (bf16[528,128]{1,0:T(8,128)(2,1)S(1)}, bf16[528,128]{1,0:T(8,128)(2,1)S(1)}, u32[]{:S(2)}, u32[]{:S(2)}) collective-permute-start(bf16[528,128]{1,0:T(8,128)(2,1)S(1)} %shard_map.120), channel_id=1, source_target_pairs={{32,0},{48,16},{64,32},{80,48},{96,64},{112,80},{128,96},{144,112}... | collective-permute-start | bytes 405512 | tf_op jit(solution)/shard_map/ppermute | solution.py:268
  72.0 21.4 %collective-permute-start.32 = (bf16[528,128]{1,0:T(8,128)(2,1)S(1)}, bf16[528,128]{1,0:T(8,128)(2,1)S(1)}, u32[]{:S(2)}, u32[]{:S(2)}) collective-permute-start(bf16[528,128]{1,0:T(8,128)(2,1)S(1)} %shard_map.120), channel_id=1, source_target_pairs={{16,0},{32,16},{48,32},{64,48},{80,64},{96,80},{112,96},{128,112},... | collective-permute-start | bytes 405512 | tf_op jit(solution)/shard_map/ppermute | solution.py:268
  78.0 7.8 %collective-permute-start.21 = (bf16[512,256]{1,0:T(8,128)(2,1)S(1)}, bf16[512,256]{1,0:T(8,128)(2,1)S(1)}, u32[]{:S(2)}, u32[]{:S(2)}) collective-permute-start(bf16[512,256]{1,0:T(8,128)(2,1)S(1)} %add_convert_fusion.4.refs_0_), channel_id=1, source_target_pairs={{0,1},{1,2},{2,3},{3,4},{4,5},{5,6},{6,7},{7,0},{8,9},{9,10},{10,1... | collective-permute-start | bytes 786440 | tf_op jit(solution)/shard_map/ppermute | solution.py:248
  78.5 10.6 %collective-permute-start.24 = (bf16[512,256]{1,0:T(8,128)(2,1)S(1)}, bf16[512,256]{1,0:T(8,128)(2,1)S(1)}, u32[]{:S(2)}, u32[]{:S(2)}) collective-permute-start(bf16[512,256]{1,0:T(8,128)(2,1)S(1)} %add_convert_fusion.2.refs_1_), channel_id=1, source_target_pairs={{0,7},{1,0},{2,1},{3,2},{4,3},{5,4},{6,5},{7,6},{8,15},{9,8},{10,9... | collective-permute-start | bytes 786440 | tf_op jit(solution)/shard_map/ppermute | solution.py:248
  81.3 13.9 %collective-permute-start.35 = (bf16[128,512]{1,0:T(8,128)(2,1)S(1)}, bf16[128,512]{1,0:T(8,128)(2,1)S(1)}, u32[]{:S(2)}, u32[]{:S(2)}) collective-permute-start(bf16[128,512]{1,0:T(8,128)(2,1)S(1)} %get-tuple-element.46), channel_id=1, source_target_pairs={{0,16},{8,72},{16,32},{24,88},{32,48},{40,104},{48,0},{56,120},{64... | collective-permute-start | bytes 393224 | tf_op jit(solution)/shard_map/ppermute | solution.py:261
  85.8 10.0 %collective-permute-start.37 = (bf16[128,512]{1,0:T(8,128)(2,1)S(1)}, bf16[128,512]{1,0:T(8,128)(2,1)S(1)}, u32[]{:S(2)}, u32[]{:S(2)}) collective-permute-start(bf16[128,512]{1,0:T(8,128)(2,1)S(1)} %get-tuple-element.47), channel_id=1, source_target_pairs={{0,48},{8,200},{16,0},{24,216},{32,16},{40,232},{48,32},{56,248},{... | collective-permute-start | bytes 393224 | tf_op jit(solution)/shard_map/ppermute | solution.py:261
  89.1 6.7 %collective-permute-start.36 = (bf16[128,512]{1,0:T(8,128)(2,1)S(1)}, bf16[128,512]{1,0:T(8,128)(2,1)S(1)}, u32[]{:S(2)}, u32[]{:S(2)}) collective-permute-start(bf16[128,512]{1,0:T(8,128)(2,1)S(1)} %get-tuple-element.48), channel_id=1, source_target_pairs={{0,32},{8,136},{16,48},{24,152},{32,0},{40,168},{48,16},{56,184},{... | collective-permute-start | bytes 393224 | tf_op jit(solution)/shard_map/ppermute | solution.py:261
  92.4 9.4 %collective-permute-start.22 = (bf16[512,256]{1,0:T(8,128)(2,1)S(1)}, bf16[512,256]{1,0:T(8,128)(2,1)S(1)}, u32[]{:S(2)}, u32[]{:S(2)}) collective-permute-start(bf16[512,256]{1,0:T(8,128)(2,1)S(1)} %add_convert_fusion.3.refs_1_), channel_id=1, source_target_pairs={{0,1},{1,2},{2,3},{3,4},{4,5},{5,6},{6,7},{7,0},{8,9},{9,10},{10,1... | collective-permute-start | bytes 786440 | tf_op jit(solution)/shard_map/ppermute | solution.py:248
  93.4 8.4 %collective-permute-start.25 = (bf16[512,256]{1,0:T(8,128)(2,1)S(1)}, bf16[512,256]{1,0:T(8,128)(2,1)S(1)}, u32[]{:S(2)}, u32[]{:S(2)}) collective-permute-start(bf16[512,256]{1,0:T(8,128)(2,1)S(1)} %add_convert_fusion.1.refs_2_), channel_id=1, source_target_pairs={{0,7},{1,0},{2,1},{3,2},{4,3},{5,4},{6,5},{7,6},{8,15},{9,8},{10,9... | collective-permute-start | bytes 786440 | tf_op jit(solution)/shard_map/ppermute | solution.py:248
  95.3 7.4 %collective-permute-start.34 = (bf16[528,128]{1,0:T(8,128)(2,1)S(1)}, bf16[528,128]{1,0:T(8,128)(2,1)S(1)}, u32[]{:S(2)}, u32[]{:S(2)}) collective-permute-start(bf16[528,128]{1,0:T(8,128)(2,1)S(1)} %shard_map.121.refs_11_), channel_id=1, source_target_pairs={{0,8},{8,0},{1,9},{9,1},{2,10},{10,2},{3,11},{11,3},{4,12},{12,4},... | collective-permute-start | bytes 405512 | tf_op jit(solution)/shard_map/ppermute | solution.py:248
  (12 other events, 46.6 us)

commit v4 on v3

--- a/solution.py
+++ b/solution.py
@@ -323,8 +323,12 @@
         right = add(value[half - 1 - s], ring(right, "z", 1))
         left = add(value[half + 1 + s], ring(left, "z", -1))
         stages.append((right, left))
-    right, left = ring(right, "z", 1), ring(left, "z", -1)
-    return (value[0].astype(F32) + right.astype(F32) + left.astype(F32)).astype(BF16), stages
+    return (value[0], ring(right, "z", 1), ring(left, "z", -1)), stages
+
+
+def sum_kernel(one_ref, two_ref, three_ref, out_ref):
+    total = one_ref[...].astype(F32) + two_ref[...].astype(F32) + three_ref[...].astype(F32)
+    out_ref[...] = total.astype(BF16)
 
 
 def swap(value):
@@ -357,24 +361,25 @@
     mixed = call(mix_kernel, [((2 * ROWS, HALF), BF16)] * LONG, [SMEM] + [VMEM] * 3, 1.9, (grads[4],))(
         at, att, att_other, w
     )
-    mixed, stages = scatter_long(mixed, c == 0)
+    shares, stages = scatter_long(mixed, c == 0)
+    own, send = call(pull_kernel, [((ROWS, STATE), F32), wide], [SMEM] + [VMEM] * (1 + LONG), 1.9)(at, w, *grads)
+    back, g = call(back_kernel, [((PAY, HD), BF16), wide], lead_specs + [VMEM] * 3, 1.6)(
+        *lead, q, own, swap(send)
+    )
+    grid = ((SIDE, SIDE, HD, STATE), BF16)
+    [r] = call(weight_grad_kernel, [grid], [SMEM] + [VMEM] * (2 + LONG), 1.9)(
+        at, att, att_other, *grads
+    )
+    r_near = scatter_side(r, "yx").astype(BF16)
+    r = scatter_side(r_near, "xy")
+    dq, dk, dv = call(grads_kernel, [wide] * 3, lead_specs + [VMEM] * 8, 3.3, (*stages[2],))(
+        *lead, q, k, v, g, state, *relay(at, back, -1, 0, stages[0], stages[1])
+    )
+    [mixed] = call(sum_kernel, [((2 * ROWS, HALF), BF16)], [VMEM] * 3, 0.5, (dq,))(*shares)
     mixed_other = swap(mixed[ROWS:])
     mixed = mixed[:ROWS]
     even, odd = jnp.where(c == 0, mixed, mixed_other), jnp.where(c == 0, mixed_other, mixed)
     mixed = jnp.concatenate([even[:, :HD], odd[:, :HD], even[:, HD:], odd[:, HD:]], axis=1)
-    own, send = call(pull_kernel, [((ROWS, STATE), F32), wide], [SMEM] + [VMEM] * (1 + LONG), 1.9)(at, w, *grads)
-    back, g = call(back_kernel, [((PAY, HD), BF16), wide], lead_specs + [VMEM] * 3, 1.6)(
-        *lead, q, own, swap(send)
-    )
-    grid = ((SIDE, SIDE, HD, STATE), BF16)
-    [r] = call(weight_grad_kernel, [grid], [SMEM] + [VMEM] * (2 + LONG), 1.9)(
-        at, att, att_other, *grads
-    )
-    r_near = scatter_side(r, "yx").astype(BF16)
-    r = scatter_side(r_near, "xy")
-    dq, dk, dv = call(grads_kernel, [wide] * 3, lead_specs + [VMEM] * 8, 3.3, (r_near, *stages[2]))(
-        *lead, q, k, v, g, state, *relay(at, back, -1, 0, stages[0], stages[1])
-    )
     return mixed, dq, dk, dv, r
 
 

time: 107 us -> 106 us (level)
  starting transfers between devices: 68.4 us -> 58.6 us
  waiting for transfers between devices: 17.3 us -> 25.6 us
    ppermute x4, waiting for transfers between devices: 2 us -> 15.6 us  [line(): return lax.ppermute(value, SEQ, pairs)]
    ppermute x2, starting transfers between devices: 6.69 us -> 0.09 us  [long_cross(): return lax.ppermute(value, ('core', 'z'), pairs)]
    ppermute x12, starting transfers between devices: 21.3 us -> 14.8 us  [cross(): return lax.ppermute(value, SEQ, pairs)]
    ppermute x12, waiting for transfers between devices: 6.07 us -> 0.03 us  [cross(): return lax.ppermute(value, SEQ, pairs)]
    ppermute x20, starting transfers between devices: 30.4 us -> 34.4 us  [ring(): lax.ppermute(value, axis, [(i, (i + steps) % count) for i in range(count)])]
    ppermute x2, waiting for transfers between devices: 0.01 us -> 1.53 us  [long_cross(): return lax.ppermute(value, ('core', 'z'), pairs)]
    pallas_call x13 -> x14, Pallas kernels: 15.4 us -> 15.5 us  [call(): return lambda *args: made(*after, *args)]
  transfers between devices with their start and end apart: 38 -> 38, of which waited for: 7 -> 11; matrix products, arithmetic and copies ran while one was open for 2% -> 2% of each run, Pallas kernels for 14% -> 15%
where the time goes in v4:
time: 106 us
  starting transfers between devices  58.6 us (55%)
  waiting for transfers between devices  25.6 us (24%)
  Pallas kernels  15.5 us (15%)
  local copies, waits for them, and re-layouts  3.13 us (3%)
  other arithmetic  2.35 us (2%)
    ppermute x20, starting transfers between devices, ring(): lax.ppermute(value, axis, [(i, (i + steps) % count) for i in range(count)])  34.4 us
    ppermute x4, waiting for transfers between devices, line(): return lax.ppermute(value, SEQ, pairs)  15.6 us
    pallas_call x14, Pallas kernels, call(): return lambda *args: made(*after, *args)  15.5 us
    ppermute x12, starting transfers between devices, cross(): return lax.ppermute(value, SEQ, pairs)  14.8 us
    ppermute x4, starting transfers between devices, line(): return lax.ppermute(value, SEQ, pairs)  9.25 us
    ppermute x20, waiting for transfers between devices, ring(): lax.ppermute(value, axis, [(i, (i + steps) % count) for i in range(count)])  8.38 us
  transfers between devices with their start and end apart: 38, of which 11 were waited for; matrix products, arithmetic and copies ran while one was open for 2% of the time, Pallas kernels for 15%

profile of v4, /device:TPU:1, one launch (start us, length us, event | category | flops | bytes accessed | tf_op | source)
XLA Modules:
  0.0 106.2 jit_solution(7193225806243758022)
XLA Ops:
  1.7 3.3 %collective-permute-start = (bf16[256,256]{1,0:T(8,128)(2,1)S(1)}, bf16[256,256]{1,0:T(8,128)(2,1)S(1)}, u32[]{:S(2)}, u32[]{:S(2)}) collective-permute-start(bf16[256,256]{1,0:T(8,128)(2,1)S(1)} %get-tuple-element.54), channel_id=1, source_target_pairs={{0,8},{8,0},{1,9},{9,1},{2,10},{10,2},{3,11},{11,3},{4,12},{12,4},... | collective-permute-start | bytes 393224 | tf_op jit(solution)/shard_map/ppermute | solution.py:248
  6.1 3.9 %collective-permute-start.4 = (bf16[512,256]{1,0:T(8,128)(2,1)S(1)}, bf16[512,256]{1,0:T(8,128)(2,1)S(1)}, u32[]{:S(2)}, u32[]{:S(2)}) collective-permute-start(bf16[512,256]{1,0:T(8,128)(2,1)S(1)} %pad_maximum_fusion.refs_2_.refs_3_), channel_id=1, source_target_pairs={{0,7},{1,0},{2,1},{3,2},{4,3},{5,4},{6,5},{7,6},{8,15},{9,8},{10,9... | collective-permute-start | bytes 786440 | tf_op jit(solution)/shard_map/ppermute | solution.py:248
  10.0 1.3 %collective-permute-start.8 = (bf16[128,512]{1,0:T(8,128)(2,1)}, bf16[128,512]{1,0:T(8,128)(2,1)S(1)}, u32[]{:S(2)}, u32[]{:S(2)}) collective-permute-start(bf16[128,512]{1,0:T(8,128)(2,1)} %refs_2_.4), channel_id=1, source_target_pairs={{0,16},{8,72},{16,32},{24,88},{32,48},{40,104},{48,0},{56,120},{64... | collective-permute-start | bytes 393224 | tf_op jit(solution)/shard_map/ppermute | solution.py:261
  11.3 2.6 %collective-permute-start.9 = (bf16[128,512]{1,0:T(8,128)(2,1)}, bf16[128,512]{1,0:T(8,128)(2,1)S(1)}, u32[]{:S(2)}, u32[]{:S(2)}) collective-permute-start(bf16[128,512]{1,0:T(8,128)(2,1)} %refs_2_.4), channel_id=1, source_target_pairs={{0,32},{8,136},{16,48},{24,152},{32,0},{40,168},{48,16},{56,184},{... | collective-permute-start | bytes 393224 | tf_op jit(solution)/shard_map/ppermute | solution.py:261
  15.1 1.2 %collective-permute-done.1.refs_0_.refs_3_.refs_4_ = bf16[512,256]{1,0:T(8,128)(2,1)S(1)} collective-permute-done((bf16[512,256]{1,0:T(8,128)(2,1)S(1)}, bf16[512,256]{1,0:T(8,128)(2,1)S(1)}, u32[]{:S(2)}, u32[]{:S(2)}) %collective-permute-start.1) | collective-permute-done | bytes 262176 | tf_op jit(solution)/shard_map/ppermute | solution.py:248
  16.3 2.7 %collective-permute-start.5 = (bf16[512,256]{1,0:T(8,128)(2,1)S(1)}, bf16[512,256]{1,0:T(8,128)(2,1)S(1)}, u32[]{:S(2)}, u32[]{:S(2)}) collective-permute-start(bf16[512,256]{1,0:T(8,128)(2,1)S(1)} %collective-permute-done.4.refs_1_.refs_9_.refs_10_), channel_id=1, source_target_pairs={{0,7},{1,0},{2,1},{3,2},{4,3},{5,4},{6,5},{7,6},{8,15},{9,8},{10,9... | collective-permute-start | bytes 786440 | tf_op jit(solution)/shard_map/ppermute | solution.py:248
  20.0 2.3 %shard_map.111 = (bf16[528,128]{1,0:T(8,128)(2,1)S(1)}, f32[256,512]{1,0:T(8,128)S(1)}) custom-call(bf16[4,128,512]{2,1,0:T(8,128)(2,1)S(1)} %shard_map.110.refs_0_, s32[16]{0:T(128)S(1)} %copy-done.5, s32[5]{0:T(128)S(1)} %stack.23.refs_2_.refs_1_.refs_0_.refs_3_, f32[4,256]{1,0:T(4,128)S(1)} %copy-done.4, bf16[256,512]{1,0:T(8,128)(2,1)S(1)} %copy-done, ...), custom_call_target="tpu_custom_call" | custom-call | flops 6899999744 | bytes 1048576 | tf_op jit(solution)/shard_map/pallas_call | solution.py:36
  22.3 1.5 %collective-permute-start.11 = (bf16[528,128]{1,0:T(8,128)(2,1)S(1)}, bf16[528,128]{1,0:T(8,128)(2,1)S(1)}, u32[]{:S(2)}, u32[]{:S(2)}) collective-permute-start(bf16[528,128]{1,0:T(8,128)(2,1)S(1)} %get-tuple-element.25.refs_3_), channel_id=1, source_target_pairs={{0,8},{8,0},{1,9},{9,1},{2,10},{10,2},{3,11},{11,3},{4,12},{12,4},... | collective-permute-start | bytes 405512 | tf_op jit(solution)/shard_map/ppermute | solution.py:248
  24.5 2.7 %collective-permute-start.6 = (bf16[512,256]{1,0:T(8,128)(2,1)S(1)}, bf16[512,256]{1,0:T(8,128)(2,1)S(1)}, u32[]{:S(2)}, u32[]{:S(2)}) collective-permute-start(bf16[512,256]{1,0:T(8,128)(2,1)S(1)} %collective-permute-done.5.refs_1_.refs_8_.refs_9_), channel_id=1, source_target_pairs={{0,7},{1,0},{2,1},{3,2},{4,3},{5,4},{6,5},{7,6},{8,15},{9,8},{10,9... | collective-permute-start | bytes 786440 | tf_op jit(solution)/shard_map/ppermute | solution.py:248
  28.4 2.5 %collective-permute-start.17 = (bf16[4,128,512]{2,1,0:T(8,128)(2,1)S(1)}, bf16[4,128,512]{2,1,0:T(8,128)(2,1)S(1)}, u32[]{:S(2)}, u32[]{:S(2)}) collective-permute-start(bf16[4,128,512]{2,1,0:T(8,128)(2,1)S(1)} %shard_map.110.refs_0_), channel_id=1, source_target_pairs={{0,128},{8,40},{16,144},{24,56},{32,160},{40,8},{48,176},{56,24},{... | collective-permute-start | bytes 1572872 | tf_op jit(solution)/shard_map/ppermute | solution.py:261
  32.6 3.5 %collective-permute-start.12 = (bf16[528,128]{1,0:T(8,128)(2,1)S(1)}, bf16[528,128]{1,0:T(8,128)(2,1)S(1)}, u32[]{:S(2)}, u32[]{:S(2)}) collective-permute-start(bf16[528,128]{1,0:T(8,128)(2,1)S(1)} %shard_map.112), channel_id=1, source_target_pairs={{0,16},{16,32},{32,48},{48,64},{64,80},{80,96},{96,112},{112,128},... | collective-permute-start | bytes 405512 | tf_op jit(solution)/shard_map/ppermute | solution.py:268
  36.1 3.2 %collective-permute-start.13 = (bf16[528,128]{1,0:T(8,128)(2,1)S(1)}, bf16[528,128]{1,0:T(8,128)(2,1)S(1)}, u32[]{:S(2)}, u32[]{:S(2)}) collective-permute-start(bf16[528,128]{1,0:T(8,128)(2,1)S(1)} %shard_map.112), channel_id=1, source_target_pairs={{0,32},{16,48},{32,64},{48,80},{64,96},{80,112},{96,128},{112,144}... | collective-permute-start | bytes 405512 | tf_op jit(solution)/shard_map/ppermute | solution.py:268
  39.4 4.0 %collective-permute-done.12.refs_2_ = bf16[528,128]{1,0:T(8,128)(2,1)S(1)} collective-permute-done((bf16[528,128]{1,0:T(8,128)(2,1)S(1)}, bf16[528,128]{1,0:T(8,128)(2,1)S(1)}, u32[]{:S(2)}, u32[]{:S(2)}) %collective-permute-start.12) | collective-permute-done | bytes 135200 | tf_op jit(solution)/shard_map/ppermute | solution.py:268
  43.3 3.6 %collective-permute-done.13.refs_3_ = bf16[528,128]{1,0:T(8,128)(2,1)S(1)} collective-permute-done((bf16[528,128]{1,0:T(8,128)(2,1)S(1)}, bf16[528,128]{1,0:T(8,128)(2,1)S(1)}, u32[]{:S(2)}, u32[]{:S(2)}) %collective-permute-start.13) | collective-permute-done | bytes 135200 | tf_op jit(solution)/shard_map/ppermute | solution.py:268
  49.7 4.3 %collective-permute-start.15 = (bf16[256,512]{1,0:T(8,128)(2,1)S(1)}, bf16[256,512]{1,0:T(8,128)(2,1)S(1)}, u32[]{:S(2)}, u32[]{:S(2)}) collective-permute-start(bf16[256,512]{1,0:T(8,128)(2,1)S(1)} %get-tuple-element.26.refs_2_.refs_1_), channel_id=1, source_target_pairs={{0,8},{8,0},{1,9},{9,1},{2,10},{10,2},{3,11},{11,3},{4,12},{12,4},... | collective-permute-start | bytes 786440 | tf_op jit(solution)/shard_map/ppermute | solution.py:248
  54.0 1.8 %shard_map.117 = (f32[256,512]{1,0:T(8,128)S(1)}, bf16[256,512]{1,0:T(8,128)(2,1)S(1)}) custom-call(s32[5]{0:T(128)S(1)} %stack.23.refs_2_.refs_1_.refs_0_.refs_3_, bf16[4,4,128,512]{3,2,1,0:T(8,128)(2,1)S(1)} %shard_map.115.refs_4_.refs_1_, bf16[512,256]{1,0:T(8,128)(2,1)S(1)} %pad_maximum_fusion.refs_2_.refs_3_, ...), custom_call_target="tpu_custom_call" | custom-call | flops 5699999744 | bytes 1048576 | tf_op jit(solution)/shard_map/pallas_call | solution.py:36
  55.9 1.9 %shard_map.116 = (bf16[512,256]{1,0:T(8,128)(2,1)S(1)}, bf16[512,256]{1,0:T(8,128)(2,1)S(1)}, bf16[512,256]{1,0:T(8,128)(2,1)S(1)}, bf16[512,256]{1,0:T(8,128)(2...) custom-call(bf16[512,256]{1,0:T(8,128)(2,1)S(1)} %collective-permute, ...), custom_call_target="tpu_custom_call" | custom-call | flops 5699999744 | bytes 1048576 | tf_op jit(solution)/shard_map/pallas_call | solution.py:36
  57.9 1.8 %shard_map.123 = bf16[4,4,128,512]{3,2,1,0:T(8,128)(2,1)S(1)} custom-call(s32[5]{0:T(128)S(1)} %stack.23.refs_2_.refs_1_.refs_0_.refs_3_, bf16[256,512]{1,0:T(8,128)(2,1)S(1)} %get-tuple-element.26.refs_2_.refs_1_, bf16[256,512]{1,0:T(8,128)(2,1)S(1)} %collective-permute-done.15.refs_3_.refs_2_, bf16[512,256]{1,0:T(8,128)(2,1)S(1)} %pad_maximum_fusion.refs_2_.refs_3_, ...), custom_call_target="tpu_custom_call" | custom-call | flops 5699999744 | bytes 1048576 | tf_op jit(solution)/shard_map/pallas_call | solution.py:36
  59.7 1.6 %shard_map.118 = (bf16[528,128]{1,0:T(8,128)(2,1)S(1)}, bf16[256,512]{1,0:T(8,128)(2,1)S(1)}) custom-call(s32[16]{0:T(128)S(1)} %copy-done.5, s32[5]{0:T(128)S(1)} %stack.23.refs_2_.refs_1_.refs_0_.refs_3_, f32[4,256]{1,0:T(4,128)S(1)} %copy-done.4, bf16[256,512]{1,0:T(8,128)(2,1)S(1)} %copy-done, f32[256,512]{1,0:T(8,128)S(1)} %get-tuple-element.34.refs_4_, ...), custom_call_target="tpu_custom_call" | custom-call | flops 4800000000 | bytes 1048576 | tf_op jit(solution)/shard_map/pallas_call | solution.py:36
  61.8 1.5 %collective-permute-done.19 = bf16[512,256]{1,0:T(8,128)(2,1)S(1)} collective-permute-done((bf16[512,256]{1,0:T(8,128)(2,1)S(1)}, bf16[512,256]{1,0:T(8,128)(2,1)S(1)}, u32[]{:S(2)}, u32[]{:S(2)}) %collective-permute-start.19) | collective-permute-done | bytes 262176 | tf_op jit(solution)/shard_map/ppermute | solution.py:299
  63.8 1.5 %collective-permute-start.33 = (bf16[4,128,512]{2,1,0:T(8,128)(2,1)S(1)}, bf16[4,128,512]{2,1,0:T(8,128)(2,1)S(1)}, u32[]{:S(2)}, u32[]{:S(2)}) collective-permute-start(bf16[4,128,512]{2,1,0:T(8,128)(2,1)S(1)} %get-tuple-element.45), channel_id=1, source_target_pairs={{0,128},{8,40},{16,144},{24,56},{32,160},{40,8},{48,176},{56,24},{... | collective-permute-start | bytes 1572872 | tf_op jit(solution)/shard_map/ppermute | solution.py:261
  65.4 2.7 %collective-permute-start.22 = (bf16[512,256]{1,0:T(8,128)(2,1)S(1)}, bf16[512,256]{1,0:T(8,128)(2,1)S(1)}, u32[]{:S(2)}, u32[]{:S(2)}) collective-permute-start(bf16[512,256]{1,0:T(8,128)(2,1)S(1)} %get-tuple-element.51.refs_1_), channel_id=1, source_target_pairs={{0,7},{1,0},{2,1},{3,2},{4,3},{5,4},{6,5},{7,6},{8,15},{9,8},{10,9... | collective-permute-start | bytes 786440 | tf_op jit(solution)/shard_map/ppermute | solution.py:248
  68.7 1.4 %collective-permute-done.20 = bf16[512,256]{1,0:T(8,128)(2,1)S(1)} collective-permute-done((bf16[512,256]{1,0:T(8,128)(2,1)S(1)}, bf16[512,256]{1,0:T(8,128)(2,1)S(1)}, u32[]{:S(2)}, u32[]{:S(2)}) %collective-permute-start.20) | collective-permute-done | bytes 262176 | tf_op jit(solution)/shard_map/ppermute | solution.py:248
  70.0 1.3 %collective-permute-start.26 = (bf16[528,128]{1,0:T(8,128)(2,1)S(1)}, bf16[528,128]{1,0:T(8,128)(2,1)S(1)}, u32[]{:S(2)}, u32[]{:S(2)}) collective-permute-start(bf16[528,128]{1,0:T(8,128)(2,1)S(1)} %shard_map.119), channel_id=1, source_target_pairs={{16,0},{32,16},{48,32},{64,48},{80,64},{96,80},{112,96},{128,112},... | collective-permute-start | bytes 405512 | tf_op jit(solution)/shard_map/ppermute | solution.py:268
  71.4 1.3 %collective-permute-start.27 = (bf16[528,128]{1,0:T(8,128)(2,1)S(1)}, bf16[528,128]{1,0:T(8,128)(2,1)S(1)}, u32[]{:S(2)}, u32[]{:S(2)}) collective-permute-start(bf16[528,128]{1,0:T(8,128)(2,1)S(1)} %shard_map.119), channel_id=1, source_target_pairs={{32,0},{48,16},{64,32},{80,48},{96,64},{112,80},{128,96},{144,112}... | collective-permute-start | bytes 405512 | tf_op jit(solution)/shard_map/ppermute | solution.py:268
  72.8 8.0 %collective-permute-done.26.refs_2_ = bf16[528,128]{1,0:T(8,128)(2,1)S(1)} collective-permute-done((bf16[528,128]{1,0:T(8,128)(2,1)S(1)}, bf16[528,128]{1,0:T(8,128)(2,1)S(1)}, u32[]{:S(2)}, u32[]{:S(2)}) %collective-permute-start.26) | collective-permute-done | bytes 135200 | tf_op jit(solution)/shard_map/ppermute | solution.py:268
  81.1 2.4 %collective-permute-start.23 = (bf16[512,256]{1,0:T(8,128)(2,1)S(1)}, bf16[512,256]{1,0:T(8,128)(2,1)S(1)}, u32[]{:S(2)}, u32[]{:S(2)}) collective-permute-start(bf16[512,256]{1,0:T(8,128)(2,1)S(1)} %add_convert_fusion.1.refs_1_), channel_id=1, source_target_pairs={{0,7},{1,0},{2,1},{3,2},{4,3},{5,4},{6,5},{7,6},{8,15},{9,8},{10,9... | collective-permute-start | bytes 786440 | tf_op jit(solution)/shard_map/ppermute | solution.py:248
  83.6 5.8 %collective-permute-start.28 = (bf16[528,128]{1,0:T(8,128)(2,1)S(1)}, bf16[528,128]{1,0:T(8,128)(2,1)S(1)}, u32[]{:S(2)}, u32[]{:S(2)}) collective-permute-start(bf16[528,128]{1,0:T(8,128)(2,1)S(1)} %shard_map.120.refs_10_), channel_id=1, source_target_pairs={{0,8},{8,0},{1,9},{9,1},{2,10},{10,2},{3,11},{11,3},{4,12},{12,4},... | collective-permute-start | bytes 405512 | tf_op jit(solution)/shard_map/ppermute | solution.py:248
  89.7 2.4 %collective-permute-start.37 = (bf16[128,512]{1,0:T(8,128)(2,1)S(1)}, bf16[128,512]{1,0:T(8,128)(2,1)S(1)}, u32[]{:S(2)}, u32[]{:S(2)}) collective-permute-start(bf16[128,512]{1,0:T(8,128)(2,1)S(1)} %get-tuple-element.47), channel_id=1, source_target_pairs={{0,48},{8,200},{16,0},{24,216},{32,16},{40,232},{48,32},{56,248},{... | collective-permute-start | bytes 393224 | tf_op jit(solution)/shard_map/ppermute | solution.py:261
  93.4 2.7 %collective-permute-start.30 = (bf16[512,256]{1,0:T(8,128)(2,1)S(1)}, bf16[512,256]{1,0:T(8,128)(2,1)S(1)}, u32[]{:S(2)}, u32[]{:S(2)}) collective-permute-start(bf16[512,256]{1,0:T(8,128)(2,1)S(1)} %add_convert_fusion.refs_1_), channel_id=1, source_target_pairs={{0,7},{1,0},{2,1},{3,2},{4,3},{5,4},{6,5},{7,6},{8,15},{9,8},{10,9... | collective-permute-start | bytes 786440 | tf_op jit(solution)/shard_map/ppermute | solution.py:248
  96.1 3.3 %shard_map.121 = (bf16[256,512]{1,0:T(8,128)(2,1)}, bf16[256,512]{1,0:T(8,128)(2,1)}, bf16[256,512]{1,0:T(8,128)(2,1)}) custom-call(bf16[512,256]{1,0:T(8,128)(2,1)S(1)} %add_convert_fusion.2.refs_0_, bf16[512,256]{1,0:T(8,128)(2,1)S(1)} %add_convert_fusion.refs_1_, s32[16]{0:T(128)S(1)} %copy-done.5, s32[5]{0:T(128)S(1)} %stack.23.refs_2_.refs_1_.refs_0_.refs_3_, ...), custom_call_target="tpu_custom_call" | custom-call | flops 9900000256 | bytes 1048576 | tf_op jit(solution)/shard_map/pallas_call | solution.py:36
  99.4 2.8 %collective-permute-done.29.refs_2_ = bf16[512,256]{1,0:T(8,128)(2,1)S(1)} collective-permute-done((bf16[512,256]{1,0:T(8,128)(2,1)S(1)}, bf16[512,256]{1,0:T(8,128)(2,1)S(1)}, u32[]{:S(2)}, u32[]{:S(2)}) %collective-permute-start.29) | collective-permute-done | bytes 262176 | tf_op jit(solution)/shard_map/ppermute | solution.py:248
  (90 shorter events, 18.6 us)
Async XLA Ops:
  6.0 10.3 %collective-permute-start.1 = (bf16[512,256]{1,0:T(8,128)(2,1)S(1)}, bf16[512,256]{1,0:T(8,128)(2,1)S(1)}, u32[]{:S(2)}, u32[]{:S(2)}) collective-permute-start(bf16[512,256]{1,0:T(8,128)(2,1)S(1)} %pad_maximum_fusion.refs_2_.refs_3_), channel_id=1, source_target_pairs={{0,1},{1,2},{2,3},{3,4},{4,5},{5,6},{6,7},{7,0},{8,9},{9,10},{10,1... | collective-permute-start | bytes 786440 | tf_op jit(solution)/shard_map/ppermute | solution.py:248
  6.1 10.2 %collective-permute-start.4 = (bf16[512,256]{1,0:T(8,128)(2,1)S(1)}, bf16[512,256]{1,0:T(8,128)(2,1)S(1)}, u32[]{:S(2)}, u32[]{:S(2)}) collective-permute-start(bf16[512,256]{1,0:T(8,128)(2,1)S(1)} %pad_maximum_fusion.refs_2_.refs_3_), channel_id=1, source_target_pairs={{0,7},{1,0},{2,1},{3,2},{4,3},{5,4},{6,5},{7,6},{8,15},{9,8},{10,9... | collective-permute-start | bytes 786440 | tf_op jit(solution)/shard_map/ppermute | solution.py:248
  10.0 9.0 %collective-permute-start.8 = (bf16[128,512]{1,0:T(8,128)(2,1)}, bf16[128,512]{1,0:T(8,128)(2,1)S(1)}, u32[]{:S(2)}, u32[]{:S(2)}) collective-permute-start(bf16[128,512]{1,0:T(8,128)(2,1)} %refs_2_.4), channel_id=1, source_target_pairs={{0,16},{8,72},{16,32},{24,88},{32,48},{40,104},{48,0},{56,120},{64... | collective-permute-start | bytes 393224 | tf_op jit(solution)/shard_map/ppermute | solution.py:261
  11.3 7.7 %collective-permute-start.9 = (bf16[128,512]{1,0:T(8,128)(2,1)}, bf16[128,512]{1,0:T(8,128)(2,1)S(1)}, u32[]{:S(2)}, u32[]{:S(2)}) collective-permute-start(bf16[128,512]{1,0:T(8,128)(2,1)} %refs_2_.4), channel_id=1, source_target_pairs={{0,32},{8,136},{16,48},{24,152},{32,0},{40,168},{48,16},{56,184},{... | collective-permute-start | bytes 393224 | tf_op jit(solution)/shard_map/ppermute | solution.py:261
  16.3 8.2 %collective-permute-start.2 = (bf16[512,256]{1,0:T(8,128)(2,1)S(1)}, bf16[512,256]{1,0:T(8,128)(2,1)S(1)}, u32[]{:S(2)}, u32[]{:S(2)}) collective-permute-start(bf16[512,256]{1,0:T(8,128)(2,1)S(1)} %collective-permute-done.1.refs_0_.refs_3_.refs_4_), channel_id=1, source_target_pairs={{0,1},{1,2},{2,3},{3,4},{4,5},{5,6},{6,7},{7,0},{8,9},{9,10},{10,1... | collective-permute-start | bytes 786440 | tf_op jit(solution)/shard_map/ppermute | solution.py:248
  16.3 8.2 %collective-permute-start.5 = (bf16[512,256]{1,0:T(8,128)(2,1)S(1)}, bf16[512,256]{1,0:T(8,128)(2,1)S(1)}, u32[]{:S(2)}, u32[]{:S(2)}) collective-permute-start(bf16[512,256]{1,0:T(8,128)(2,1)S(1)} %collective-permute-done.4.refs_1_.refs_9_.refs_10_), channel_id=1, source_target_pairs={{0,7},{1,0},{2,1},{3,2},{4,3},{5,4},{6,5},{7,6},{8,15},{9,8},{10,9... | collective-permute-start | bytes 786440 | tf_op jit(solution)/shard_map/ppermute | solution.py:248
  22.3 8.5 %collective-permute-start.11 = (bf16[528,128]{1,0:T(8,128)(2,1)S(1)}, bf16[528,128]{1,0:T(8,128)(2,1)S(1)}, u32[]{:S(2)}, u32[]{:S(2)}) collective-permute-start(bf16[528,128]{1,0:T(8,128)(2,1)S(1)} %get-tuple-element.25.refs_3_), channel_id=1, source_target_pairs={{0,8},{8,0},{1,9},{9,1},{2,10},{10,2},{3,11},{11,3},{4,12},{12,4},... | collective-permute-start | bytes 405512 | tf_op jit(solution)/shard_map/ppermute | solution.py:248
  24.5 8.1 %collective-permute-start.3 = (bf16[512,256]{1,0:T(8,128)(2,1)S(1)}, bf16[512,256]{1,0:T(8,128)(2,1)S(1)}, u32[]{:S(2)}, u32[]{:S(2)}) collective-permute-start(bf16[512,256]{1,0:T(8,128)(2,1)S(1)} %collective-permute-done.2.refs_0_.refs_4_.refs_5_), channel_id=1, source_target_pairs={{0,1},{1,2},{2,3},{3,4},{4,5},{5,6},{6,7},{7,0},{8,9},{9,10},{10,1... | collective-permute-start | bytes 786440 | tf_op jit(solution)/shard_map/ppermute | solution.py:248
  24.5 11.6 %collective-permute-start.6 = (bf16[512,256]{1,0:T(8,128)(2,1)S(1)}, bf16[512,256]{1,0:T(8,128)(2,1)S(1)}, u32[]{:S(2)}, u32[]{:S(2)}) collective-permute-start(bf16[512,256]{1,0:T(8,128)(2,1)S(1)} %collective-permute-done.5.refs_1_.refs_8_.refs_9_), channel_id=1, source_target_pairs={{0,7},{1,0},{2,1},{3,2},{4,3},{5,4},{6,5},{7,6},{8,15},{9,8},{10,9... | collective-permute-start | bytes 786440 | tf_op jit(solution)/shard_map/ppermute | solution.py:248
  27.2 20.0 %collective-permute-start.16 = (bf16[4,128,512]{2,1,0:T(8,128)(2,1)S(1)}, bf16[4,128,512]{2,1,0:T(8,128)(2,1)S(1)}, u32[]{:S(2)}, u32[]{:S(2)}) collective-permute-start(bf16[4,128,512]{2,1,0:T(8,128)(2,1)S(1)} %shard_map.110.refs_0_), channel_id=1, source_target_pairs={{0,64},{8,24},{16,80},{24,40},{32,96},{40,56},{48,112},{56,8},{64,... | collective-permute-start | bytes 1572872 | tf_op jit(solution)/shard_map/ppermute | solution.py:261
  28.4 18.8 %collective-permute-start.17 = (bf16[4,128,512]{2,1,0:T(8,128)(2,1)S(1)}, bf16[4,128,512]{2,1,0:T(8,128)(2,1)S(1)}, u32[]{:S(2)}, u32[]{:S(2)}) collective-permute-start(bf16[4,128,512]{2,1,0:T(8,128)(2,1)S(1)} %shard_map.110.refs_0_), channel_id=1, source_target_pairs={{0,128},{8,40},{16,144},{24,56},{32,160},{40,8},{48,176},{56,24},{... | collective-permute-start | bytes 1572872 | tf_op jit(solution)/shard_map/ppermute | solution.py:261
  30.8 16.4 %collective-permute-start.18 = (bf16[4,128,512]{2,1,0:T(8,128)(2,1)S(1)}, bf16[4,128,512]{2,1,0:T(8,128)(2,1)S(1)}, u32[]{:S(2)}, u32[]{:S(2)}) collective-permute-start(bf16[4,128,512]{2,1,0:T(8,128)(2,1)S(1)} %shard_map.110.refs_0_), channel_id=1, source_target_pairs={{0,192},{8,56},{16,208},{24,8},{32,224},{40,24},{48,240},{56,40},{... | collective-permute-start | bytes 1572872 | tf_op jit(solution)/shard_map/ppermute | solution.py:261
  32.6 10.7 %collective-permute-start.12 = (bf16[528,128]{1,0:T(8,128)(2,1)S(1)}, bf16[528,128]{1,0:T(8,128)(2,1)S(1)}, u32[]{:S(2)}, u32[]{:S(2)}) collective-permute-start(bf16[528,128]{1,0:T(8,128)(2,1)S(1)} %shard_map.112), channel_id=1, source_target_pairs={{0,16},{16,32},{32,48},{48,64},{64,80},{80,96},{96,112},{112,128},... | collective-permute-start | bytes 405512 | tf_op jit(solution)/shard_map/ppermute | solution.py:268
  36.1 10.9 %collective-permute-start.13 = (bf16[528,128]{1,0:T(8,128)(2,1)S(1)}, bf16[528,128]{1,0:T(8,128)(2,1)S(1)}, u32[]{:S(2)}, u32[]{:S(2)}) collective-permute-start(bf16[528,128]{1,0:T(8,128)(2,1)S(1)} %shard_map.112), channel_id=1, source_target_pairs={{0,32},{16,48},{32,64},{48,80},{64,96},{80,112},{96,128},{112,144}... | collective-permute-start | bytes 405512 | tf_op jit(solution)/shard_map/ppermute | solution.py:268
  43.3 10.6 %collective-permute-start.7 = (bf16[512,256]{1,0:T(8,128)(2,1)S(1)}, bf16[512,256]{1,0:T(8,128)(2,1)S(1)}, u32[]{:S(2)}, u32[]{:S(2)}) collective-permute-start(bf16[512,256]{1,0:T(8,128)(2,1)S(1)} %broadcast_select_fusion), channel_id=1, source_target_pairs={{0,1},{1,2},{2,3},{3,4},{4,5},{5,6},{6,7},{7,0},{8,15},{9,8},{10,9... | collective-permute-start | bytes 786440 | tf_op jit(solution)/shard_map/ppermute | solution.py:299
  49.7 6.2 %collective-permute-start.15 = (bf16[256,512]{1,0:T(8,128)(2,1)S(1)}, bf16[256,512]{1,0:T(8,128)(2,1)S(1)}, u32[]{:S(2)}, u32[]{:S(2)}) collective-permute-start(bf16[256,512]{1,0:T(8,128)(2,1)S(1)} %get-tuple-element.26.refs_2_.refs_1_), channel_id=1, source_target_pairs={{0,8},{8,0},{1,9},{9,1},{2,10},{10,2},{3,11},{11,3},{4,12},{12,4},... | collective-permute-start | bytes 786440 | tf_op jit(solution)/shard_map/ppermute | solution.py:248
  57.8 5.6 %collective-permute-start.19 = (bf16[512,256]{1,0:T(8,128)(2,1)S(1)}, bf16[512,256]{1,0:T(8,128)(2,1)S(1)}, u32[]{:S(2)}, u32[]{:S(2)}) collective-permute-start(bf16[512,256]{1,0:T(8,128)(2,1)S(1)} %get-tuple-element.30), channel_id=1, source_target_pairs={{0,1},{1,2},{2,3},{3,4},{4,5},{5,6},{6,7},{7,0},{8,15},{9,8},{10,9... | collective-permute-start | bytes 786440 | tf_op jit(solution)/shard_map/ppermute | solution.py:299
  63.5 6.5 %collective-permute-start.20 = (bf16[512,256]{1,0:T(8,128)(2,1)S(1)}, bf16[512,256]{1,0:T(8,128)(2,1)S(1)}, u32[]{:S(2)}, u32[]{:S(2)}) collective-permute-start(bf16[512,256]{1,0:T(8,128)(2,1)S(1)} %get-tuple-element.52.refs_0_), channel_id=1, source_target_pairs={{0,1},{1,2},{2,3},{3,4},{4,5},{5,6},{6,7},{7,0},{8,9},{9,10},{10,1... | collective-permute-start | bytes 786440 | tf_op jit(solution)/shard_map/ppermute | solution.py:248
  63.7 19.9 %collective-permute-start.34 = (bf16[4,128,512]{2,1,0:T(8,128)(2,1)S(1)}, bf16[4,128,512]{2,1,0:T(8,128)(2,1)S(1)}, u32[]{:S(2)}, u32[]{:S(2)}) collective-permute-start(bf16[4,128,512]{2,1,0:T(8,128)(2,1)S(1)} %get-tuple-element.44), channel_id=1, source_target_pairs={{0,192},{8,56},{16,208},{24,8},{32,224},{40,24},{48,240},{56,40},{... | collective-permute-start | bytes 1572872 | tf_op jit(solution)/shard_map/ppermute | solution.py:261
  63.8 25.6 %collective-permute-start.33 = (bf16[4,128,512]{2,1,0:T(8,128)(2,1)S(1)}, bf16[4,128,512]{2,1,0:T(8,128)(2,1)S(1)}, u32[]{:S(2)}, u32[]{:S(2)}) collective-permute-start(bf16[4,128,512]{2,1,0:T(8,128)(2,1)S(1)} %get-tuple-element.45), channel_id=1, source_target_pairs={{0,128},{8,40},{16,144},{24,56},{32,160},{40,8},{48,176},{56,24},{... | collective-permute-start | bytes 1572872 | tf_op jit(solution)/shard_map/ppermute | solution.py:261
  65.4 24.0 %collective-permute-start.32 = (bf16[4,128,512]{2,1,0:T(8,128)(2,1)S(1)}, bf16[4,128,512]{2,1,0:T(8,128)(2,1)S(1)}, u32[]{:S(2)}, u32[]{:S(2)}) collective-permute-start(bf16[4,128,512]{2,1,0:T(8,128)(2,1)S(1)} %get-tuple-element.43), channel_id=1, source_target_pairs={{0,64},{8,24},{16,80},{24,40},{32,96},{40,56},{48,112},{56,8},{64,... | collective-permute-start | bytes 1572872 | tf_op jit(solution)/shard_map/ppermute | solution.py:261
  65.4 6.0 %collective-permute-start.22 = (bf16[512,256]{1,0:T(8,128)(2,1)S(1)}, bf16[512,256]{1,0:T(8,128)(2,1)S(1)}, u32[]{:S(2)}, u32[]{:S(2)}) collective-permute-start(bf16[512,256]{1,0:T(8,128)(2,1)S(1)} %get-tuple-element.51.refs_1_), channel_id=1, source_target_pairs={{0,7},{1,0},{2,1},{3,2},{4,3},{5,4},{6,5},{7,6},{8,15},{9,8},{10,9... | collective-permute-start | bytes 786440 | tf_op jit(solution)/shard_map/ppermute | solution.py:248
  70.0 10.8 %collective-permute-start.26 = (bf16[528,128]{1,0:T(8,128)(2,1)S(1)}, bf16[528,128]{1,0:T(8,128)(2,1)S(1)}, u32[]{:S(2)}, u32[]{:S(2)}) collective-permute-start(bf16[528,128]{1,0:T(8,128)(2,1)S(1)} %shard_map.119), channel_id=1, source_target_pairs={{16,0},{32,16},{48,32},{64,48},{80,64},{96,80},{112,96},{128,112},... | collective-permute-start | bytes 405512 | tf_op jit(solution)/shard_map/ppermute | solution.py:268
  71.4 9.7 %collective-permute-start.27 = (bf16[528,128]{1,0:T(8,128)(2,1)S(1)}, bf16[528,128]{1,0:T(8,128)(2,1)S(1)}, u32[]{:S(2)}, u32[]{:S(2)}) collective-permute-start(bf16[528,128]{1,0:T(8,128)(2,1)S(1)} %shard_map.119), channel_id=1, source_target_pairs={{32,0},{48,16},{64,32},{80,48},{96,64},{112,80},{128,96},{144,112}... | collective-permute-start | bytes 405512 | tf_op jit(solution)/shard_map/ppermute | solution.py:268
  80.8 12.3 %collective-permute-start.21 = (bf16[512,256]{1,0:T(8,128)(2,1)S(1)}, bf16[512,256]{1,0:T(8,128)(2,1)S(1)}, u32[]{:S(2)}, u32[]{:S(2)}) collective-permute-start(bf16[512,256]{1,0:T(8,128)(2,1)S(1)} %add_convert_fusion.3.refs_0_), channel_id=1, source_target_pairs={{0,1},{1,2},{2,3},{3,4},{4,5},{5,6},{6,7},{7,0},{8,9},{9,10},{10,1... | collective-permute-start | bytes 786440 | tf_op jit(solution)/shard_map/ppermute | solution.py:248
  81.1 12.1 %collective-permute-start.23 = (bf16[512,256]{1,0:T(8,128)(2,1)S(1)}, bf16[512,256]{1,0:T(8,128)(2,1)S(1)}, u32[]{:S(2)}, u32[]{:S(2)}) collective-permute-start(bf16[512,256]{1,0:T(8,128)(2,1)S(1)} %add_convert_fusion.1.refs_1_), channel_id=1, source_target_pairs={{0,7},{1,0},{2,1},{3,2},{4,3},{5,4},{6,5},{7,6},{8,15},{9,8},{10,9... | collective-permute-start | bytes 786440 | tf_op jit(solution)/shard_map/ppermute | solution.py:248
  83.6 9.8 %collective-permute-start.28 = (bf16[528,128]{1,0:T(8,128)(2,1)S(1)}, bf16[528,128]{1,0:T(8,128)(2,1)S(1)}, u32[]{:S(2)}, u32[]{:S(2)}) collective-permute-start(bf16[528,128]{1,0:T(8,128)(2,1)S(1)} %shard_map.120.refs_10_), channel_id=1, source_target_pairs={{0,8},{8,0},{1,9},{9,1},{2,10},{10,2},{3,11},{11,3},{4,12},{12,4},... | collective-permute-start | bytes 405512 | tf_op jit(solution)/shard_map/ppermute | solution.py:248
  89.7 14.7 %collective-permute-start.37 = (bf16[128,512]{1,0:T(8,128)(2,1)S(1)}, bf16[128,512]{1,0:T(8,128)(2,1)S(1)}, u32[]{:S(2)}, u32[]{:S(2)}) collective-permute-start(bf16[128,512]{1,0:T(8,128)(2,1)S(1)} %get-tuple-element.47), channel_id=1, source_target_pairs={{0,48},{8,200},{16,0},{24,216},{32,16},{40,232},{48,32},{56,248},{... | collective-permute-start | bytes 393224 | tf_op jit(solution)/shard_map/ppermute | solution.py:261
  92.1 12.3 %collective-permute-start.36 = (bf16[128,512]{1,0:T(8,128)(2,1)S(1)}, bf16[128,512]{1,0:T(8,128)(2,1)S(1)}, u32[]{:S(2)}, u32[]{:S(2)}) collective-permute-start(bf16[128,512]{1,0:T(8,128)(2,1)S(1)} %get-tuple-element.48), channel_id=1, source_target_pairs={{0,32},{8,136},{16,48},{24,152},{32,0},{40,168},{48,16},{56,184},{... | collective-permute-start | bytes 393224 | tf_op jit(solution)/shard_map/ppermute | solution.py:261
  93.1 11.3 %collective-permute-start.35 = (bf16[128,512]{1,0:T(8,128)(2,1)S(1)}, bf16[128,512]{1,0:T(8,128)(2,1)S(1)}, u32[]{:S(2)}, u32[]{:S(2)}) collective-permute-start(bf16[128,512]{1,0:T(8,128)(2,1)S(1)} %get-tuple-element.46), channel_id=1, source_target_pairs={{0,16},{8,72},{16,32},{24,88},{32,48},{40,104},{48,0},{56,120},{64... | collective-permute-start | bytes 393224 | tf_op jit(solution)/shard_map/ppermute | solution.py:261
  93.2 9.0 %collective-permute-start.29 = (bf16[512,256]{1,0:T(8,128)(2,1)S(1)}, bf16[512,256]{1,0:T(8,128)(2,1)S(1)}, u32[]{:S(2)}, u32[]{:S(2)}) collective-permute-start(bf16[512,256]{1,0:T(8,128)(2,1)S(1)} %add_convert_fusion.2.refs_0_), channel_id=1, source_target_pairs={{0,1},{1,2},{2,3},{3,4},{4,5},{5,6},{6,7},{7,0},{8,9},{9,10},{10,1... | collective-permute-start | bytes 786440 | tf_op jit(solution)/shard_map/ppermute | solution.py:248
  93.4 8.8 %collective-permute-start.30 = (bf16[512,256]{1,0:T(8,128)(2,1)S(1)}, bf16[512,256]{1,0:T(8,128)(2,1)S(1)}, u32[]{:S(2)}, u32[]{:S(2)}) collective-permute-start(bf16[512,256]{1,0:T(8,128)(2,1)S(1)} %add_convert_fusion.refs_1_), channel_id=1, source_target_pairs={{0,7},{1,0},{2,1},{3,2},{4,3},{5,4},{6,5},{7,6},{8,15},{9,8},{10,9... | collective-permute-start | bytes 786440 | tf_op jit(solution)/shard_map/ppermute | solution.py:248
  (13 other events, 47.5 us)

commit v5 on v4

--- a/solution.py
+++ b/solution.py
@@ -367,7 +367,7 @@
         *lead, q, own, swap(send)
     )
     grid = ((SIDE, SIDE, HD, STATE), BF16)
-    [r] = call(weight_grad_kernel, [grid], [SMEM] + [VMEM] * (2 + LONG), 1.9)(
+    [r] = call(weight_grad_kernel, [grid], [SMEM] + [VMEM] * (2 + LONG), 1.9, (g,))(
         at, att, att_other, *grads
     )
     r_near = scatter_side(r, "yx").astype(BF16)

time: 106 us -> 106 us (level)
  no operation moved by 1% of the time
where the time goes in v5:
time: 106 us
  starting transfers between devices  58.6 us (55%)
  waiting for transfers between devices  25.6 us (24%)
  Pallas kernels  15.4 us (15%)
  local copies, waits for them, and re-layouts  3.12 us (3%)
  other arithmetic  2.35 us (2%)
    ppermute x20, starting transfers between devices, ring(): lax.ppermute(value, axis, [(i, (i + steps) % count) for i in range(count)])  34.4 us
    ppermute x4, waiting for transfers between devices, line(): return lax.ppermute(value, SEQ, pairs)  15.6 us
    pallas_call x14, Pallas kernels, call(): return lambda *args: made(*after, *args)  15.4 us
    ppermute x12, starting transfers between devices, cross(): return lax.ppermute(value, SEQ, pairs)  14.8 us
    ppermute x4, starting transfers between devices, line(): return lax.ppermute(value, SEQ, pairs)  9.25 us
    ppermute x20, waiting for transfers between devices, ring(): lax.ppermute(value, axis, [(i, (i + steps) % count) for i in range(count)])  8.38 us
  transfers between devices with their start and end apart: 38, of which 11 were waited for; matrix products, arithmetic and copies ran while one was open for 2% of the time, Pallas kernels for 15%

profile of v5, /device:TPU:1, one launch (start us, length us, event | category | flops | bytes accessed | tf_op | source)
XLA Modules:
  0.0 106.2 jit_solution(14683935959498056980)
XLA Ops:
  1.7 3.3 %collective-permute-start = (bf16[256,256]{1,0:T(8,128)(2,1)S(1)}, bf16[256,256]{1,0:T(8,128)(2,1)S(1)}, u32[]{:S(2)}, u32[]{:S(2)}) collective-permute-start(bf16[256,256]{1,0:T(8,128)(2,1)S(1)} %get-tuple-element.54), channel_id=1, source_target_pairs={{0,8},{8,0},{1,9},{9,1},{2,10},{10,2},{3,11},{11,3},{4,12},{12,4},... | collective-permute-start | bytes 393224 | tf_op jit(solution)/shard_map/ppermute | solution.py:248
  6.1 3.9 %collective-permute-start.4 = (bf16[512,256]{1,0:T(8,128)(2,1)S(1)}, bf16[512,256]{1,0:T(8,128)(2,1)S(1)}, u32[]{:S(2)}, u32[]{:S(2)}) collective-permute-start(bf16[512,256]{1,0:T(8,128)(2,1)S(1)} %pad_maximum_fusion.refs_2_.refs_4_), channel_id=1, source_target_pairs={{0,7},{1,0},{2,1},{3,2},{4,3},{5,4},{6,5},{7,6},{8,15},{9,8},{10,9... | collective-permute-start | bytes 786440 | tf_op jit(solution)/shard_map/ppermute | solution.py:248
  10.0 1.3 %collective-permute-start.8 = (bf16[128,512]{1,0:T(8,128)(2,1)}, bf16[128,512]{1,0:T(8,128)(2,1)S(1)}, u32[]{:S(2)}, u32[]{:S(2)}) collective-permute-start(bf16[128,512]{1,0:T(8,128)(2,1)} %refs_2_.4), channel_id=1, source_target_pairs={{0,16},{8,72},{16,32},{24,88},{32,48},{40,104},{48,0},{56,120},{64... | collective-permute-start | bytes 393224 | tf_op jit(solution)/shard_map/ppermute | solution.py:261
  11.3 2.6 %collective-permute-start.9 = (bf16[128,512]{1,0:T(8,128)(2,1)}, bf16[128,512]{1,0:T(8,128)(2,1)S(1)}, u32[]{:S(2)}, u32[]{:S(2)}) collective-permute-start(bf16[128,512]{1,0:T(8,128)(2,1)} %refs_2_.4), channel_id=1, source_target_pairs={{0,32},{8,136},{16,48},{24,152},{32,0},{40,168},{48,16},{56,184},{... | collective-permute-start | bytes 393224 | tf_op jit(solution)/shard_map/ppermute | solution.py:261
  15.1 1.2 %collective-permute-done.1.refs_0_.refs_3_.refs_5_ = bf16[512,256]{1,0:T(8,128)(2,1)S(1)} collective-permute-done((bf16[512,256]{1,0:T(8,128)(2,1)S(1)}, bf16[512,256]{1,0:T(8,128)(2,1)S(1)}, u32[]{:S(2)}, u32[]{:S(2)}) %collective-permute-start.1) | collective-permute-done | bytes 262176 | tf_op jit(solution)/shard_map/ppermute | solution.py:248
  16.3 2.7 %collective-permute-start.5 = (bf16[512,256]{1,0:T(8,128)(2,1)S(1)}, bf16[512,256]{1,0:T(8,128)(2,1)S(1)}, u32[]{:S(2)}, u32[]{:S(2)}) collective-permute-start(bf16[512,256]{1,0:T(8,128)(2,1)S(1)} %collective-permute-done.4.refs_1_.refs_9_.refs_11_), channel_id=1, source_target_pairs={{0,7},{1,0},{2,1},{3,2},{4,3},{5,4},{6,5},{7,6},{8,15},{9,8},{10,9... | collective-permute-start | bytes 786440 | tf_op jit(solution)/shard_map/ppermute | solution.py:248
  20.0 2.3 %shard_map.111 = (bf16[528,128]{1,0:T(8,128)(2,1)S(1)}, f32[256,512]{1,0:T(8,128)S(1)}) custom-call(bf16[4,128,512]{2,1,0:T(8,128)(2,1)S(1)} %shard_map.110.refs_0_, s32[16]{0:T(128)S(1)} %copy-done.5, s32[5]{0:T(128)S(1)} %stack.23.refs_2_.refs_1_.refs_0_.refs_3_, f32[4,256]{1,0:T(4,128)S(1)} %copy-done.4, bf16[256,512]{1,0:T(8,128)(2,1)S(1)} %copy-done, ...), custom_call_target="tpu_custom_call" | custom-call | flops 6899999744 | bytes 1048576 | tf_op jit(solution)/shard_map/pallas_call | solution.py:36
  22.3 1.5 %collective-permute-start.11 = (bf16[528,128]{1,0:T(8,128)(2,1)S(1)}, bf16[528,128]{1,0:T(8,128)(2,1)S(1)}, u32[]{:S(2)}, u32[]{:S(2)}) collective-permute-start(bf16[528,128]{1,0:T(8,128)(2,1)S(1)} %get-tuple-element.25.refs_3_), channel_id=1, source_target_pairs={{0,8},{8,0},{1,9},{9,1},{2,10},{10,2},{3,11},{11,3},{4,12},{12,4},... | collective-permute-start | bytes 405512 | tf_op jit(solution)/shard_map/ppermute | solution.py:248
  24.5 2.7 %collective-permute-start.6 = (bf16[512,256]{1,0:T(8,128)(2,1)S(1)}, bf16[512,256]{1,0:T(8,128)(2,1)S(1)}, u32[]{:S(2)}, u32[]{:S(2)}) collective-permute-start(bf16[512,256]{1,0:T(8,128)(2,1)S(1)} %collective-permute-done.5.refs_1_.refs_8_.refs_10_), channel_id=1, source_target_pairs={{0,7},{1,0},{2,1},{3,2},{4,3},{5,4},{6,5},{7,6},{8,15},{9,8},{10,9... | collective-permute-start | bytes 786440 | tf_op jit(solution)/shard_map/ppermute | solution.py:248
  28.4 2.5 %collective-permute-start.17 = (bf16[4,128,512]{2,1,0:T(8,128)(2,1)S(1)}, bf16[4,128,512]{2,1,0:T(8,128)(2,1)S(1)}, u32[]{:S(2)}, u32[]{:S(2)}) collective-permute-start(bf16[4,128,512]{2,1,0:T(8,128)(2,1)S(1)} %shard_map.110.refs_0_), channel_id=1, source_target_pairs={{0,128},{8,40},{16,144},{24,56},{32,160},{40,8},{48,176},{56,24},{... | collective-permute-start | bytes 1572872 | tf_op jit(solution)/shard_map/ppermute | solution.py:261
  32.6 3.5 %collective-permute-start.12 = (bf16[528,128]{1,0:T(8,128)(2,1)S(1)}, bf16[528,128]{1,0:T(8,128)(2,1)S(1)}, u32[]{:S(2)}, u32[]{:S(2)}) collective-permute-start(bf16[528,128]{1,0:T(8,128)(2,1)S(1)} %shard_map.112), channel_id=1, source_target_pairs={{0,16},{16,32},{32,48},{48,64},{64,80},{80,96},{96,112},{112,128},... | collective-permute-start | bytes 405512 | tf_op jit(solution)/shard_map/ppermute | solution.py:268
  36.1 3.2 %collective-permute-start.13 = (bf16[528,128]{1,0:T(8,128)(2,1)S(1)}, bf16[528,128]{1,0:T(8,128)(2,1)S(1)}, u32[]{:S(2)}, u32[]{:S(2)}) collective-permute-start(bf16[528,128]{1,0:T(8,128)(2,1)S(1)} %shard_map.112), channel_id=1, source_target_pairs={{0,32},{16,48},{32,64},{48,80},{64,96},{80,112},{96,128},{112,144}... | collective-permute-start | bytes 405512 | tf_op jit(solution)/shard_map/ppermute | solution.py:268
  39.4 4.0 %collective-permute-done.12.refs_2_ = bf16[528,128]{1,0:T(8,128)(2,1)S(1)} collective-permute-done((bf16[528,128]{1,0:T(8,128)(2,1)S(1)}, bf16[528,128]{1,0:T(8,128)(2,1)S(1)}, u32[]{:S(2)}, u32[]{:S(2)}) %collective-permute-start.12) | collective-permute-done | bytes 135200 | tf_op jit(solution)/shard_map/ppermute | solution.py:268
  43.3 3.6 %collective-permute-done.13.refs_3_ = bf16[528,128]{1,0:T(8,128)(2,1)S(1)} collective-permute-done((bf16[528,128]{1,0:T(8,128)(2,1)S(1)}, bf16[528,128]{1,0:T(8,128)(2,1)S(1)}, u32[]{:S(2)}, u32[]{:S(2)}) %collective-permute-start.13) | collective-permute-done | bytes 135200 | tf_op jit(solution)/shard_map/ppermute | solution.py:268
  49.7 4.3 %collective-permute-start.15 = (bf16[256,512]{1,0:T(8,128)(2,1)S(1)}, bf16[256,512]{1,0:T(8,128)(2,1)S(1)}, u32[]{:S(2)}, u32[]{:S(2)}) collective-permute-start(bf16[256,512]{1,0:T(8,128)(2,1)S(1)} %get-tuple-element.26.refs_2_), channel_id=1, source_target_pairs={{0,8},{8,0},{1,9},{9,1},{2,10},{10,2},{3,11},{11,3},{4,12},{12,4},... | collective-permute-start | bytes 786440 | tf_op jit(solution)/shard_map/ppermute | solution.py:248
  54.0 1.8 %shard_map.117 = (f32[256,512]{1,0:T(8,128)S(1)}, bf16[256,512]{1,0:T(8,128)(2,1)S(1)}) custom-call(s32[5]{0:T(128)S(1)} %stack.23.refs_2_.refs_1_.refs_0_.refs_3_, bf16[4,4,128,512]{3,2,1,0:T(8,128)(2,1)S(1)} %shard_map.115.refs_4_.refs_1_, bf16[512,256]{1,0:T(8,128)(2,1)S(1)} %pad_maximum_fusion.refs_2_.refs_4_, ...), custom_call_target="tpu_custom_call" | custom-call | flops 5699999744 | bytes 1048576 | tf_op jit(solution)/shard_map/pallas_call | solution.py:36
  55.9 1.8 %shard_map.116 = (bf16[512,256]{1,0:T(8,128)(2,1)S(1)}, bf16[512,256]{1,0:T(8,128)(2,1)S(1)}, bf16[512,256]{1,0:T(8,128)(2,1)S(1)}, bf16[512,256]{1,0:T(8,128)(2...) custom-call(bf16[512,256]{1,0:T(8,128)(2,1)S(1)} %collective-permute, ...), custom_call_target="tpu_custom_call" | custom-call | flops 5699999744 | bytes 1048576 | tf_op jit(solution)/shard_map/pallas_call | solution.py:36
  57.8 1.6 %shard_map.118 = (bf16[528,128]{1,0:T(8,128)(2,1)S(1)}, bf16[256,512]{1,0:T(8,128)(2,1)S(1)}) custom-call(s32[16]{0:T(128)S(1)} %copy-done.5, s32[5]{0:T(128)S(1)} %stack.23.refs_2_.refs_1_.refs_0_.refs_3_, f32[4,256]{1,0:T(4,128)S(1)} %copy-done.4, bf16[256,512]{1,0:T(8,128)(2,1)S(1)} %copy-done, f32[256,512]{1,0:T(8,128)S(1)} %get-tuple-element.34.refs_4_, ...), custom_call_target="tpu_custom_call" | custom-call | flops 4800000000 | bytes 1048576 | tf_op jit(solution)/shard_map/pallas_call | solution.py:36
  60.0 1.8 %shard_map.123 = bf16[4,4,128,512]{3,2,1,0:T(8,128)(2,1)S(1)} custom-call(bf16[256,512]{1,0:T(8,128)(2,1)S(1)} %get-tuple-element.36.refs_8_.refs_0_, s32[5]{0:T(128)S(1)} %stack.23.refs_2_.refs_1_.refs_0_.refs_3_, bf16[256,512]{1,0:T(8,128)(2,1)S(1)} %get-tuple-element.26.refs_2_, bf16[256,512]{1,0:T(8,128)(2,1)S(1)} %collective-permute-done.15.refs_3_, ...), custom_call_target="tpu_custom_call" | custom-call | flops 5699999744 | bytes 1048576 | tf_op jit(solution)/shard_map/pallas_call | solution.py:36
  61.8 1.5 %collective-permute-done.19 = bf16[512,256]{1,0:T(8,128)(2,1)S(1)} collective-permute-done((bf16[512,256]{1,0:T(8,128)(2,1)S(1)}, bf16[512,256]{1,0:T(8,128)(2,1)S(1)}, u32[]{:S(2)}, u32[]{:S(2)}) %collective-permute-start.19) | collective-permute-done | bytes 262176 | tf_op jit(solution)/shard_map/ppermute | solution.py:299
  63.8 1.5 %collective-permute-start.33 = (bf16[4,128,512]{2,1,0:T(8,128)(2,1)S(1)}, bf16[4,128,512]{2,1,0:T(8,128)(2,1)S(1)}, u32[]{:S(2)}, u32[]{:S(2)}) collective-permute-start(bf16[4,128,512]{2,1,0:T(8,128)(2,1)S(1)} %get-tuple-element.45), channel_id=1, source_target_pairs={{0,128},{8,40},{16,144},{24,56},{32,160},{40,8},{48,176},{56,24},{... | collective-permute-start | bytes 1572872 | tf_op jit(solution)/shard_map/ppermute | solution.py:261
  65.3 2.7 %collective-permute-start.22 = (bf16[512,256]{1,0:T(8,128)(2,1)S(1)}, bf16[512,256]{1,0:T(8,128)(2,1)S(1)}, u32[]{:S(2)}, u32[]{:S(2)}) collective-permute-start(bf16[512,256]{1,0:T(8,128)(2,1)S(1)} %get-tuple-element.51.refs_1_), channel_id=1, source_target_pairs={{0,7},{1,0},{2,1},{3,2},{4,3},{5,4},{6,5},{7,6},{8,15},{9,8},{10,9... | collective-permute-start | bytes 786440 | tf_op jit(solution)/shard_map/ppermute | solution.py:248
  68.6 1.4 %collective-permute-done.20 = bf16[512,256]{1,0:T(8,128)(2,1)S(1)} collective-permute-done((bf16[512,256]{1,0:T(8,128)(2,1)S(1)}, bf16[512,256]{1,0:T(8,128)(2,1)S(1)}, u32[]{:S(2)}, u32[]{:S(2)}) %collective-permute-start.20) | collective-permute-done | bytes 262176 | tf_op jit(solution)/shard_map/ppermute | solution.py:248
  70.0 1.3 %collective-permute-start.26 = (bf16[528,128]{1,0:T(8,128)(2,1)S(1)}, bf16[528,128]{1,0:T(8,128)(2,1)S(1)}, u32[]{:S(2)}, u32[]{:S(2)}) collective-permute-start(bf16[528,128]{1,0:T(8,128)(2,1)S(1)} %shard_map.119), channel_id=1, source_target_pairs={{16,0},{32,16},{48,32},{64,48},{80,64},{96,80},{112,96},{128,112},... | collective-permute-start | bytes 405512 | tf_op jit(solution)/shard_map/ppermute | solution.py:268
  71.4 1.3 %collective-permute-start.27 = (bf16[528,128]{1,0:T(8,128)(2,1)S(1)}, bf16[528,128]{1,0:T(8,128)(2,1)S(1)}, u32[]{:S(2)}, u32[]{:S(2)}) collective-permute-start(bf16[528,128]{1,0:T(8,128)(2,1)S(1)} %shard_map.119), channel_id=1, source_target_pairs={{32,0},{48,16},{64,32},{80,48},{96,64},{112,80},{128,96},{144,112}... | collective-permute-start | bytes 405512 | tf_op jit(solution)/shard_map/ppermute | solution.py:268
  72.7 8.0 %collective-permute-done.26.refs_2_ = bf16[528,128]{1,0:T(8,128)(2,1)S(1)} collective-permute-done((bf16[528,128]{1,0:T(8,128)(2,1)S(1)}, bf16[528,128]{1,0:T(8,128)(2,1)S(1)}, u32[]{:S(2)}, u32[]{:S(2)}) %collective-permute-start.26) | collective-permute-done | bytes 135200 | tf_op jit(solution)/shard_map/ppermute | solution.py:268
  81.1 2.4 %collective-permute-start.23 = (bf16[512,256]{1,0:T(8,128)(2,1)S(1)}, bf16[512,256]{1,0:T(8,128)(2,1)S(1)}, u32[]{:S(2)}, u32[]{:S(2)}) collective-permute-start(bf16[512,256]{1,0:T(8,128)(2,1)S(1)} %add_convert_fusion.1.refs_1_), channel_id=1, source_target_pairs={{0,7},{1,0},{2,1},{3,2},{4,3},{5,4},{6,5},{7,6},{8,15},{9,8},{10,9... | collective-permute-start | bytes 786440 | tf_op jit(solution)/shard_map/ppermute | solution.py:248
  83.6 5.8 %collective-permute-start.28 = (bf16[528,128]{1,0:T(8,128)(2,1)S(1)}, bf16[528,128]{1,0:T(8,128)(2,1)S(1)}, u32[]{:S(2)}, u32[]{:S(2)}) collective-permute-start(bf16[528,128]{1,0:T(8,128)(2,1)S(1)} %shard_map.120.refs_10_), channel_id=1, source_target_pairs={{0,8},{8,0},{1,9},{9,1},{2,10},{10,2},{3,11},{11,3},{4,12},{12,4},... | collective-permute-start | bytes 405512 | tf_op jit(solution)/shard_map/ppermute | solution.py:248
  89.7 2.4 %collective-permute-start.37 = (bf16[128,512]{1,0:T(8,128)(2,1)S(1)}, bf16[128,512]{1,0:T(8,128)(2,1)S(1)}, u32[]{:S(2)}, u32[]{:S(2)}) collective-permute-start(bf16[128,512]{1,0:T(8,128)(2,1)S(1)} %get-tuple-element.47), channel_id=1, source_target_pairs={{0,48},{8,200},{16,0},{24,216},{32,16},{40,232},{48,32},{56,248},{... | collective-permute-start | bytes 393224 | tf_op jit(solution)/shard_map/ppermute | solution.py:261
  93.4 2.7 %collective-permute-start.30 = (bf16[512,256]{1,0:T(8,128)(2,1)S(1)}, bf16[512,256]{1,0:T(8,128)(2,1)S(1)}, u32[]{:S(2)}, u32[]{:S(2)}) collective-permute-start(bf16[512,256]{1,0:T(8,128)(2,1)S(1)} %add_convert_fusion.refs_1_), channel_id=1, source_target_pairs={{0,7},{1,0},{2,1},{3,2},{4,3},{5,4},{6,5},{7,6},{8,15},{9,8},{10,9... | collective-permute-start | bytes 786440 | tf_op jit(solution)/shard_map/ppermute | solution.py:248
  96.1 3.3 %shard_map.121 = (bf16[256,512]{1,0:T(8,128)(2,1)}, bf16[256,512]{1,0:T(8,128)(2,1)}, bf16[256,512]{1,0:T(8,128)(2,1)}) custom-call(bf16[512,256]{1,0:T(8,128)(2,1)S(1)} %add_convert_fusion.2.refs_0_, bf16[512,256]{1,0:T(8,128)(2,1)S(1)} %add_convert_fusion.refs_1_, s32[16]{0:T(128)S(1)} %copy-done.5, s32[5]{0:T(128)S(1)} %stack.23.refs_2_.refs_1_.refs_0_.refs_3_, ...), custom_call_target="tpu_custom_call" | custom-call | flops 9900000256 | bytes 1048576 | tf_op jit(solution)/shard_map/pallas_call | solution.py:36
  99.4 2.8 %collective-permute-done.29.refs_2_ = bf16[512,256]{1,0:T(8,128)(2,1)S(1)} collective-permute-done((bf16[512,256]{1,0:T(8,128)(2,1)S(1)}, bf16[512,256]{1,0:T(8,128)(2,1)S(1)}, u32[]{:S(2)}, u32[]{:S(2)}) %collective-permute-start.29) | collective-permute-done | bytes 262176 | tf_op jit(solution)/shard_map/ppermute | solution.py:248
  (90 shorter events, 18.6 us)
Async XLA Ops:
  6.0 10.3 %collective-permute-start.1 = (bf16[512,256]{1,0:T(8,128)(2,1)S(1)}, bf16[512,256]{1,0:T(8,128)(2,1)S(1)}, u32[]{:S(2)}, u32[]{:S(2)}) collective-permute-start(bf16[512,256]{1,0:T(8,128)(2,1)S(1)} %pad_maximum_fusion.refs_2_.refs_4_), channel_id=1, source_target_pairs={{0,1},{1,2},{2,3},{3,4},{4,5},{5,6},{6,7},{7,0},{8,9},{9,10},{10,1... | collective-permute-start | bytes 786440 | tf_op jit(solution)/shard_map/ppermute | solution.py:248
  6.1 10.2 %collective-permute-start.4 = (bf16[512,256]{1,0:T(8,128)(2,1)S(1)}, bf16[512,256]{1,0:T(8,128)(2,1)S(1)}, u32[]{:S(2)}, u32[]{:S(2)}) collective-permute-start(bf16[512,256]{1,0:T(8,128)(2,1)S(1)} %pad_maximum_fusion.refs_2_.refs_4_), channel_id=1, source_target_pairs={{0,7},{1,0},{2,1},{3,2},{4,3},{5,4},{6,5},{7,6},{8,15},{9,8},{10,9... | collective-permute-start | bytes 786440 | tf_op jit(solution)/shard_map/ppermute | solution.py:248
  10.0 9.0 %collective-permute-start.8 = (bf16[128,512]{1,0:T(8,128)(2,1)}, bf16[128,512]{1,0:T(8,128)(2,1)S(1)}, u32[]{:S(2)}, u32[]{:S(2)}) collective-permute-start(bf16[128,512]{1,0:T(8,128)(2,1)} %refs_2_.4), channel_id=1, source_target_pairs={{0,16},{8,72},{16,32},{24,88},{32,48},{40,104},{48,0},{56,120},{64... | collective-permute-start | bytes 393224 | tf_op jit(solution)/shard_map/ppermute | solution.py:261
  11.3 7.7 %collective-permute-start.9 = (bf16[128,512]{1,0:T(8,128)(2,1)}, bf16[128,512]{1,0:T(8,128)(2,1)S(1)}, u32[]{:S(2)}, u32[]{:S(2)}) collective-permute-start(bf16[128,512]{1,0:T(8,128)(2,1)} %refs_2_.4), channel_id=1, source_target_pairs={{0,32},{8,136},{16,48},{24,152},{32,0},{40,168},{48,16},{56,184},{... | collective-permute-start | bytes 393224 | tf_op jit(solution)/shard_map/ppermute | solution.py:261
  16.3 8.2 %collective-permute-start.2 = (bf16[512,256]{1,0:T(8,128)(2,1)S(1)}, bf16[512,256]{1,0:T(8,128)(2,1)S(1)}, u32[]{:S(2)}, u32[]{:S(2)}) collective-permute-start(bf16[512,256]{1,0:T(8,128)(2,1)S(1)} %collective-permute-done.1.refs_0_.refs_3_.refs_5_), channel_id=1, source_target_pairs={{0,1},{1,2},{2,3},{3,4},{4,5},{5,6},{6,7},{7,0},{8,9},{9,10},{10,1... | collective-permute-start | bytes 786440 | tf_op jit(solution)/shard_map/ppermute | solution.py:248
  16.3 8.2 %collective-permute-start.5 = (bf16[512,256]{1,0:T(8,128)(2,1)S(1)}, bf16[512,256]{1,0:T(8,128)(2,1)S(1)}, u32[]{:S(2)}, u32[]{:S(2)}) collective-permute-start(bf16[512,256]{1,0:T(8,128)(2,1)S(1)} %collective-permute-done.4.refs_1_.refs_9_.refs_11_), channel_id=1, source_target_pairs={{0,7},{1,0},{2,1},{3,2},{4,3},{5,4},{6,5},{7,6},{8,15},{9,8},{10,9... | collective-permute-start | bytes 786440 | tf_op jit(solution)/shard_map/ppermute | solution.py:248
  22.3 8.5 %collective-permute-start.11 = (bf16[528,128]{1,0:T(8,128)(2,1)S(1)}, bf16[528,128]{1,0:T(8,128)(2,1)S(1)}, u32[]{:S(2)}, u32[]{:S(2)}) collective-permute-start(bf16[528,128]{1,0:T(8,128)(2,1)S(1)} %get-tuple-element.25.refs_3_), channel_id=1, source_target_pairs={{0,8},{8,0},{1,9},{9,1},{2,10},{10,2},{3,11},{11,3},{4,12},{12,4},... | collective-permute-start | bytes 405512 | tf_op jit(solution)/shard_map/ppermute | solution.py:248
  24.5 8.1 %collective-permute-start.3 = (bf16[512,256]{1,0:T(8,128)(2,1)S(1)}, bf16[512,256]{1,0:T(8,128)(2,1)S(1)}, u32[]{:S(2)}, u32[]{:S(2)}) collective-permute-start(bf16[512,256]{1,0:T(8,128)(2,1)S(1)} %collective-permute-done.2.refs_0_.refs_4_.refs_6_), channel_id=1, source_target_pairs={{0,1},{1,2},{2,3},{3,4},{4,5},{5,6},{6,7},{7,0},{8,9},{9,10},{10,1... | collective-permute-start | bytes 786440 | tf_op jit(solution)/shard_map/ppermute | solution.py:248
  24.5 11.6 %collective-permute-start.6 = (bf16[512,256]{1,0:T(8,128)(2,1)S(1)}, bf16[512,256]{1,0:T(8,128)(2,1)S(1)}, u32[]{:S(2)}, u32[]{:S(2)}) collective-permute-start(bf16[512,256]{1,0:T(8,128)(2,1)S(1)} %collective-permute-done.5.refs_1_.refs_8_.refs_10_), channel_id=1, source_target_pairs={{0,7},{1,0},{2,1},{3,2},{4,3},{5,4},{6,5},{7,6},{8,15},{9,8},{10,9... | collective-permute-start | bytes 786440 | tf_op jit(solution)/shard_map/ppermute | solution.py:248
  27.2 20.0 %collective-permute-start.16 = (bf16[4,128,512]{2,1,0:T(8,128)(2,1)S(1)}, bf16[4,128,512]{2,1,0:T(8,128)(2,1)S(1)}, u32[]{:S(2)}, u32[]{:S(2)}) collective-permute-start(bf16[4,128,512]{2,1,0:T(8,128)(2,1)S(1)} %shard_map.110.refs_0_), channel_id=1, source_target_pairs={{0,64},{8,24},{16,80},{24,40},{32,96},{40,56},{48,112},{56,8},{64,... | collective-permute-start | bytes 1572872 | tf_op jit(solution)/shard_map/ppermute | solution.py:261
  28.4 18.8 %collective-permute-start.17 = (bf16[4,128,512]{2,1,0:T(8,128)(2,1)S(1)}, bf16[4,128,512]{2,1,0:T(8,128)(2,1)S(1)}, u32[]{:S(2)}, u32[]{:S(2)}) collective-permute-start(bf16[4,128,512]{2,1,0:T(8,128)(2,1)S(1)} %shard_map.110.refs_0_), channel_id=1, source_target_pairs={{0,128},{8,40},{16,144},{24,56},{32,160},{40,8},{48,176},{56,24},{... | collective-permute-start | bytes 1572872 | tf_op jit(solution)/shard_map/ppermute | solution.py:261
  30.8 16.4 %collective-permute-start.18 = (bf16[4,128,512]{2,1,0:T(8,128)(2,1)S(1)}, bf16[4,128,512]{2,1,0:T(8,128)(2,1)S(1)}, u32[]{:S(2)}, u32[]{:S(2)}) collective-permute-start(bf16[4,128,512]{2,1,0:T(8,128)(2,1)S(1)} %shard_map.110.refs_0_), channel_id=1, source_target_pairs={{0,192},{8,56},{16,208},{24,8},{32,224},{40,24},{48,240},{56,40},{... | collective-permute-start | bytes 1572872 | tf_op jit(solution)/shard_map/ppermute | solution.py:261
  32.6 10.7 %collective-permute-start.12 = (bf16[528,128]{1,0:T(8,128)(2,1)S(1)}, bf16[528,128]{1,0:T(8,128)(2,1)S(1)}, u32[]{:S(2)}, u32[]{:S(2)}) collective-permute-start(bf16[528,128]{1,0:T(8,128)(2,1)S(1)} %shard_map.112), channel_id=1, source_target_pairs={{0,16},{16,32},{32,48},{48,64},{64,80},{80,96},{96,112},{112,128},... | collective-permute-start | bytes 405512 | tf_op jit(solution)/shard_map/ppermute | solution.py:268
  36.1 10.9 %collective-permute-start.13 = (bf16[528,128]{1,0:T(8,128)(2,1)S(1)}, bf16[528,128]{1,0:T(8,128)(2,1)S(1)}, u32[]{:S(2)}, u32[]{:S(2)}) collective-permute-start(bf16[528,128]{1,0:T(8,128)(2,1)S(1)} %shard_map.112), channel_id=1, source_target_pairs={{0,32},{16,48},{32,64},{48,80},{64,96},{80,112},{96,128},{112,144}... | collective-permute-start | bytes 405512 | tf_op jit(solution)/shard_map/ppermute | solution.py:268
  43.3 10.6 %collective-permute-start.7 = (bf16[512,256]{1,0:T(8,128)(2,1)S(1)}, bf16[512,256]{1,0:T(8,128)(2,1)S(1)}, u32[]{:S(2)}, u32[]{:S(2)}) collective-permute-start(bf16[512,256]{1,0:T(8,128)(2,1)S(1)} %broadcast_select_fusion), channel_id=1, source_target_pairs={{0,1},{1,2},{2,3},{3,4},{4,5},{5,6},{6,7},{7,0},{8,15},{9,8},{10,9... | collective-permute-start | bytes 786440 | tf_op jit(solution)/shard_map/ppermute | solution.py:299
  49.7 6.2 %collective-permute-start.15 = (bf16[256,512]{1,0:T(8,128)(2,1)S(1)}, bf16[256,512]{1,0:T(8,128)(2,1)S(1)}, u32[]{:S(2)}, u32[]{:S(2)}) collective-permute-start(bf16[256,512]{1,0:T(8,128)(2,1)S(1)} %get-tuple-element.26.refs_2_), channel_id=1, source_target_pairs={{0,8},{8,0},{1,9},{9,1},{2,10},{10,2},{3,11},{11,3},{4,12},{12,4},... | collective-permute-start | bytes 786440 | tf_op jit(solution)/shard_map/ppermute | solution.py:248
  59.4 5.9 %collective-permute-start.25 = (bf16[528,128]{1,0:T(8,128)(2,1)S(1)}, bf16[528,128]{1,0:T(8,128)(2,1)S(1)}, u32[]{:S(2)}, u32[]{:S(2)}) collective-permute-start(bf16[528,128]{1,0:T(8,128)(2,1)S(1)} %get-tuple-element.38.refs_3_), channel_id=1, source_target_pairs={{0,8},{8,0},{1,9},{9,1},{2,10},{10,2},{3,11},{11,3},{4,12},{12,4},... | collective-permute-start | bytes 405512 | tf_op jit(solution)/shard_map/ppermute | solution.py:248
  63.5 6.5 %collective-permute-start.20 = (bf16[512,256]{1,0:T(8,128)(2,1)S(1)}, bf16[512,256]{1,0:T(8,128)(2,1)S(1)}, u32[]{:S(2)}, u32[]{:S(2)}) collective-permute-start(bf16[512,256]{1,0:T(8,128)(2,1)S(1)} %get-tuple-element.52.refs_0_), channel_id=1, source_target_pairs={{0,1},{1,2},{2,3},{3,4},{4,5},{5,6},{6,7},{7,0},{8,9},{9,10},{10,1... | collective-permute-start | bytes 786440 | tf_op jit(solution)/shard_map/ppermute | solution.py:248
  63.7 19.9 %collective-permute-start.34 = (bf16[4,128,512]{2,1,0:T(8,128)(2,1)S(1)}, bf16[4,128,512]{2,1,0:T(8,128)(2,1)S(1)}, u32[]{:S(2)}, u32[]{:S(2)}) collective-permute-start(bf16[4,128,512]{2,1,0:T(8,128)(2,1)S(1)} %get-tuple-element.44), channel_id=1, source_target_pairs={{0,192},{8,56},{16,208},{24,8},{32,224},{40,24},{48,240},{56,40},{... | collective-permute-start | bytes 1572872 | tf_op jit(solution)/shard_map/ppermute | solution.py:261
  63.8 25.6 %collective-permute-start.33 = (bf16[4,128,512]{2,1,0:T(8,128)(2,1)S(1)}, bf16[4,128,512]{2,1,0:T(8,128)(2,1)S(1)}, u32[]{:S(2)}, u32[]{:S(2)}) collective-permute-start(bf16[4,128,512]{2,1,0:T(8,128)(2,1)S(1)} %get-tuple-element.45), channel_id=1, source_target_pairs={{0,128},{8,40},{16,144},{24,56},{32,160},{40,8},{48,176},{56,24},{... | collective-permute-start | bytes 1572872 | tf_op jit(solution)/shard_map/ppermute | solution.py:261
  65.3 24.0 %collective-permute-start.32 = (bf16[4,128,512]{2,1,0:T(8,128)(2,1)S(1)}, bf16[4,128,512]{2,1,0:T(8,128)(2,1)S(1)}, u32[]{:S(2)}, u32[]{:S(2)}) collective-permute-start(bf16[4,128,512]{2,1,0:T(8,128)(2,1)S(1)} %get-tuple-element.43), channel_id=1, source_target_pairs={{0,64},{8,24},{16,80},{24,40},{32,96},{40,56},{48,112},{56,8},{64,... | collective-permute-start | bytes 1572872 | tf_op jit(solution)/shard_map/ppermute | solution.py:261
  65.3 6.0 %collective-permute-start.22 = (bf16[512,256]{1,0:T(8,128)(2,1)S(1)}, bf16[512,256]{1,0:T(8,128)(2,1)S(1)}, u32[]{:S(2)}, u32[]{:S(2)}) collective-permute-start(bf16[512,256]{1,0:T(8,128)(2,1)S(1)} %get-tuple-element.51.refs_1_), channel_id=1, source_target_pairs={{0,7},{1,0},{2,1},{3,2},{4,3},{5,4},{6,5},{7,6},{8,15},{9,8},{10,9... | collective-permute-start | bytes 786440 | tf_op jit(solution)/shard_map/ppermute | solution.py:248
  70.0 10.8 %collective-permute-start.26 = (bf16[528,128]{1,0:T(8,128)(2,1)S(1)}, bf16[528,128]{1,0:T(8,128)(2,1)S(1)}, u32[]{:S(2)}, u32[]{:S(2)}) collective-permute-start(bf16[528,128]{1,0:T(8,128)(2,1)S(1)} %shard_map.119), channel_id=1, source_target_pairs={{16,0},{32,16},{48,32},{64,48},{80,64},{96,80},{112,96},{128,112},... | collective-permute-start | bytes 405512 | tf_op jit(solution)/shard_map/ppermute | solution.py:268
  71.4 9.7 %collective-permute-start.27 = (bf16[528,128]{1,0:T(8,128)(2,1)S(1)}, bf16[528,128]{1,0:T(8,128)(2,1)S(1)}, u32[]{:S(2)}, u32[]{:S(2)}) collective-permute-start(bf16[528,128]{1,0:T(8,128)(2,1)S(1)} %shard_map.119), channel_id=1, source_target_pairs={{32,0},{48,16},{64,32},{80,48},{96,64},{112,80},{128,96},{144,112}... | collective-permute-start | bytes 405512 | tf_op jit(solution)/shard_map/ppermute | solution.py:268
  80.8 12.3 %collective-permute-start.21 = (bf16[512,256]{1,0:T(8,128)(2,1)S(1)}, bf16[512,256]{1,0:T(8,128)(2,1)S(1)}, u32[]{:S(2)}, u32[]{:S(2)}) collective-permute-start(bf16[512,256]{1,0:T(8,128)(2,1)S(1)} %add_convert_fusion.3.refs_0_), channel_id=1, source_target_pairs={{0,1},{1,2},{2,3},{3,4},{4,5},{5,6},{6,7},{7,0},{8,9},{9,10},{10,1... | collective-permute-start | bytes 786440 | tf_op jit(solution)/shard_map/ppermute | solution.py:248
  81.1 12.1 %collective-permute-start.23 = (bf16[512,256]{1,0:T(8,128)(2,1)S(1)}, bf16[512,256]{1,0:T(8,128)(2,1)S(1)}, u32[]{:S(2)}, u32[]{:S(2)}) collective-permute-start(bf16[512,256]{1,0:T(8,128)(2,1)S(1)} %add_convert_fusion.1.refs_1_), channel_id=1, source_target_pairs={{0,7},{1,0},{2,1},{3,2},{4,3},{5,4},{6,5},{7,6},{8,15},{9,8},{10,9... | collective-permute-start | bytes 786440 | tf_op jit(solution)/shard_map/ppermute | solution.py:248
  83.6 9.8 %collective-permute-start.28 = (bf16[528,128]{1,0:T(8,128)(2,1)S(1)}, bf16[528,128]{1,0:T(8,128)(2,1)S(1)}, u32[]{:S(2)}, u32[]{:S(2)}) collective-permute-start(bf16[528,128]{1,0:T(8,128)(2,1)S(1)} %shard_map.120.refs_10_), channel_id=1, source_target_pairs={{0,8},{8,0},{1,9},{9,1},{2,10},{10,2},{3,11},{11,3},{4,12},{12,4},... | collective-permute-start | bytes 405512 | tf_op jit(solution)/shard_map/ppermute | solution.py:248
  89.7 14.7 %collective-permute-start.37 = (bf16[128,512]{1,0:T(8,128)(2,1)S(1)}, bf16[128,512]{1,0:T(8,128)(2,1)S(1)}, u32[]{:S(2)}, u32[]{:S(2)}) collective-permute-start(bf16[128,512]{1,0:T(8,128)(2,1)S(1)} %get-tuple-element.47), channel_id=1, source_target_pairs={{0,48},{8,200},{16,0},{24,216},{32,16},{40,232},{48,32},{56,248},{... | collective-permute-start | bytes 393224 | tf_op jit(solution)/shard_map/ppermute | solution.py:261
  92.0 12.3 %collective-permute-start.36 = (bf16[128,512]{1,0:T(8,128)(2,1)S(1)}, bf16[128,512]{1,0:T(8,128)(2,1)S(1)}, u32[]{:S(2)}, u32[]{:S(2)}) collective-permute-start(bf16[128,512]{1,0:T(8,128)(2,1)S(1)} %get-tuple-element.48), channel_id=1, source_target_pairs={{0,32},{8,136},{16,48},{24,152},{32,0},{40,168},{48,16},{56,184},{... | collective-permute-start | bytes 393224 | tf_op jit(solution)/shard_map/ppermute | solution.py:261
  93.1 11.3 %collective-permute-start.35 = (bf16[128,512]{1,0:T(8,128)(2,1)S(1)}, bf16[128,512]{1,0:T(8,128)(2,1)S(1)}, u32[]{:S(2)}, u32[]{:S(2)}) collective-permute-start(bf16[128,512]{1,0:T(8,128)(2,1)S(1)} %get-tuple-element.46), channel_id=1, source_target_pairs={{0,16},{8,72},{16,32},{24,88},{32,48},{40,104},{48,0},{56,120},{64... | collective-permute-start | bytes 393224 | tf_op jit(solution)/shard_map/ppermute | solution.py:261
  93.2 9.0 %collective-permute-start.29 = (bf16[512,256]{1,0:T(8,128)(2,1)S(1)}, bf16[512,256]{1,0:T(8,128)(2,1)S(1)}, u32[]{:S(2)}, u32[]{:S(2)}) collective-permute-start(bf16[512,256]{1,0:T(8,128)(2,1)S(1)} %add_convert_fusion.2.refs_0_), channel_id=1, source_target_pairs={{0,1},{1,2},{2,3},{3,4},{4,5},{5,6},{6,7},{7,0},{8,9},{9,10},{10,1... | collective-permute-start | bytes 786440 | tf_op jit(solution)/shard_map/ppermute | solution.py:248
  93.4 8.8 %collective-permute-start.30 = (bf16[512,256]{1,0:T(8,128)(2,1)S(1)}, bf16[512,256]{1,0:T(8,128)(2,1)S(1)}, u32[]{:S(2)}, u32[]{:S(2)}) collective-permute-start(bf16[512,256]{1,0:T(8,128)(2,1)S(1)} %add_convert_fusion.refs_1_), channel_id=1, source_target_pairs={{0,7},{1,0},{2,1},{3,2},{4,3},{5,4},{6,5},{7,6},{8,15},{9,8},{10,9... | collective-permute-start | bytes 786440 | tf_op jit(solution)/shard_map/ppermute | solution.py:248
  (13 other events, 47.1 us)
